TPU v7x, 128 devices: a whole 4x4x4 slice. The times are simulated.
128 devices in a mesh: ctx: 32 (over y, z, core), wt: 4 (over x).
Axes of the slice: x: 4, y: 4, z: 4, core: 2. Of those that a mesh axis runs over, the one named last changes fastest.
Arguments:
- layer_input: bfloat16 [4, 8192, 960], P('wt', 'ctx'), may hold values from -6 to 6
- doc_bounds: int32 [4, 2], P('wt'), may hold values from 1 to 8191, as said below
- attn_gain: bfloat16 [960], P('wt'), may hold values from 0.099609375 to 1.8984375
- w_query: bfloat16 [960, 960], P('wt'), may hold values from -0.1875 to 0.1875
- key_weight: bfloat16 [960, 320], P('wt'), may hold values from -0.1875 to 0.1875
- value_weight: bfloat16 [960, 320], P('wt'), may hold values from -0.1875 to 0.1875
- w_out: bfloat16 [960, 960], P('wt'), may hold values from -3.5 to 3.5
- mlp_gain: bfloat16 [960], P('wt'), may hold values from 0.099609375 to 1.8984375
- w_gate: bfloat16 [960, 2560], P('wt'), may hold values from -0.1875 to 0.1875
- w_up: bfloat16 [960, 2560], P('wt'), may hold values from -0.1875 to 0.1875
- w_down: bfloat16 [2560, 960], P('wt'), may hold values from -0.125 to 0.125
- cotangent: bfloat16 [4, 8192, 960], P('wt', 'ctx'), may hold values from -6 to 6
Outputs:
- layer_output: bfloat16 [4, 8192, 960], P('wt', 'ctx')
- input_grad: float32 [4, 8192, 960], P('wt', 'ctx')
- grad_attn_gain: float32 [960], P('wt')
- grad_w_query: float32 [960, 960], P('wt')
- grad_w_key: float32 [960, 320], P('wt')
- grad_w_value: float32 [960, 320], P('wt')
- grad_w_out: float32 [960, 960], P('wt')
- grad_mlp_gain: float32 [960], P('wt')
- grad_w_gate: float32 [960, 2560], P('wt')
- grad_w_up: float32 [960, 2560], P('wt')
- grad_w_down: float32 [2560, 960], P('wt')
Inputs may be any that keep to these rules, and one draw needn't show every extreme that they name: `doc_bounds`: in every stream the first boundary lies among the first 128 tokens after token 0 and the second among the last 128 tokens, so the middle document spans the stream from its first device to its last.
All inputs are finite; a program needn't handle non-finite values.
Results may differ from a plain program's by a relative error of at most 0.03.
Values may be sent and summed in bfloat16 or wider, within the bound.
A program may use at most 128 MiB of HBM per device.

v0:
```python
import jax
import jax.numpy as jnp
from jax import lax
from jax.sharding import PartitionSpec as P

QUERY_HEADS = 15
KEY_VALUE_HEADS = 5
HEAD_SIZE = 64


EPSILON = 1e-05
NEGATIVE_FILL = -1e30


def shifted(array, axis, by):
    devices = lax.axis_size(axis)
    pairs = [(i, i + by) for i in range(devices) if 0 <= i + by < devices]
    return lax.ppermute(array, axis, pairs)


def from_behind(block, axis, distance):
    devices = range(lax.axis_size(axis))
    route = [((i - distance) % len(devices), i) for i in devices]
    return lax.ppermute(block, axis, route)


def keep_state(current):
    return current


def rms_forward(values, gain):
    inverse = lax.rsqrt(jnp.mean(values * values, axis=-1, keepdims=True) + EPSILON)
    normal = values * inverse
    return (normal * gain, normal, inverse)


def rms_backward(upstream, gain, normal, inverse):
    scaled = upstream * gain
    inner = jnp.mean(scaled * normal, axis=-1, keepdims=True)
    return (inverse * (scaled - normal * inner), jnp.sum(upstream * normal, axis=0))


def rope_tables(positions):
    half = HEAD_SIZE // 2
    freqs = 10000.0 ** (-jnp.arange(half, dtype=jnp.float32) * 2.0 / HEAD_SIZE)
    angles = positions.astype(jnp.float32)[:, None] * freqs[None, :]
    angles = jnp.concatenate([angles, angles], axis=-1)
    return (jnp.cos(angles)[:, None, :], jnp.sin(angles)[:, None, :])


def rotate_forward(values, cosine_table, sine_table):
    half = values.shape[-1] // 2
    turned = jnp.concatenate([-values[..., half:], values[..., :half]], axis=-1)
    return values * cosine_table + turned * sine_table


def rotation_backward(gradient, cosine_table, sine_table):
    half = gradient.shape[-1] // 2
    weighted = gradient * sine_table
    turned = jnp.concatenate([weighted[..., half:], -weighted[..., :half]], axis=-1)
    return gradient * cosine_table + turned


def doc_layout(doc_edges, device, rows_per_block):
    token_index = device * rows_per_block + jnp.arange(rows_per_block, dtype=jnp.int32)
    segment = (token_index >= doc_edges[0]).astype(jnp.int32) + (
        token_index >= doc_edges[1]
    ).astype(jnp.int32)
    starts = jnp.where(segment == 0, 0, jnp.where(segment == 1, doc_edges[0], doc_edges[1]))
    return (token_index, segment, token_index - starts)


def visible_mask(doc_edges, query_device, key_device, rows_per_block):
    query_index, query_segment, query_position = doc_layout(doc_edges, query_device, rows_per_block)
    key_index, key_segment, key_position = doc_layout(doc_edges, key_device, rows_per_block)
    return (key_index[None, :] <= query_index[:, None]) & (
        key_segment[None, :] == query_segment[:, None]
    )


def attend_block(query_head_set, key_block, value_block, visible, running, score_scale):
    row_peak, row_mass, summed = running
    scores = (
        jnp.einsum("jgqd,kjd->jgqk", query_head_set, key_block, preferred_element_type=jnp.float32)
        * score_scale
    )
    scores = jnp.where(visible, scores, NEGATIVE_FILL)
    new_peak = jnp.maximum(row_peak, jnp.max(scores, axis=-1))
    weights_soft = jnp.where(visible, jnp.exp(scores - new_peak[..., None]), 0.0)
    factor = jnp.exp(row_peak - new_peak)
    row_mass = row_mass * factor + jnp.sum(weights_soft, axis=-1)
    summed = summed * factor[..., None] + jnp.einsum(
        "jgqk,kjd->jgqd",
        weights_soft.astype(jnp.bfloat16),
        value_block,
        preferred_element_type=jnp.float32,
    )
    return (new_peak, row_mass, summed)


def grad_block(
    query_head_set,
    heads_gradient,
    log_total,
    grad_dot,
    key_block,
    value_block,
    visible,
    score_scale,
):
    scores = (
        jnp.einsum("jgqd,kjd->jgqk", query_head_set, key_block, preferred_element_type=jnp.float32)
        * score_scale
    )
    weights_soft = jnp.where(visible, jnp.exp(scores - log_total[..., None]), 0.0)
    value_gradient = jnp.einsum(
        "jgqk,jgqd->kjd",
        weights_soft.astype(jnp.bfloat16),
        heads_gradient,
        preferred_element_type=jnp.float32,
    )
    weight_grad = jnp.einsum(
        "jgqd,kjd->jgqk", heads_gradient, value_block, preferred_element_type=jnp.float32
    )
    score_grad = (weights_soft * (weight_grad - grad_dot[..., None])).astype(jnp.bfloat16)
    query_grad = (
        jnp.einsum("jgqk,kjd->jgqd", score_grad, key_block, preferred_element_type=jnp.float32)
        * score_scale
    )
    key_gradient = (
        jnp.einsum("jgqk,jgqd->kjd", score_grad, query_head_set, preferred_element_type=jnp.float32)
        * score_scale
    )
    return (query_grad, key_gradient, value_gradient)


def per_device(
    layer_input,
    doc_bounds,
    attn_gain,
    w_query,
    key_weight,
    value_weight,
    w_out,
    mlp_gain,
    w_gate,
    w_up,
    w_down,
    cotangent,
):
    cycle_size = lax.axis_size("ctx")
    my_index = lax.axis_index("ctx")
    rows_per_block = layer_input.shape[1]
    group_count = QUERY_HEADS // KEY_VALUE_HEADS
    score_scale = HEAD_SIZE ** (-0.5)
    doc_edges = doc_bounds[0]
    single_float = jnp.float32
    brain_float_half = jnp.bfloat16
    gain_attn, full_query, complete_key, full_value, full_out = (
        lax.all_gather(attn_gain, "wt", axis=0, tiled=True),
        lax.all_gather(w_query, "wt", axis=0, tiled=True),
        lax.all_gather(key_weight, "wt", axis=0, tiled=True),
        lax.all_gather(value_weight, "wt", axis=0, tiled=True),
        lax.all_gather(w_out, "wt", axis=0, tiled=True),
    )
    gain_mlp, full_gate, full_up, full_down = (
        lax.all_gather(mlp_gain, "wt", axis=0, tiled=True),
        lax.all_gather(w_gate, "wt", axis=0, tiled=True),
        lax.all_gather(w_up, "wt", axis=0, tiled=True),
        lax.all_gather(w_down, "wt", axis=0, tiled=True),
    )
    gain_attn_f = gain_attn.astype(single_float)
    gain_mlp_f = gain_mlp.astype(single_float)
    residual_in = layer_input[0].astype(single_float)
    normed_attn, normal_attn, inverse_attn = rms_forward(residual_in, gain_attn_f)
    normalized_reduced = normed_attn.astype(brain_float_half)
    query_raw = jnp.dot(
        normalized_reduced, full_query, preferred_element_type=single_float
    ).reshape(rows_per_block, QUERY_HEADS, HEAD_SIZE)
    unrotated_key = jnp.dot(
        normalized_reduced, complete_key, preferred_element_type=single_float
    ).reshape(rows_per_block, KEY_VALUE_HEADS, HEAD_SIZE)
    value_low = (
        jnp.dot(normalized_reduced, full_value, preferred_element_type=single_float)
        .astype(brain_float_half)
        .reshape(rows_per_block, KEY_VALUE_HEADS, HEAD_SIZE)
    )
    own_index, own_segment, positions = doc_layout(doc_edges, my_index, rows_per_block)
    cosine_table, sine_table = rope_tables(positions)
    query_reduced = rotate_forward(query_raw, cosine_table, sine_table).astype(brain_float_half)
    key_low = rotate_forward(unrotated_key, cosine_table, sine_table).astype(brain_float_half)
    query_head_set = query_reduced.reshape(
        rows_per_block, KEY_VALUE_HEADS, group_count, HEAD_SIZE
    ).transpose(1, 2, 0, 3)

    def forward_step(running, key_block, value_block, source_dev):
        visible = visible_mask(doc_edges, my_index, source_dev, rows_per_block)

        def forward_active(current):
            return attend_block(
                query_head_set, key_block, value_block, visible, current, score_scale
            )

        return lax.cond(source_dev <= my_index, forward_active, keep_state, running)

    def cycle_forward(step_index, carry):
        running, moving = carry
        running = forward_step(running, moving[0], moving[1], (my_index - step_index) % cycle_size)
        moving = shifted((moving[0], moving[1]), "ctx", 1)
        return (running, moving)

    running = (
        jnp.full((KEY_VALUE_HEADS, group_count, rows_per_block), NEGATIVE_FILL, single_float),
        jnp.zeros((KEY_VALUE_HEADS, group_count, rows_per_block), single_float),
        jnp.zeros((KEY_VALUE_HEADS, group_count, rows_per_block, HEAD_SIZE), single_float),
    )
    running, moving = lax.fori_loop(
        0, cycle_size - 1, cycle_forward, (running, (key_low, value_low))
    )
    running = forward_step(
        running, moving[0], moving[1], (my_index - (cycle_size - 1)) % cycle_size
    )
    row_peak, row_mass, summed = running
    attended = summed / row_mass[..., None]
    log_total = row_peak + jnp.log(row_mass)
    mixed_low = (
        attended.transpose(2, 0, 1, 3)
        .reshape(rows_per_block, QUERY_HEADS * HEAD_SIZE)
        .astype(brain_float_half)
    )
    resid = residual_in + jnp.dot(mixed_low, full_out, preferred_element_type=single_float)
    normed_mlp, normal_mlp, inverse_mlp = rms_forward(resid, gain_mlp_f)
    normed_two = normed_mlp.astype(brain_float_half)
    gate_pre = jnp.dot(normed_two, full_gate, preferred_element_type=single_float)
    up_part = jnp.dot(normed_two, full_up, preferred_element_type=single_float)
    gate_sigmoid = jax.nn.sigmoid(gate_pre)
    activated = gate_pre * gate_sigmoid
    hidden_low = (activated * up_part).astype(brain_float_half)
    output = resid + jnp.dot(hidden_low, full_down, preferred_element_type=single_float)
    layer_output = output.astype(brain_float_half)[None]
    upstream = cotangent[0]
    grad_w_down = jnp.dot(hidden_low.T, upstream, preferred_element_type=single_float)
    grad_hidden = jnp.dot(upstream, full_down.T, preferred_element_type=single_float)
    grad_up_in = (grad_hidden * activated).astype(brain_float_half)
    grad_gate_in = (
        grad_hidden * up_part * gate_sigmoid * (1.0 + gate_pre * (1.0 - gate_sigmoid))
    ).astype(brain_float_half)
    grad_w_gate = jnp.dot(normed_two.T, grad_gate_in, preferred_element_type=single_float)
    grad_w_up = jnp.dot(normed_two.T, grad_up_in, preferred_element_type=single_float)
    grad_normed_two = jnp.dot(
        grad_gate_in, full_gate.T, preferred_element_type=single_float
    ) + jnp.dot(grad_up_in, full_up.T, preferred_element_type=single_float)
    grad_resid_mlp, grad_mlp_gain = rms_backward(
        grad_normed_two, gain_mlp_f, normal_mlp, inverse_mlp
    )
    grad_resid = upstream.astype(single_float) + grad_resid_mlp
    grad_mixed = grad_resid.astype(brain_float_half)
    grad_w_out = jnp.dot(mixed_low.T, grad_mixed, preferred_element_type=single_float)
    attended_gradient = jnp.dot(grad_mixed, full_out.T, preferred_element_type=single_float).astype(
        brain_float_half
    )
    heads_gradient = attended_gradient.reshape(
        rows_per_block, KEY_VALUE_HEADS, group_count, HEAD_SIZE
    ).transpose(1, 2, 0, 3)
    grad_dot = jnp.sum(heads_gradient.astype(single_float) * attended, axis=-1)
    empty_query = jnp.zeros((KEY_VALUE_HEADS, group_count, rows_per_block, HEAD_SIZE), single_float)
    empty_pair = jnp.zeros((rows_per_block, KEY_VALUE_HEADS, HEAD_SIZE), single_float)

    def block_compute(step_index, key_block, value_block, accums):
        source_dev = (my_index - step_index) % cycle_size
        visible = visible_mask(doc_edges, my_index, source_dev, rows_per_block)

        def block_active(parts):
            query_more, key_more, value_more = grad_block(
                query_head_set,
                heads_gradient,
                log_total,
                grad_dot,
                key_block,
                value_block,
                visible,
                score_scale,
            )
            return (parts[0] + query_more, parts[1] + key_more, parts[2] + value_more)

        return lax.cond(source_dev <= my_index, block_active, keep_state, accums)

    def pass_grads(key_acc, value_acc):
        return (
            from_behind(key_acc.astype(jnp.bfloat16), "ctx", 1).astype(key_acc.dtype),
            from_behind(value_acc.astype(jnp.bfloat16), "ctx", 1).astype(value_acc.dtype),
        )

    def block_loop(step_index, carry):
        moving, accums = carry
        moving = shifted((moving[0], moving[1]), "ctx", 1)
        key_acc, value_acc = pass_grads(accums[1], accums[2])
        accums = block_compute(step_index, moving[0], moving[1], (accums[0], key_acc, value_acc))
        return (moving, accums)

    accums = block_compute(0, key_low, value_low, (empty_query, empty_pair, empty_pair))
    moving, accums = lax.fori_loop(1, cycle_size, block_loop, ((key_low, value_low), accums))
    query_grad = accums[0]
    key_gradient, value_gradient = pass_grads(accums[1], accums[2])
    query_turned = query_grad.transpose(2, 0, 1, 3).reshape(rows_per_block, QUERY_HEADS, HEAD_SIZE)
    grad_query_low = (
        rotation_backward(query_turned, cosine_table, sine_table)
        .reshape(rows_per_block, QUERY_HEADS * HEAD_SIZE)
        .astype(brain_float_half)
    )
    grad_key_low = (
        rotation_backward(key_gradient, cosine_table, sine_table)
        .reshape(rows_per_block, KEY_VALUE_HEADS * HEAD_SIZE)
        .astype(brain_float_half)
    )
    value_gradient_reduced = value_gradient.reshape(
        rows_per_block, KEY_VALUE_HEADS * HEAD_SIZE
    ).astype(brain_float_half)
    grad_w_query = jnp.dot(
        normalized_reduced.T, grad_query_low, preferred_element_type=single_float
    )
    grad_w_key = jnp.dot(normalized_reduced.T, grad_key_low, preferred_element_type=single_float)
    grad_w_value = jnp.dot(
        normalized_reduced.T, value_gradient_reduced, preferred_element_type=single_float
    )
    grad_normed = jnp.dot(grad_query_low, full_query.T, preferred_element_type=single_float)
    grad_normed = grad_normed + jnp.dot(
        grad_key_low, complete_key.T, preferred_element_type=single_float
    )
    grad_normed = grad_normed + jnp.dot(
        value_gradient_reduced, full_value.T, preferred_element_type=single_float
    )
    grad_input_attn, grad_attn_gain = rms_backward(
        grad_normed, gain_attn_f, normal_attn, inverse_attn
    )
    input_grad = (grad_resid + grad_input_attn)[None]
    (
        attn_gain_part,
        query_part,
        key_part,
        value_part,
        out_part,
        mlp_gain_part,
        gate_part,
        up_weight_part,
        down_part,
    ) = (
        lax.psum_scatter(
            grad_attn_gain.astype(jnp.bfloat16), "wt", scatter_dimension=0, tiled=True
        ).astype(jnp.float32),
        lax.psum_scatter(
            grad_w_query.astype(jnp.bfloat16), "wt", scatter_dimension=0, tiled=True
        ).astype(jnp.float32),
        lax.psum_scatter(
            grad_w_key.astype(jnp.bfloat16), "wt", scatter_dimension=0, tiled=True
        ).astype(jnp.float32),
        lax.psum_scatter(
            grad_w_value.astype(jnp.bfloat16), "wt", scatter_dimension=0, tiled=True
        ).astype(jnp.float32),
        lax.psum_scatter(
            grad_w_out.astype(jnp.bfloat16), "wt", scatter_dimension=0, tiled=True
        ).astype(jnp.float32),
        lax.psum_scatter(
            grad_mlp_gain.astype(jnp.bfloat16), "wt", scatter_dimension=0, tiled=True
        ).astype(jnp.float32),
        lax.psum_scatter(
            grad_w_gate.astype(jnp.bfloat16), "wt", scatter_dimension=0, tiled=True
        ).astype(jnp.float32),
        lax.psum_scatter(
            grad_w_up.astype(jnp.bfloat16), "wt", scatter_dimension=0, tiled=True
        ).astype(jnp.float32),
        lax.psum_scatter(
            grad_w_down.astype(jnp.bfloat16), "wt", scatter_dimension=0, tiled=True
        ).astype(jnp.float32),
    )
    every_sum = (
        lax.psum(attn_gain_part.astype(jnp.bfloat16), "ctx").astype(jnp.float32),
        lax.psum(query_part.astype(jnp.bfloat16), "ctx").astype(jnp.float32),
        lax.psum(key_part.astype(jnp.bfloat16), "ctx").astype(jnp.float32),
        lax.psum(value_part.astype(jnp.bfloat16), "ctx").astype(jnp.float32),
        lax.psum(out_part.astype(jnp.bfloat16), "ctx").astype(jnp.float32),
        lax.psum(mlp_gain_part.astype(jnp.bfloat16), "ctx").astype(jnp.float32),
        lax.psum(gate_part.astype(jnp.bfloat16), "ctx").astype(jnp.float32),
        lax.psum(up_weight_part.astype(jnp.bfloat16), "ctx").astype(jnp.float32),
        lax.psum(down_part.astype(jnp.bfloat16), "ctx").astype(jnp.float32),
    )
    return (
        layer_output,
        input_grad,
        every_sum[0],
        every_sum[1],
        every_sum[2],
        every_sum[3],
        every_sum[4],
        every_sum[5],
        every_sum[6],
        every_sum[7],
        every_sum[8],
    )


def solution(mesh):
    return jax.shard_map(
        per_device,
        mesh=mesh,
        in_specs=(
            P("wt", "ctx", None),
            P("wt", None),
            P("wt"),
            P("wt", None),
            P("wt", None),
            P("wt", None),
            P("wt", None),
            P("wt"),
            P("wt", None),
            P("wt", None),
            P("wt", None),
            P("wt", "ctx", None),
        ),
        out_specs=(
            P("wt", "ctx", None),
            P("wt", "ctx", None),
            P("wt"),
            P("wt", None),
            P("wt", None),
            P("wt", None),
            P("wt", None),
            P("wt"),
            P("wt", None),
            P("wt", None),
            P("wt", None),
        ),
        check_vma=False,
    )
```

profile of v0, /device:TPU:1, one launch (start us, length us, event | category | flops | bytes accessed | tf_op | source)
XLA Modules:
  0.0 1630.5 jit_solution(11818366438945758711)
XLA Ops:
  18.3 14.9 all-gather
  36.2 8.5 all-reduce.7
  45.7 11.0 all-gather.1
  65.5 406.2 %while.46 = (s32[]{:T(128)}, f32[5,3,256]{2,1,0:T(4,128)S(1)}, f32[5,3,256]{2,1,0:T(4,128)S(1)}, f32[5,3,256,64]{2,3,1,0:T(8,128)S(1)}, bf16[256,5,64]{0,2,1:T(8...) while((s32[]{:T(128)}, f32[5,3,256]{2,1,0:T(4,128)S(1)}, ...), condition=%wide.region_6.7_spmd, body=%wide.region_1.6_spmd.sunk | while | flops 265137168 | bytes 17072696 | solution.py:217
  66.1 11.5 collective-permute-start
  115.0 7.8 collective-permute-start
  133.5 6.9 collective-permute-start.1
  154.6 8.8 collective-permute-start
  194.3 8.7 collective-permute-start
  214.0 6.9 collective-permute-start.1
  235.0 7.2 collective-permute-start
  488.3 7.6 multiply_convert_fusion.2
  506.2 8.0 conditional.5
  514.2 667.1 %while.47 = (s32[]{:T(128)}, bf16[256,5,64]{0,2,1:T(8,128)(2,1)S(1)}, bf16[256,5,64]{0,2,1:T(8,128)(2,1)}, f32[5,3,256,64]{2,3,1,0:T(8,128)S(1)}, f32[256,5,64]{...) while((s32[]{:T(128)}, ...), condition=%wide.region_19.20_spmd, body=%wide.region_16.19_spmd.sunk | while | flops 640241152 | bytes 28931768 | solution.py:302
  530.7 7.0 conditional.9
  555.5 11.4 collective-permute-start.2
  583.0 9.1 collective-permute-start.3
  608.2 10.8 collective-permute-start.4
  635.9 7.1 collective-permute-start.5
  664.2 11.3 collective-permute-start.2
  691.7 8.3 collective-permute-start.3
  717.0 10.8 collective-permute-start.4
  771.8 10.6 collective-permute-start.2
  799.3 8.3 collective-permute-start.3
  823.9 10.7 collective-permute-start.4
  852.3 6.4 collective-permute-start.5
  880.5 10.6 collective-permute-start.2
  908.1 7.5 collective-permute-start.3
  932.5 10.8 collective-permute-start.4
  986.2 10.6 collective-permute-start.2
  1013.7 8.3 collective-permute-start.3
  1038.3 10.7 collective-permute-start.4
  1066.7 6.4 collective-permute-start.5
  1094.9 10.6 collective-permute-start.2
  1122.5 7.5 collective-permute-start.3
  1146.9 10.8 collective-permute-start.4
  1183.1 16.0 collective-permute-done.6
  1203.6 16.9 %collective-permute-done.7 = bf16[256,5,64]{0,2,1:T(8,128)(2,1)S(1)} collective-permute-done((bf16[256,5,64]{0,2,1:T(8,128)(2,1)S(1)}, bf16[256,5,64]{0,2,1:T(8,128)(2,1)S(1)}, u32[]{:S(2)}, u32[]{:S(2)}) %collective-permute-start.7) | collective-permute-done | bytes 163872 | tf_op jit(solution)/shard_map/ppermute | solution.py:24
  1227.3 7.9 copy.60
  1253.6 6.2 reduce-scatter.24.cloned.1.call-done
  1261.5 57.0 %reduce-scatter.26.cloned.1.call-done = bf16[640,960]{1,0:T(8,128)(2,1)} async-done(((bf16[2560,960]{1,0:T(8,128)(2,1)}), bf16[640,960]{1,0:T(8,128)(2,1)}) %reduce-scatter.26.cloned.1.call-update) | async-done | bytes 1228816
  1320.9 28.9 %reduce-scatter.14.cloned.1.call-done = bf16[240,960]{1,0:T(8,128)(2,1)} async-done(((bf16[960,960]{1,0:T(8,128)(2,1)}), bf16[240,960]{1,0:T(8,128)(2,1)}) %reduce-scatter.14.cloned.1.call-update) | async-done | bytes 460816 | tf_op jit(solution)/shard_map/reduce_scatter | solution.py:351
  1349.8 31.2 %reduce-scatter.16.cloned.1.call-done = bf16[240,960]{1,0:T(8,128)(2,1)} async-done(((bf16[960,960]{1,0:T(8,128)(2,1)}), bf16[240,960]{1,0:T(8,128)(2,1)}) %reduce-scatter.16.cloned.1.call-update) | async-done | bytes 460816 | tf_op jit(solution)/shard_map/reduce_scatter | solution.py:360
  1381.0 54.9 %reduce-scatter.18.cloned.1.call-done = bf16[240,2560]{1,0:T(8,128)(2,1)} async-done(((bf16[960,2560]{1,0:T(8,128)(2,1)}), bf16[240,2560]{1,0:T(8,128)(2,1)}) %reduce-scatter.18.cloned.1.call-update) | async-done | bytes 1228816 | tf_op jit(solution)/shard_map/reduce_scatter | solution.py:366
  1435.9 54.9 %reduce-scatter.20.cloned.1.call-done = bf16[240,2560]{1,0:T(8,128)(2,1)} async-done(((bf16[960,2560]{1,0:T(8,128)(2,1)}), bf16[240,2560]{1,0:T(8,128)(2,1)}) %reduce-scatter.20.cloned.1.call-update) | async-done | bytes 1228816 | tf_op jit(solution)/shard_map/reduce_scatter | solution.py:369
  1501.3 7.0 all-reduce.6
  1508.4 64.9 %all-reduce.4 = (bf16[240]{0:T(256)(128)(2,1)S(1)}, bf16[240]{0:T(256)(128)(2,1)S(1)}) all-reduce(bf16[240]{0:T(256)(128)(2,1)S(1)} %dynamic-slice.3, bf16[240]{0:T(256)(128)(2,1)S(1)} %dynamic-slice.5), channel_id=1, replica_groups=mesh['ctx'=32,'wt'=4] {'ctx'}, use_global_device_ids=true, to_apply=%region_23.24 | all-reduce | flops 480 | bytes 1920 | tf_op jit(solution)/shard_map/psum | solution.py:377
  1575.6 35.2 %all-reduce.10.cloned.1.call-done = (bf16[240,960]{1,0:T(8,128)(2,1)}, bf16[240,320]{0,1:T(8,128)(2,1)}, bf16[240,320]{0,1:T(8,128)(2,1)}, bf16[240,960]{1,0:T(8...) async-done(((bf16[240,960]{1,0:T(8,128)(2,1)}, bf16[240,320]{0,1:T(8,128)(2,1)}, bf16[240,320]{0,1:T(8,128)(2,1)}, ...) | async-done | bytes 4915216 | tf_op jit(solution)/shard_map/psum | solution.py:378
  (1207 shorter events, 938.2 us)
Async XLA Ops:
  7.2 51.1 %all-gather.8.cloned.1.call-start = ((), (), s32[]{:S(2)}) async-start(), calls=%async_computation.7 | async-start | bytes 2457600 | tf_op jit(solution)/shard_map/all_gather | solution.py:161
  8.0 465.5 %all-gather.10.cloned.1.call-start = ((), (), s32[]{:S(2)}) async-start(), calls=%async_computation.8 | async-start | bytes 2457600 | tf_op jit(solution)/shard_map/all_gather | solution.py:164
  8.7 468.6 %all-gather.12.cloned.1.call-start = ((), (), s32[]{:S(2)}) async-start(), calls=%async_computation.9 | async-start | bytes 6144000 | tf_op jit(solution)/shard_map/all_gather | solution.py:168
  9.5 473.3 %all-gather.14.cloned.1.call-start = ((), (), s32[]{:S(2)}) async-start(), calls=%async_computation.10 | async-start | bytes 6144000 | tf_op jit(solution)/shard_map/all_gather | solution.py:169
  10.0 478.2 %all-gather.16.cloned.1.call-start = ((), (), s32[]{:S(2)}) async-start(), calls=%async_computation.11 | async-start | bytes 6144000 | tf_op jit(solution)/shard_map/all_gather | solution.py:170
  10.6 1241.2 %reduce-scatter.22.cloned.1.call-start = ((), (), s32[]{:S(2)}) async-start(), calls=%async_computation.16 | async-start | bytes 921600
  66.1 22.4 %collective-permute-start = (bf16[256,5,64]{0,2,1:T(8,128)(2,1)}, bf16[256,5,64]{0,2,1:T(8,128)(2,1)S(1)}, u32[]{:S(2)}, u32[]{:S(2)}) collective-permute-start(bf16[256,5,64]{0,2,1:T(8,128)(2,1)} %copy.86), channel_id=1, source_target_pairs={{0,4},{4,8},{8,12},{12,16},{16,20},{20,24},{24,28},{28,32},{32,36}... | collective-permute-start | bytes 491528 | tf_op jit(solution)/shard_map/while/body/eval_jaxpr/ppermute | solution.py:18
  555.5 22.4 %collective-permute-start.2 = (bf16[256,5,64]{0,2,1:T(8,128)(2,1)S(1)}, bf16[256,5,64]{0,2,1:T(8,128)(2,1)S(1)}, u32[]{:S(2)}, u32[]{:S(2)}) collective-permute-start(bf16[256,5,64]{0,2,1:T(8,128)(2,1)S(1)} %get-tuple-element.1249), channel_id=1, source_target_pairs={{0,4},{4,8},{8,12},{12,16},{16,20},{20,24},{24,28},{28,32},{32,36}... | collective-permute-start | bytes 491528 | tf_op jit(solution)/shard_map/while/body/eval_jaxpr/ppermute | solution.py:18
  578.6 22.4 %collective-permute-start.2 = (bf16[256,5,64]{0,2,1:T(8,128)(2,1)S(1)}, bf16[256,5,64]{0,2,1:T(8,128)(2,1)S(1)}, u32[]{:S(2)}, u32[]{:S(2)}) collective-permute-start(bf16[256,5,64]{0,2,1:T(8,128)(2,1)S(1)} %get-tuple-element.1249), channel_id=1, source_target_pairs={{0,4},{4,8},{8,12},{12,16},{16,20},{20,24},{24,28},{28,32},{32,36}... | collective-permute-start | bytes 491528 | tf_op jit(solution)/shard_map/while/body/eval_jaxpr/ppermute | solution.py:18
  583.0 18.0 %collective-permute-start.3 = (bf16[256,5,64]{0,2,1:T(8,128)(2,1)}, bf16[256,5,64]{0,2,1:T(8,128)(2,1)S(1)}, u32[]{:S(2)}, u32[]{:S(2)}) collective-permute-start(bf16[256,5,64]{0,2,1:T(8,128)(2,1)} %get-tuple-element.1250), channel_id=1, source_target_pairs={{0,4},{4,8},{8,12},{12,16},{16,20},{20,24},{24,28},{28,32},{32,36}... | collective-permute-start | bytes 491528 | tf_op jit(solution)/shard_map/while/body/eval_jaxpr/ppermute | solution.py:18
  601.8 22.4 %collective-permute-start.2 = (bf16[256,5,64]{0,2,1:T(8,128)(2,1)S(1)}, bf16[256,5,64]{0,2,1:T(8,128)(2,1)S(1)}, u32[]{:S(2)}, u32[]{:S(2)}) collective-permute-start(bf16[256,5,64]{0,2,1:T(8,128)(2,1)S(1)} %get-tuple-element.1249), channel_id=1, source_target_pairs={{0,4},{4,8},{8,12},{12,16},{16,20},{20,24},{24,28},{28,32},{32,36}... | collective-permute-start | bytes 491528 | tf_op jit(solution)/shard_map/while/body/eval_jaxpr/ppermute | solution.py:18
  606.1 18.0 %collective-permute-start.3 = (bf16[256,5,64]{0,2,1:T(8,128)(2,1)}, bf16[256,5,64]{0,2,1:T(8,128)(2,1)S(1)}, u32[]{:S(2)}, u32[]{:S(2)}) collective-permute-start(bf16[256,5,64]{0,2,1:T(8,128)(2,1)} %get-tuple-element.1250), channel_id=1, source_target_pairs={{0,4},{4,8},{8,12},{12,16},{16,20},{20,24},{24,28},{28,32},{32,36}... | collective-permute-start | bytes 491528 | tf_op jit(solution)/shard_map/while/body/eval_jaxpr/ppermute | solution.py:18
  624.9 22.4 %collective-permute-start.2 = (bf16[256,5,64]{0,2,1:T(8,128)(2,1)S(1)}, bf16[256,5,64]{0,2,1:T(8,128)(2,1)S(1)}, u32[]{:S(2)}, u32[]{:S(2)}) collective-permute-start(bf16[256,5,64]{0,2,1:T(8,128)(2,1)S(1)} %get-tuple-element.1249), channel_id=1, source_target_pairs={{0,4},{4,8},{8,12},{12,16},{16,20},{20,24},{24,28},{28,32},{32,36}... | collective-permute-start | bytes 491528 | tf_op jit(solution)/shard_map/while/body/eval_jaxpr/ppermute | solution.py:18
  629.3 18.0 %collective-permute-start.3 = (bf16[256,5,64]{0,2,1:T(8,128)(2,1)}, bf16[256,5,64]{0,2,1:T(8,128)(2,1)S(1)}, u32[]{:S(2)}, u32[]{:S(2)}) collective-permute-start(bf16[256,5,64]{0,2,1:T(8,128)(2,1)} %get-tuple-element.1250), channel_id=1, source_target_pairs={{0,4},{4,8},{8,12},{12,16},{16,20},{20,24},{24,28},{28,32},{32,36}... | collective-permute-start | bytes 491528 | tf_op jit(solution)/shard_map/while/body/eval_jaxpr/ppermute | solution.py:18
  664.2 22.4 %collective-permute-start.2 = (bf16[256,5,64]{0,2,1:T(8,128)(2,1)S(1)}, bf16[256,5,64]{0,2,1:T(8,128)(2,1)S(1)}, u32[]{:S(2)}, u32[]{:S(2)}) collective-permute-start(bf16[256,5,64]{0,2,1:T(8,128)(2,1)S(1)} %get-tuple-element.1249), channel_id=1, source_target_pairs={{0,4},{4,8},{8,12},{12,16},{16,20},{20,24},{24,28},{28,32},{32,36}... | collective-permute-start | bytes 491528 | tf_op jit(solution)/shard_map/while/body/eval_jaxpr/ppermute | solution.py:18
  687.3 22.4 %collective-permute-start.2 = (bf16[256,5,64]{0,2,1:T(8,128)(2,1)S(1)}, bf16[256,5,64]{0,2,1:T(8,128)(2,1)S(1)}, u32[]{:S(2)}, u32[]{:S(2)}) collective-permute-start(bf16[256,5,64]{0,2,1:T(8,128)(2,1)S(1)} %get-tuple-element.1249), channel_id=1, source_target_pairs={{0,4},{4,8},{8,12},{12,16},{16,20},{20,24},{24,28},{28,32},{32,36}... | collective-permute-start | bytes 491528 | tf_op jit(solution)/shard_map/while/body/eval_jaxpr/ppermute | solution.py:18
  691.7 18.0 %collective-permute-start.3 = (bf16[256,5,64]{0,2,1:T(8,128)(2,1)}, bf16[256,5,64]{0,2,1:T(8,128)(2,1)S(1)}, u32[]{:S(2)}, u32[]{:S(2)}) collective-permute-start(bf16[256,5,64]{0,2,1:T(8,128)(2,1)} %get-tuple-element.1250), channel_id=1, source_target_pairs={{0,4},{4,8},{8,12},{12,16},{16,20},{20,24},{24,28},{28,32},{32,36}... | collective-permute-start | bytes 491528 | tf_op jit(solution)/shard_map/while/body/eval_jaxpr/ppermute | solution.py:18
  710.5 22.4 %collective-permute-start.2 = (bf16[256,5,64]{0,2,1:T(8,128)(2,1)S(1)}, bf16[256,5,64]{0,2,1:T(8,128)(2,1)S(1)}, u32[]{:S(2)}, u32[]{:S(2)}) collective-permute-start(bf16[256,5,64]{0,2,1:T(8,128)(2,1)S(1)} %get-tuple-element.1249), channel_id=1, source_target_pairs={{0,4},{4,8},{8,12},{12,16},{16,20},{20,24},{24,28},{28,32},{32,36}... | collective-permute-start | bytes 491528 | tf_op jit(solution)/shard_map/while/body/eval_jaxpr/ppermute | solution.py:18
  714.9 18.0 %collective-permute-start.3 = (bf16[256,5,64]{0,2,1:T(8,128)(2,1)}, bf16[256,5,64]{0,2,1:T(8,128)(2,1)S(1)}, u32[]{:S(2)}, u32[]{:S(2)}) collective-permute-start(bf16[256,5,64]{0,2,1:T(8,128)(2,1)} %get-tuple-element.1250), channel_id=1, source_target_pairs={{0,4},{4,8},{8,12},{12,16},{16,20},{20,24},{24,28},{28,32},{32,36}... | collective-permute-start | bytes 491528 | tf_op jit(solution)/shard_map/while/body/eval_jaxpr/ppermute | solution.py:18
  733.6 20.5 %collective-permute-start.2 = (bf16[256,5,64]{0,2,1:T(8,128)(2,1)S(1)}, bf16[256,5,64]{0,2,1:T(8,128)(2,1)S(1)}, u32[]{:S(2)}, u32[]{:S(2)}) collective-permute-start(bf16[256,5,64]{0,2,1:T(8,128)(2,1)S(1)} %get-tuple-element.1249), channel_id=1, source_target_pairs={{0,4},{4,8},{8,12},{12,16},{16,20},{20,24},{24,28},{28,32},{32,36}... | collective-permute-start | bytes 491528 | tf_op jit(solution)/shard_map/while/body/eval_jaxpr/ppermute | solution.py:18
  771.8 22.4 %collective-permute-start.2 = (bf16[256,5,64]{0,2,1:T(8,128)(2,1)S(1)}, bf16[256,5,64]{0,2,1:T(8,128)(2,1)S(1)}, u32[]{:S(2)}, u32[]{:S(2)}) collective-permute-start(bf16[256,5,64]{0,2,1:T(8,128)(2,1)S(1)} %get-tuple-element.1249), channel_id=1, source_target_pairs={{0,4},{4,8},{8,12},{12,16},{16,20},{20,24},{24,28},{28,32},{32,36}... | collective-permute-start | bytes 491528 | tf_op jit(solution)/shard_map/while/body/eval_jaxpr/ppermute | solution.py:18
  795.0 21.7 %collective-permute-start.2 = (bf16[256,5,64]{0,2,1:T(8,128)(2,1)S(1)}, bf16[256,5,64]{0,2,1:T(8,128)(2,1)S(1)}, u32[]{:S(2)}, u32[]{:S(2)}) collective-permute-start(bf16[256,5,64]{0,2,1:T(8,128)(2,1)S(1)} %get-tuple-element.1249), channel_id=1, source_target_pairs={{0,4},{4,8},{8,12},{12,16},{16,20},{20,24},{24,28},{28,32},{32,36}... | collective-permute-start | bytes 491528 | tf_op jit(solution)/shard_map/while/body/eval_jaxpr/ppermute | solution.py:18
  817.4 22.3 %collective-permute-start.2 = (bf16[256,5,64]{0,2,1:T(8,128)(2,1)S(1)}, bf16[256,5,64]{0,2,1:T(8,128)(2,1)S(1)}, u32[]{:S(2)}, u32[]{:S(2)}) collective-permute-start(bf16[256,5,64]{0,2,1:T(8,128)(2,1)S(1)} %get-tuple-element.1249), channel_id=1, source_target_pairs={{0,4},{4,8},{8,12},{12,16},{16,20},{20,24},{24,28},{28,32},{32,36}... | collective-permute-start | bytes 491528 | tf_op jit(solution)/shard_map/while/body/eval_jaxpr/ppermute | solution.py:18
  821.8 17.9 %collective-permute-start.3 = (bf16[256,5,64]{0,2,1:T(8,128)(2,1)}, bf16[256,5,64]{0,2,1:T(8,128)(2,1)S(1)}, u32[]{:S(2)}, u32[]{:S(2)}) collective-permute-start(bf16[256,5,64]{0,2,1:T(8,128)(2,1)} %get-tuple-element.1250), channel_id=1, source_target_pairs={{0,4},{4,8},{8,12},{12,16},{16,20},{20,24},{24,28},{28,32},{32,36}... | collective-permute-start | bytes 491528 | tf_op jit(solution)/shard_map/while/body/eval_jaxpr/ppermute | solution.py:18
  840.5 22.4 %collective-permute-start.2 = (bf16[256,5,64]{0,2,1:T(8,128)(2,1)S(1)}, bf16[256,5,64]{0,2,1:T(8,128)(2,1)S(1)}, u32[]{:S(2)}, u32[]{:S(2)}) collective-permute-start(bf16[256,5,64]{0,2,1:T(8,128)(2,1)S(1)} %get-tuple-element.1249), channel_id=1, source_target_pairs={{0,4},{4,8},{8,12},{12,16},{16,20},{20,24},{24,28},{28,32},{32,36}... | collective-permute-start | bytes 491528 | tf_op jit(solution)/shard_map/while/body/eval_jaxpr/ppermute | solution.py:18
  844.8 18.0 %collective-permute-start.3 = (bf16[256,5,64]{0,2,1:T(8,128)(2,1)}, bf16[256,5,64]{0,2,1:T(8,128)(2,1)S(1)}, u32[]{:S(2)}, u32[]{:S(2)}) collective-permute-start(bf16[256,5,64]{0,2,1:T(8,128)(2,1)} %get-tuple-element.1250), channel_id=1, source_target_pairs={{0,4},{4,8},{8,12},{12,16},{16,20},{20,24},{24,28},{28,32},{32,36}... | collective-permute-start | bytes 491528 | tf_op jit(solution)/shard_map/while/body/eval_jaxpr/ppermute | solution.py:18
  880.5 22.4 %collective-permute-start.2 = (bf16[256,5,64]{0,2,1:T(8,128)(2,1)S(1)}, bf16[256,5,64]{0,2,1:T(8,128)(2,1)S(1)}, u32[]{:S(2)}, u32[]{:S(2)}) collective-permute-start(bf16[256,5,64]{0,2,1:T(8,128)(2,1)S(1)} %get-tuple-element.1249), channel_id=1, source_target_pairs={{0,4},{4,8},{8,12},{12,16},{16,20},{20,24},{24,28},{28,32},{32,36}... | collective-permute-start | bytes 491528 | tf_op jit(solution)/shard_map/while/body/eval_jaxpr/ppermute | solution.py:18
  903.7 21.6 %collective-permute-start.2 = (bf16[256,5,64]{0,2,1:T(8,128)(2,1)S(1)}, bf16[256,5,64]{0,2,1:T(8,128)(2,1)S(1)}, u32[]{:S(2)}, u32[]{:S(2)}) collective-permute-start(bf16[256,5,64]{0,2,1:T(8,128)(2,1)S(1)} %get-tuple-element.1249), channel_id=1, source_target_pairs={{0,4},{4,8},{8,12},{12,16},{16,20},{20,24},{24,28},{28,32},{32,36}... | collective-permute-start | bytes 491528 | tf_op jit(solution)/shard_map/while/body/eval_jaxpr/ppermute | solution.py:18
  926.0 22.4 %collective-permute-start.2 = (bf16[256,5,64]{0,2,1:T(8,128)(2,1)S(1)}, bf16[256,5,64]{0,2,1:T(8,128)(2,1)S(1)}, u32[]{:S(2)}, u32[]{:S(2)}) collective-permute-start(bf16[256,5,64]{0,2,1:T(8,128)(2,1)S(1)} %get-tuple-element.1249), channel_id=1, source_target_pairs={{0,4},{4,8},{8,12},{12,16},{16,20},{20,24},{24,28},{28,32},{32,36}... | collective-permute-start | bytes 491528 | tf_op jit(solution)/shard_map/while/body/eval_jaxpr/ppermute | solution.py:18
  930.4 18.0 %collective-permute-start.3 = (bf16[256,5,64]{0,2,1:T(8,128)(2,1)}, bf16[256,5,64]{0,2,1:T(8,128)(2,1)S(1)}, u32[]{:S(2)}, u32[]{:S(2)}) collective-permute-start(bf16[256,5,64]{0,2,1:T(8,128)(2,1)} %get-tuple-element.1250), channel_id=1, source_target_pairs={{0,4},{4,8},{8,12},{12,16},{16,20},{20,24},{24,28},{28,32},{32,36}... | collective-permute-start | bytes 491528 | tf_op jit(solution)/shard_map/while/body/eval_jaxpr/ppermute | solution.py:18
  949.2 19.3 %collective-permute-start.2 = (bf16[256,5,64]{0,2,1:T(8,128)(2,1)S(1)}, bf16[256,5,64]{0,2,1:T(8,128)(2,1)S(1)}, u32[]{:S(2)}, u32[]{:S(2)}) collective-permute-start(bf16[256,5,64]{0,2,1:T(8,128)(2,1)S(1)} %get-tuple-element.1249), channel_id=1, source_target_pairs={{0,4},{4,8},{8,12},{12,16},{16,20},{20,24},{24,28},{28,32},{32,36}... | collective-permute-start | bytes 491528 | tf_op jit(solution)/shard_map/while/body/eval_jaxpr/ppermute | solution.py:18
  986.2 22.4 %collective-permute-start.2 = (bf16[256,5,64]{0,2,1:T(8,128)(2,1)S(1)}, bf16[256,5,64]{0,2,1:T(8,128)(2,1)S(1)}, u32[]{:S(2)}, u32[]{:S(2)}) collective-permute-start(bf16[256,5,64]{0,2,1:T(8,128)(2,1)S(1)} %get-tuple-element.1249), channel_id=1, source_target_pairs={{0,4},{4,8},{8,12},{12,16},{16,20},{20,24},{24,28},{28,32},{32,36}... | collective-permute-start | bytes 491528 | tf_op jit(solution)/shard_map/while/body/eval_jaxpr/ppermute | solution.py:18
  1009.4 21.7 %collective-permute-start.2 = (bf16[256,5,64]{0,2,1:T(8,128)(2,1)S(1)}, bf16[256,5,64]{0,2,1:T(8,128)(2,1)S(1)}, u32[]{:S(2)}, u32[]{:S(2)}) collective-permute-start(bf16[256,5,64]{0,2,1:T(8,128)(2,1)S(1)} %get-tuple-element.1249), channel_id=1, source_target_pairs={{0,4},{4,8},{8,12},{12,16},{16,20},{20,24},{24,28},{28,32},{32,36}... | collective-permute-start | bytes 491528 | tf_op jit(solution)/shard_map/while/body/eval_jaxpr/ppermute | solution.py:18
  1031.8 22.3 %collective-permute-start.2 = (bf16[256,5,64]{0,2,1:T(8,128)(2,1)S(1)}, bf16[256,5,64]{0,2,1:T(8,128)(2,1)S(1)}, u32[]{:S(2)}, u32[]{:S(2)}) collective-permute-start(bf16[256,5,64]{0,2,1:T(8,128)(2,1)S(1)} %get-tuple-element.1249), channel_id=1, source_target_pairs={{0,4},{4,8},{8,12},{12,16},{16,20},{20,24},{24,28},{28,32},{32,36}... | collective-permute-start | bytes 491528 | tf_op jit(solution)/shard_map/while/body/eval_jaxpr/ppermute | solution.py:18
  1036.2 17.9 %collective-permute-start.3 = (bf16[256,5,64]{0,2,1:T(8,128)(2,1)}, bf16[256,5,64]{0,2,1:T(8,128)(2,1)S(1)}, u32[]{:S(2)}, u32[]{:S(2)}) collective-permute-start(bf16[256,5,64]{0,2,1:T(8,128)(2,1)} %get-tuple-element.1250), channel_id=1, source_target_pairs={{0,4},{4,8},{8,12},{12,16},{16,20},{20,24},{24,28},{28,32},{32,36}... | collective-permute-start | bytes 491528 | tf_op jit(solution)/shard_map/while/body/eval_jaxpr/ppermute | solution.py:18
  1054.9 22.4 %collective-permute-start.2 = (bf16[256,5,64]{0,2,1:T(8,128)(2,1)S(1)}, bf16[256,5,64]{0,2,1:T(8,128)(2,1)S(1)}, u32[]{:S(2)}, u32[]{:S(2)}) collective-permute-start(bf16[256,5,64]{0,2,1:T(8,128)(2,1)S(1)} %get-tuple-element.1249), channel_id=1, source_target_pairs={{0,4},{4,8},{8,12},{12,16},{16,20},{20,24},{24,28},{28,32},{32,36}... | collective-permute-start | bytes 491528 | tf_op jit(solution)/shard_map/while/body/eval_jaxpr/ppermute | solution.py:18
  1059.2 18.0 %collective-permute-start.3 = (bf16[256,5,64]{0,2,1:T(8,128)(2,1)}, bf16[256,5,64]{0,2,1:T(8,128)(2,1)S(1)}, u32[]{:S(2)}, u32[]{:S(2)}) collective-permute-start(bf16[256,5,64]{0,2,1:T(8,128)(2,1)} %get-tuple-element.1250), channel_id=1, source_target_pairs={{0,4},{4,8},{8,12},{12,16},{16,20},{20,24},{24,28},{28,32},{32,36}... | collective-permute-start | bytes 491528 | tf_op jit(solution)/shard_map/while/body/eval_jaxpr/ppermute | solution.py:18
  1094.9 22.4 %collective-permute-start.2 = (bf16[256,5,64]{0,2,1:T(8,128)(2,1)S(1)}, bf16[256,5,64]{0,2,1:T(8,128)(2,1)S(1)}, u32[]{:S(2)}, u32[]{:S(2)}) collective-permute-start(bf16[256,5,64]{0,2,1:T(8,128)(2,1)S(1)} %get-tuple-element.1249), channel_id=1, source_target_pairs={{0,4},{4,8},{8,12},{12,16},{16,20},{20,24},{24,28},{28,32},{32,36}... | collective-permute-start | bytes 491528 | tf_op jit(solution)/shard_map/while/body/eval_jaxpr/ppermute | solution.py:18
  1118.1 21.6 %collective-permute-start.2 = (bf16[256,5,64]{0,2,1:T(8,128)(2,1)S(1)}, bf16[256,5,64]{0,2,1:T(8,128)(2,1)S(1)}, u32[]{:S(2)}, u32[]{:S(2)}) collective-permute-start(bf16[256,5,64]{0,2,1:T(8,128)(2,1)S(1)} %get-tuple-element.1249), channel_id=1, source_target_pairs={{0,4},{4,8},{8,12},{12,16},{16,20},{20,24},{24,28},{28,32},{32,36}... | collective-permute-start | bytes 491528 | tf_op jit(solution)/shard_map/while/body/eval_jaxpr/ppermute | solution.py:18
  1140.4 22.4 %collective-permute-start.2 = (bf16[256,5,64]{0,2,1:T(8,128)(2,1)S(1)}, bf16[256,5,64]{0,2,1:T(8,128)(2,1)S(1)}, u32[]{:S(2)}, u32[]{:S(2)}) collective-permute-start(bf16[256,5,64]{0,2,1:T(8,128)(2,1)S(1)} %get-tuple-element.1249), channel_id=1, source_target_pairs={{0,4},{4,8},{8,12},{12,16},{16,20},{20,24},{24,28},{28,32},{32,36}... | collective-permute-start | bytes 491528 | tf_op jit(solution)/shard_map/while/body/eval_jaxpr/ppermute | solution.py:18
  1144.8 18.0 %collective-permute-start.3 = (bf16[256,5,64]{0,2,1:T(8,128)(2,1)}, bf16[256,5,64]{0,2,1:T(8,128)(2,1)S(1)}, u32[]{:S(2)}, u32[]{:S(2)}) collective-permute-start(bf16[256,5,64]{0,2,1:T(8,128)(2,1)} %get-tuple-element.1250), channel_id=1, source_target_pairs={{0,4},{4,8},{8,12},{12,16},{16,20},{20,24},{24,28},{28,32},{32,36}... | collective-permute-start | bytes 491528 | tf_op jit(solution)/shard_map/while/body/eval_jaxpr/ppermute | solution.py:18
  1203.5 56.3 %reduce-scatter.24.cloned.1.call-start = ((), (), s32[]{:S(2)}) async-start(), calls=%async_computation.17 | async-start | bytes 921600
  1222.1 96.3 %reduce-scatter.26.cloned.1.call-start = ((), (), s32[]{:S(2)}) async-start(), calls=%async_computation.18 | async-start | bytes 6553600
  1235.2 114.6 %reduce-scatter.14.cloned.1.call-start = ((), (), s32[]{:S(2)}) async-start(), calls=%async_computation.12 | async-start | bytes 2457600 | tf_op jit(solution)/shard_map/reduce_scatter | solution.py:351
  1239.4 141.6 %reduce-scatter.16.cloned.1.call-start = ((), (), s32[]{:S(2)}) async-start(), calls=%async_computation.13 | async-start | bytes 2457600 | tf_op jit(solution)/shard_map/reduce_scatter | solution.py:360
  1241.5 194.4 %reduce-scatter.18.cloned.1.call-start = ((), (), s32[]{:S(2)}) async-start(), calls=%async_computation.14 | async-start | bytes 6144000 | tf_op jit(solution)/shard_map/reduce_scatter | solution.py:366
  1246.6 244.2 %reduce-scatter.20.cloned.1.call-start = ((), (), s32[]{:S(2)}) async-start(), calls=%async_computation.15 | async-start | bytes 6144000 | tf_op jit(solution)/shard_map/reduce_scatter | solution.py:369
  1251.8 359.0 %all-reduce.10.cloned.1.call-start = ((), (), s32[]{:S(2)}) async-start(), calls=%async_computation.19 | async-start | bytes 9994240 | tf_op jit(solution)/shard_map/psum | solution.py:378
  (197 other events, 2651.9 us)
Sparse Core Ops, SparseCore 0:
  9.7 36.5 all-gather.7
  48.0 31.3 all-gather.9
  81.1 54.0 all-gather.11
  136.6 54.6 all-gather.13
  192.9 54.6 all-gather.15
  1203.6 31.7 reduce-scatter.21
  1237.8 21.9 reduce-scatter.23
  1262.2 56.2 reduce-scatter.25
  1321.5 28.3 reduce-scatter.13
  1352.7 28.3 reduce-scatter.15
  1383.5 52.3 reduce-scatter.17
  1438.3 52.4 reduce-scatter.19
  1495.8 114.9 all-reduce.9
where the time goes:
time: 1650 us; the launch traced here: 1630 us
  starting transfers between devices  737 us (45%)
  waiting for transfers between devices  306 us (19%)
  other arithmetic  246 us (15%)
  local copies, waits for them, and re-layouts  127 us (8%)
  blocking collectives  106 us (6%)
  matrix products  82.6 us (5%)
  between operations  16.5 us (1%)
    ppermute x124, starting transfers between devices, shifted(): return lax.ppermute(array, axis, pairs)  529 us
    ppermute x64, starting transfers between devices, from_behind(): return lax.ppermute(block, axis, route)  208 us
    convert_element_type x126, other arithmetic, doc_layout(): segment = (token_index >= doc_edges[0]).astype(jnp.int32) + (token_index...  164 us
    unnamed x16, waiting for transfers between devices  66.4 us
    psum x1, blocking collectives, per_device(): lax.psum(attn_gain_part.astype(jnp.bfloat16), 'ctx').astype(jnp.float32)  64.9 us
    reduce_scatter x1, waiting for transfers between devices, per_device(): lax.psum_scatter(grad_w_up.astype(jnp.bfloat16), 'wt', scatter_dimension=...  54.9 us
    reduce_scatter x1, waiting for transfers between devices, per_device(): lax.psum_scatter(grad_w_gate.astype(jnp.bfloat16), 'wt', scatter_dimensio...  54.9 us
    another operation x63, local copies, waits for them, and re-layouts  41.6 us
  transfers between devices with their start and end apart: 201, of which 11 were waited for; matrix products, arithmetic and copies ran while one was open for 23% of the time, Pallas kernels for 0%

commit v1 on v0

v1 whole, which is shorter than its diff:
```python
import functools

import jax
import jax.numpy as jnp
from jax import lax
from jax.experimental import pallas as pl
from jax.experimental.pallas import tpu as pltpu
from jax.sharding import PartitionSpec as P

QUERY_HEADS = 15
KEY_VALUE_HEADS = 5
HEAD_SIZE = 64
GROUP = QUERY_HEADS // KEY_VALUE_HEADS
PAIR = 2 * HEAD_SIZE
EPSILON = 1e-05
NEG = -1e30
BIG = 1e30
LOG2E = 1.4426950408889634
F32 = jnp.float32
BF16 = jnp.bfloat16
HEAD_SETS = ((0, KEY_VALUE_HEADS),)


def dot_f32(left, right, dims=((1,), (0,))):
    return lax.dot_general(left, right, (dims, ((), ())), preferred_element_type=F32)


def ranges(me, half):
    light = me < half
    first = jnp.where(light, 0, me - half + 1)
    mirrored = jnp.where(light, half - me, 0)
    return first, mirrored


def visible_pairs(b0, b1, key_start, query_start, rows):
    key = key_start + lax.broadcasted_iota(jnp.int32, (rows, rows), 0)
    query = query_start + lax.broadcasted_iota(jnp.int32, (rows, rows), 1)
    return (key <= query) & ((key >= b0) | (query < b0)) & ((key >= b1) | (query < b1))


def sweep(me, n, step):
    first, mirrored = ranges(me, n // 2)
    step_own = lambda block, masked, diagonal: step(0, block, masked, diagonal)

    @pl.when((first == 0) & (me > 0))
    def _():
        step_own(0, True, False)

    def own(block, carry):
        step_own(block, False, False)
        return carry

    lax.fori_loop(jnp.maximum(first, 1), me, own, 0)
    step_own(me, True, True)

    @pl.when(mirrored > 0)
    def _():
        step(1, 0, True, False)

        def other(block, carry):
            step(1, block, False, False)
            return carry

        lax.fori_loop(1, mirrored, other, 0)


def forward_kernel(n, place, kv_ref, q_ref, o_ref, stat_ref, peak, mass, total):
    me, b0, b1 = place[0], place[1], place[2]
    rows = q_ref.shape[-1]
    peak[...] = jnp.full_like(peak, NEG)
    mass[...] = jnp.zeros_like(mass)
    total[...] = jnp.zeros_like(total)

    def step(which, block, masked, diagonal):
        kv = kv_ref[block]
        v_turned = kv.T[HEAD_SIZE:]
        if diagonal:
            query = me * rows + lax.broadcasted_iota(jnp.int32, (1, rows), 1)
            fresh = query >= b1
            for g in range(GROUP):
                peak[which, g] = jnp.where(fresh, NEG, peak[which, g])
                mass[which, g] = jnp.where(fresh, 0.0, mass[which, g])
                total[which, g] = jnp.where(fresh, 0.0, total[which, g])
        if masked:
            owner = me if which == 0 else n - 1 - me
            seen = visible_pairs(b0, b1, block * rows, owner * rows, rows)
        for g in range(GROUP):
            scores = dot_f32(kv, q_ref[which, g])
            if masked:
                scores = jnp.where(seen, scores, NEG)
            old = peak[which, g]
            new = jnp.maximum(old, jnp.max(scores, axis=0, keepdims=True))
            weights = jnp.exp2((scores - new) * LOG2E)
            factor = jnp.exp2((old - new) * LOG2E)
            peak[which, g] = new
            mass[which, g] = mass[which, g] * factor + jnp.sum(weights, axis=0, keepdims=True)
            total[which, g] = total[which, g] * factor + dot_f32(v_turned, weights.astype(BF16))

    sweep(me, n, step)
    for which in range(2):
        for g in range(GROUP):
            held = mass[which, g]
            live = held > 0.0
            safe = jnp.where(live, held, 1.0)
            o_ref[which, g] = total[which, g] / safe
            stat_ref[which, g] = jnp.where(live, peak[which, g] + jnp.log(safe), NEG)


def backward_kernel(n, place, kv_ref, q_ref, do_ref, q_flat, do_flat, stat_ref, dq_ref, dkv_ref, gathered):
    me, b0, b1 = place[0], place[1], place[2]
    rows = q_ref.shape[-1]
    half = n // 2
    first, _ = ranges(me, half)
    gathered[...] = jnp.zeros_like(gathered)
    dq_ref[...] = jnp.zeros_like(dq_ref)

    def step(which, block, masked, diagonal):
        kv = kv_ref[block]
        k_turned = kv.T[:HEAD_SIZE]
        stats = 2 if diagonal else which
        if masked:
            owner = me if which == 0 else n - 1 - me
            seen = visible_pairs(b0, b1, block * rows, owner * rows, rows)
        more = jnp.zeros((rows, PAIR), F32)
        for g in range(GROUP):
            scores = dot_f32(kv, q_ref[which, g])
            weights = jnp.exp2((scores - stat_ref[stats, g, 0:1]) * LOG2E)
            if masked:
                weights = jnp.where(seen, weights, 0.0)
            weight_grad = dot_f32(kv, do_ref[which, g])
            score_grad = (weights * (weight_grad - stat_ref[stats, g, 1:2])).astype(BF16)
            more += dot_f32(score_grad, q_flat[which, g])
            more += dot_f32(weights.astype(BF16), do_flat[which, g])
            dq_ref[which, g] += dot_f32(k_turned, score_grad)
        gathered[block - first] += more

    sweep(me, n, step)
    for block in range(n):
        slot = block - first
        inside = (slot >= 0) & (slot < half)

        @pl.when(inside)
        def _():
            dkv_ref[block] = gathered[slot].astype(BF16)

        @pl.when(jnp.logical_not(inside))
        def _():
            dkv_ref[block] = jnp.zeros(dkv_ref.shape[1:], BF16)


def whole_set(per_head):
    return pl.BlockSpec(per_head, lambda j: (0, j) + (0,) * (len(per_head) - 2))


def attention_forward(n, place, kv, q_turned):
    heads, rows = kv.shape[0], kv.shape[2]
    units = (n + 1) * heads
    return pl.pallas_call(
        functools.partial(forward_kernel, n),
        grid=(heads,),
        out_shape=(
            jax.ShapeDtypeStruct((2, heads * GROUP, HEAD_SIZE, rows), F32),
            jax.ShapeDtypeStruct((2, heads * GROUP, 1, rows), F32),
        ),
        in_specs=[
            pl.BlockSpec(memory_space=pltpu.SMEM),
            pl.BlockSpec((None, n, rows, PAIR), lambda j: (j, 0, 0, 0)),
            whole_set((2, GROUP, PAIR, rows)),
        ],
        out_specs=(whole_set((2, GROUP, HEAD_SIZE, rows)), whole_set((2, GROUP, 1, rows))),
        scratch_shapes=[
            pltpu.VMEM((2, GROUP, 1, rows), F32),
            pltpu.VMEM((2, GROUP, 1, rows), F32),
            pltpu.VMEM((2, GROUP, HEAD_SIZE, rows), F32),
        ],
        compiler_params=pltpu.CompilerParams(vmem_limit_bytes=40 * 2**20),
        cost_estimate=pl.CostEstimate(
            flops=units * GROUP * rows * rows * 4 * PAIR,
            bytes_accessed=2 * n * rows * PAIR * heads,
            transcendentals=units * GROUP * rows * rows,
        ),
        name="attend_forward",
    )(place, kv, q_turned)


def attention_backward(n, place, kv, q_turned, do_turned, q_flat, do_flat, stats):
    heads, rows = kv.shape[0], kv.shape[2]
    units = (n + 1) * heads
    return pl.pallas_call(
        functools.partial(backward_kernel, n),
        grid=(heads,),
        out_shape=(
            jax.ShapeDtypeStruct((2, heads * GROUP, HEAD_SIZE, rows), F32),
            jax.ShapeDtypeStruct((heads, n, rows, PAIR), BF16),
        ),
        in_specs=[
            pl.BlockSpec(memory_space=pltpu.SMEM),
            pl.BlockSpec((None, n, rows, PAIR), lambda j: (j, 0, 0, 0)),
            whole_set((2, GROUP, PAIR, rows)),
            whole_set((2, GROUP, PAIR, rows)),
            whole_set((2, GROUP, rows, PAIR)),
            whole_set((2, GROUP, rows, PAIR)),
            whole_set((3, GROUP, 2, rows)),
        ],
        out_specs=(
            whole_set((2, GROUP, HEAD_SIZE, rows)),
            pl.BlockSpec((None, n, rows, PAIR), lambda j: (j, 0, 0, 0)),
        ),
        scratch_shapes=[pltpu.VMEM((n // 2, rows, PAIR), F32)],
        compiler_params=pltpu.CompilerParams(vmem_limit_bytes=40 * 2**20),
        cost_estimate=pl.CostEstimate(
            flops=units * GROUP * rows * rows * 10 * PAIR,
            bytes_accessed=4 * n * rows * PAIR * heads,
            transcendentals=units * GROUP * rows * rows,
        ),
        name="attend_backward",
    )(place, kv, q_turned, do_turned, q_flat, do_flat, stats)


def rms_forward(values, gain):
    inverse = lax.rsqrt(jnp.mean(values * values, axis=-1, keepdims=True) + EPSILON)
    normal = values * inverse
    return (normal * gain, normal, inverse)


def rms_backward(upstream, gain, normal, inverse):
    scaled = upstream * gain
    inner = jnp.mean(scaled * normal, axis=-1, keepdims=True)
    return (inverse * (scaled - normal * inner), jnp.sum(upstream * normal, axis=0))


def positions_of(edges, me, rows):
    token = me * rows + jnp.arange(rows, dtype=jnp.int32)
    start = jnp.where(token >= edges[1], edges[1], jnp.where(token >= edges[0], edges[0], 0))
    return token, token - start


def turn(heads, cosine, sine):
    half = HEAD_SIZE // 2
    low, high = heads[:, :half], heads[:, half:]
    return jnp.concatenate([low * cosine - high * sine, high * cosine + low * sine], axis=1)


def turn_back(heads, cosine, sine):
    half = HEAD_SIZE // 2
    low, high = heads[:, :half], heads[:, half:]
    return jnp.concatenate([low * cosine + high * sine, high * cosine - low * sine], axis=1)


def three_parts(values):
    first = lax.reduce_precision(values, 8, 7)
    rest = values - first
    second = lax.reduce_precision(rest, 8, 7)
    third = rest - second
    return [part.astype(BF16) for part in (first, second, third)]


def joined(parts):
    return parts[0].astype(F32) + parts[1].astype(F32) + parts[2].astype(F32)


def gather_weight(shard):
    return lax.all_gather(shard, "wt", axis=0, tiled=True)


def reduce_gradient(gradient):
    part = lax.psum_scatter(gradient.astype(BF16), "wt", scatter_dimension=0, tiled=True)
    return lax.psum(part, "ctx").astype(F32)


def per_device(
    layer_input,
    doc_bounds,
    attn_gain,
    w_query,
    key_weight,
    value_weight,
    w_out,
    mlp_gain,
    w_gate,
    w_up,
    w_down,
    cotangent,
):
    n = lax.axis_size("ctx")
    me = lax.axis_index("ctx")
    rows, width = layer_input.shape[1:]
    queries = QUERY_HEADS * HEAD_SIZE
    keys = KEY_VALUE_HEADS * HEAD_SIZE
    edges = doc_bounds[0]
    place = jnp.concatenate([jnp.full((1,), me, jnp.int32), edges])
    across = [(i, n - 1 - i) for i in range(n)]

    gains = jnp.pad(jnp.stack([attn_gain, mlp_gain], axis=1), ((0, 0), (0, 62)))
    shard_qkv = jnp.concatenate([w_query, key_weight, value_weight, gains], axis=1)
    full_qkv = gather_weight(shard_qkv)
    gain_rows = full_qkv[:, queries + 2 * keys : queries + 2 * keys + 2].T.astype(F32)
    attn_scale, mlp_scale = gain_rows[0], gain_rows[1]
    full_qkv = full_qkv[:, : queries + 2 * keys]

    x = layer_input[0].astype(F32)
    normed, normal_in, inverse_in = rms_forward(x, attn_scale)
    normed = normed.astype(BF16)
    turned = dot_f32(full_qkv, normed, ((0,), (1,)))
    token, position = positions_of(edges, me, rows)
    freqs = 10000.0 ** (-jnp.arange(HEAD_SIZE // 2, dtype=F32) * 2.0 / HEAD_SIZE)
    angles = freqs[:, None] * position.astype(F32)[None, :]
    cosine, sine = jnp.cos(angles), jnp.sin(angles)

    q = turn(turned[:queries].reshape(QUERY_HEADS, HEAD_SIZE, rows), cosine, sine).astype(BF16)
    k = turn(turned[queries : queries + keys].reshape(KEY_VALUE_HEADS, HEAD_SIZE, rows), cosine, sine).astype(BF16)
    v = turned[queries + keys :].reshape(KEY_VALUE_HEADS, HEAD_SIZE, rows).astype(BF16)
    q = q * BF16(HEAD_SIZE**-0.5)
    own_kv = jnp.concatenate([k, v], axis=1).transpose(0, 2, 1)

    kv_sets = [lax.all_gather(own_kv[j : j + c], "ctx", axis=1) for j, c in HEAD_SETS]
    q_both = jnp.stack([q, lax.ppermute(q, "ctx", across)])
    blank = jnp.zeros_like(q_both)
    q_turned = jnp.concatenate([q_both, blank], axis=2)
    q_flat = q_turned.transpose(0, 1, 3, 2)

    later = token >= edges[1]
    own_o, own_stat = [], []
    for (j, c), kv in zip(HEAD_SETS, kv_sets):
        some = slice(j * GROUP, (j + c) * GROUP)
        o_part, stat_part = attention_forward(n, place, kv, q_turned[:, some])
        sent = jnp.concatenate([o_part[1].astype(BF16)] + three_parts(stat_part[1]) , axis=1)
        got = lax.ppermute(sent, "ctx", across)
        other_stat = joined([got[:, HEAD_SIZE + i : HEAD_SIZE + i + 1] for i in range(3)])
        other_stat = jnp.where(later, NEG, other_stat)
        stat = jnp.logaddexp(stat_part[0], other_stat)
        own_o.append(
            o_part[0] * jnp.exp(stat_part[0] - stat)
            + got[:, :HEAD_SIZE].astype(F32) * jnp.exp(other_stat - stat)
        )
        own_stat.append(stat)
    attended = jnp.concatenate(own_o)
    log_total = jnp.concatenate(own_stat)
    mixed = attended.reshape(queries, rows).astype(BF16)

    full_out = gather_weight(w_out)
    full_gate = gather_weight(w_gate)
    full_up = gather_weight(w_up)
    full_down = gather_weight(w_down)
    resid = x + dot_f32(mixed, full_out, ((0,), (0,)))
    normed_two, normal_mlp, inverse_mlp = rms_forward(resid, mlp_scale)
    normed_two = normed_two.astype(BF16)
    gate = dot_f32(normed_two, full_gate)
    up = dot_f32(normed_two, full_up)
    sig = jax.nn.sigmoid(gate)
    activated = gate * sig
    hidden = (activated * up).astype(BF16)
    layer_output = (resid + dot_f32(hidden, full_down)).astype(BF16)[None]
    upstream = cotangent[0]
    grad_w_down = dot_f32(hidden, upstream, ((0,), (0,)))
    grad_hidden = dot_f32(upstream, full_down, ((1,), (1,)))
    grad_up_in = (grad_hidden * activated).astype(BF16)
    grad_gate_in = (grad_hidden * up * sig * (1.0 + gate * (1.0 - sig))).astype(BF16)
    grad_w_gate = dot_f32(normed_two, grad_gate_in, ((0,), (0,)))
    grad_w_up = dot_f32(normed_two, grad_up_in, ((0,), (0,)))
    grad_normed_two = dot_f32(grad_gate_in, full_gate, ((1,), (1,))) + dot_f32(
        grad_up_in, full_up, ((1,), (1,))
    )
    grad_resid_mlp, grad_mlp_gain = rms_backward(grad_normed_two, mlp_scale, normal_mlp, inverse_mlp)
    grad_resid = upstream.astype(F32) + grad_resid_mlp
    grad_mixed = grad_resid.astype(BF16)
    grad_w_out = dot_f32(mixed, grad_mixed)
    grad_attended = dot_f32(full_out, grad_mixed, ((1,), (1,))).astype(BF16)
    grad_attended = grad_attended.reshape(QUERY_HEADS, HEAD_SIZE, rows)
    grad_dot = jnp.sum(grad_attended.astype(F32) * attended, axis=1, keepdims=True)

    before = jnp.where(later, BIG, log_total)
    sent = jnp.concatenate([grad_attended] + three_parts(before) + three_parts(grad_dot), axis=1)
    got = lax.ppermute(sent, "ctx", across)
    piece = lambda i: got[:, HEAD_SIZE + i : HEAD_SIZE + i + 1]
    stats = jnp.stack(
        [
            jnp.concatenate([before, grad_dot], axis=1),
            jnp.concatenate([joined([piece(0), piece(1), piece(2)]), joined([piece(3), piece(4), piece(5)])], axis=1),
            jnp.concatenate([log_total, grad_dot], axis=1),
        ]
    )
    do_both = jnp.stack([grad_attended, got[:, :HEAD_SIZE]])
    do_turned = jnp.concatenate([blank, do_both], axis=2)
    do_flat = do_turned.transpose(0, 1, 3, 2)
    dq_all, dkv_all = [], []
    for (j, c), kv in zip(HEAD_SETS, kv_sets):
        some = slice(j * GROUP, (j + c) * GROUP)
        dq, dkv = attention_backward(
            n, place, kv, q_turned[:, some], do_turned[:, some], q_flat[:, some], do_flat[:, some], stats[:, some]
        )
        other = lax.ppermute(dq[1].astype(BF16), "ctx", across)
        dq_all.append(dq[0] + other.astype(F32))
        dkv_all.append(lax.psum_scatter(dkv, "ctx", scatter_dimension=1, tiled=False))
    grad_q = turn_back(jnp.concatenate(dq_all) * HEAD_SIZE**-0.5, cosine, sine).astype(BF16)
    dkv = jnp.concatenate(dkv_all).astype(F32).transpose(0, 2, 1)
    grad_k = turn_back(dkv[:, :HEAD_SIZE], cosine, sine).astype(BF16)
    grad_v = dkv[:, HEAD_SIZE:].astype(BF16)
    grad_qkv = jnp.concatenate(
        [grad_q.reshape(queries, rows), grad_k.reshape(keys, rows), grad_v.reshape(keys, rows)]
    )
    grad_w_qkv = dot_f32(normed, grad_qkv, ((0,), (1,)))
    grad_normed = dot_f32(grad_qkv, full_qkv, ((0,), (1,)))
    grad_in, grad_attn_gain = rms_backward(grad_normed, attn_scale, normal_in, inverse_in)
    input_grad = (grad_resid + grad_in)[None]

    sum_qkv = reduce_gradient(grad_w_qkv)
    gain_sum = lax.psum(jnp.stack([grad_attn_gain, grad_mlp_gain]).astype(BF16), ("wt", "ctx"))
    mine = lax.dynamic_slice_in_dim(gain_sum, lax.axis_index("wt") * attn_gain.shape[0], attn_gain.shape[0], 1)
    mine = mine.astype(F32)
    return (
        layer_output,
        input_grad,
        mine[0],
        sum_qkv[:, :queries],
        sum_qkv[:, queries : queries + keys],
        sum_qkv[:, queries + keys :],
        reduce_gradient(grad_w_out),
        mine[1],
        reduce_gradient(grad_w_gate),
        reduce_gradient(grad_w_up),
        reduce_gradient(grad_w_down),
    )


def solution(mesh):
    tokens, weights, gains = P("wt", "ctx", None), P("wt", None), P("wt")
    return jax.shard_map(
        per_device,
        mesh=mesh,
        in_specs=(
            tokens, weights, gains, weights, weights, weights, weights, gains, weights, weights, weights, tokens,
        ),
        out_specs=(
            tokens, tokens, gains, weights, weights, weights, weights, gains, weights, weights, weights,
        ),
        check_vma=False,
    )
```

time: 1650 us -> 978 us (0.59)
  starting transfers between devices: 737 us -> 12.9 us
  waiting for transfers between devices: 306 us -> 569 us
  other arithmetic: 246 us -> 33.7 us
  Pallas kernels: 0 us -> 153 us
  local copies, waits for them, and re-layouts: 127 us -> 59.5 us
  blocking collectives: 106 us -> 65.6 us
  matrix products: 82.6 us -> 59.6 us
    ppermute x188 -> x4, starting transfers between devices: 737 us -> 12.4 us  [the longest x2 5.99 us: per_device(): got = lax.ppermute(sent, 'ctx', across)]
    convert_element_type x271 -> x13, other arithmetic: 234 us -> 10.7 us  [the longest x4 6.09 us: reduce_gradient(): return lax.psum(part, 'ctx').astype(F32)]
    pallas_call x0 -> x2, Pallas kernels: none -> 153 us  [the longest x1 76.6 us: attention_forward(): pl.pallas_call(functools.partial(forward_kernel, n), grid=(heads,), out_s...]
    all_gather x5 -> x6, waiting for transfers between devices: 0.07 us -> 151 us  [the longest x5 123 us: gather_weight(): return lax.all_gather(shard, 'wt', axis=0, tiled=True)]
    unnamed x16 -> x15, waiting for transfers between devices: 66.4 us -> 135 us
    another operation x63 -> x7, local copies, waits for them, and re-layouts: 41.6 us -> 1.82 us  [the longest x2 1.32 us: per_device(): gains = jnp.pad(jnp.stack([attn_gain, mlp_gain], axis=1), ((0, 0), (0, 62)))]
    slice x63 -> x12, local copies, waits for them, and re-layouts: 36.7 us -> 4.23 us  [the longest x1 1.3 us: per_device(): sum_qkv[:, queries + keys:]]
    all_gather x2 -> x0, blocking collectives: 26 us -> none  [the longest x1 14.9 us: per_device(): lax.all_gather(key_weight, 'wt', axis=0, tiled=True)]
  transfers between devices with their start and end apart: 201 -> 17, of which waited for: 11 -> 15; matrix products, arithmetic and copies ran while one was open for 23% -> 9% of each run, Pallas kernels for 0% -> 8%
where the time goes in v1:
time: 978 us; the launch traced here: 968 us
  waiting for transfers between devices  569 us (58%)
  Pallas kernels  153 us (16%)
  blocking collectives  65.6 us (7%)
  matrix products  59.6 us (6%)
  local copies, waits for them, and re-layouts  59.5 us (6%)
  other arithmetic  33.7 us (3%)
  between operations  15 us (2%)
  starting transfers between devices  12.9 us (1%)
    reduce_scatter x4, waiting for transfers between devices, reduce_gradient(): lax.psum_scatter(gradient.astype(BF16), 'wt', scatter_dimension=0, tiled=...  180 us
    unnamed x15, waiting for transfers between devices  135 us
    all_gather x5, waiting for transfers between devices, gather_weight(): return lax.all_gather(shard, 'wt', axis=0, tiled=True)  123 us
    pallas_call x1, Pallas kernels, attention_forward(): pl.pallas_call(functools.partial(forward_kernel, n), grid=(heads,), out_s...  76.6 us
    pallas_call x1, Pallas kernels, attention_backward(): pl.pallas_call(functools.partial(backward_kernel, n), grid=(heads,), out_...  76.4 us
    psum x1, blocking collectives, per_device(): lax.psum(jnp.stack([grad_attn_gain, grad_mlp_gain]).astype(BF16), ('wt',...  65.6 us
    dot_general x15, matrix products, dot_f32(): lax.dot_general(left, right, (dims, ((), ())), preferred_element_type=F32)  59.6 us
    psum x1, waiting for transfers between devices, reduce_gradient(): return lax.psum(part, 'ctx').astype(F32)  43.7 us
  transfers between devices with their start and end apart: 17, of which 15 were waited for; matrix products, arithmetic and copies ran while one was open for 9% of the time, Pallas kernels for 8%

profile of v1, /device:TPU:1, one launch (start us, length us, event | category | flops | bytes accessed | tf_op | source)
XLA Modules:
  0.0 968.0 jit_solution(10137589100370126767)
XLA Ops:
  11.0 2.0 concatenate.63
  15.3 40.9 %all-gather.8.cloned.1.call-done = bf16[960,1664]{1,0:T(8,128)(2,1)} async-done(((bf16[240,1664]{1,0:T(8,128)(2,1)}), bf16[960,1664]{1,0:T(8,128)(2,1)}) %all-gather.8.cloned.1.call-update) | async-done | bytes 3194896 | tf_op jit(solution)/shard_map/all_gather | solution.py:263
  57.8 3.2 fusion.6
  65.8 1.8 copy.110
  67.6 1.8 copy.111
  69.5 2.7 subtract_convert_fusion.1
  73.9 5.4 collective-permute-start
  80.9 14.6 %collective-permute-done = bf16[15,64,256]{2,1,0:T(8,128)(2,1)S(1)} collective-permute-done((bf16[15,64,256]{2,1,0:T(8,128)(2,1)}, bf16[15,64,256]{2,1,0:T(8,128)(2,1)S(1)}, u32[]{:S(2)}, u32[]{:S(2)}) %collective-permute-start) | collective-permute-done | bytes 491552 | tf_op jit(solution)/shard_map/ppermute | solution.py:317
  96.8 3.1 fusion.58
  99.9 2.3 copy.90.q_ref
  102.2 27.6 %all-gather.18.cloned.1.call-done = bf16[5,8192,128]{2,1,0:T(8,128)(2,1)} async-done(((bf16[5,256,128]{2,1,0:T(8,128)(2,1)}), bf16[5,8192,128]{2,1,0:T(8,128)(2,1)}) %all-gather.18.cloned.1.call-update) | async-done | bytes 10485776 | tf_op jit(solution)/shard_map/all_gather | solution.py:316
  131.4 4.0 copy-done.5
  135.3 76.6 %attend_forward.1 = (f32[2,15,64,256]{3,2,1,0:T(8,128)S(1)}, f32[2,15,1,256]{3,2,1,0:T(1,128)S(1)}) custom-call(s32[3]{0:T(128)S(1)} %pad_add_fusion.place, bf16[5,32,256,128]{3,2,1,0:T(8,128)(2,1)S(1)} %bitcast.138, bf16[2,15,128,256]{3,2,1,0:T(8,128)(2,1)S(1)} %copy-done.1), custom_call_target="tpu_custom_call" | custom-call | flops 16609443840 | bytes 10485760 | tf_op jit(solution)/shard_map/attend_forward/pallas_call | solution.py:158
  213.2 16.7 %collective-permute-done.1 = bf16[15,67,256]{2,0,1:T(8,128)(2,1)S(1)} collective-permute-done((bf16[15,67,256]{2,0,1:T(8,128)(2,1)S(1)}, bf16[15,67,256]{2,0,1:T(8,128)(2,1)S(1)}, u32[]{:S(2)}, u32[]{:S(2)}) %collective-permute-start.1) | collective-permute-done | bytes 514592 | tf_op jit(solution)/shard_map/ppermute | solution.py:328
  232.4 2.6 multiply_reduce_fusion.3
  235.3 5.6 fusion.64
  240.9 31.4 %all-gather.14.cloned.1.call-done = bf16[960,2560]{1,0:T(8,128)(2,1)} async-done(((bf16[240,2560]{1,0:T(8,128)(2,1)}), bf16[960,2560]{1,0:T(8,128)(2,1)}) %all-gather.14.cloned.1.call-update) | async-done | bytes 4915216 | tf_op jit(solution)/shard_map/all_gather | solution.py:263
  272.3 5.5 fusion.65
  277.8 50.7 %all-gather.16.cloned.1.call-done = bf16[2560,960]{0,1:T(8,128)(2,1)} async-done(((bf16[640,960]{0,1:T(8,128)(2,1)}), bf16[2560,960]{0,1:T(8,128)(2,1)}) %all-gather.16.cloned.1.call-update) | async-done | bytes 4915216 | tf_op jit(solution)/shard_map/all_gather | solution.py:263
  328.5 7.8 multiply_convert_fusion
  336.3 4.9 fusion.66
  341.3 2.2 multiply_reduce_fusion
  347.4 2.8 concatenate.71
  350.2 5.7 collective-permute-start.2
  358.1 10.7 %collective-permute-done.2 = bf16[15,70,256]{2,1,0:T(8,128)(2,1)S(1)} collective-permute-done((bf16[15,70,256]{2,1,0:T(8,128)(2,1)S(1)}, bf16[15,70,256]{2,1,0:T(8,128)(2,1)S(1)}, u32[]{:S(2)}, u32[]{:S(2)}) %collective-permute-start.2) | collective-permute-done | bytes 537632 | tf_op jit(solution)/shard_map/ppermute | solution.py:374
  369.5 2.6 fusion.57
  372.1 2.3 copy.97.do_flat
  382.8 76.4 %attend_backward.1 = (f32[2,15,64,256]{3,2,1,0:T(8,128)S(1)}, bf16[5,32,256,128]{3,2,1,0:T(8,128)(2,1)}) custom-call(s32[3]{0:T(128)S(1)} %pad_add_fusion.place, bf16[5,32,256,128]{3,2,1,0:T(8,128)(2,1)} %bitcast.137, bf16[2,15,128,256]{3,2,1,0:T(8,128)(2,1)S(1)} %copy-done.2, bf16[2,15,128,256]{3,2,1,0:T(8,128)(2,1)S(1)} %copy-done.3, ...), custom_call_target="tpu_custom_call" | custom-call | flops 41523609600 | bytes 20971520 | tf_op jit(solution)/shard_map/attend_backward/pallas_call | solution.py:189
  459.2 5.1 convolution_convert_fusion
  464.3 7.9 copy.106
  472.3 3.0 convolution_convert_fusion.4
  475.4 5.0 convolution_convert_fusion.2
  480.4 5.0 convolution_convert_fusion.1
  487.2 2.6 copy.98
  489.8 17.9 %collective-permute-done.3 = bf16[15,64,256]{2,1,0:T(8,128)(2,1)} collective-permute-done((bf16[15,64,256]{2,1,0:T(8,128)(2,1)S(1)}, bf16[15,64,256]{2,1,0:T(8,128)(2,1)}, u32[]{:S(2)}, u32[]{:S(2)}) %collective-permute-start.3) | collective-permute-done | bytes 491552 | tf_op jit(solution)/shard_map/ppermute | solution.py:392
  509.2 1.9 fusion.12
  512.7 79.3 %all-reduce.8.cloned.1.call-done = bf16[5,32,256,128]{3,2,1,0:T(8,128)(2,1)} async-done(((bf16[5,32,256,128]{3,2,1,0:T(8,128)(2,1)}), bf16[5,32,256,128]{3,2,1,0:T(8,128)(2,1)}) %all-reduce.8.cloned.1.call-update) | async-done | bytes 10485776
  594.1 2.8 convolution_convert_fusion.3
  596.9 53.0 %reduce-scatter.19.cloned.1.call-done = bf16[640,960]{1,0:T(8,128)(2,1)} async-done(((bf16[2560,960]{1,0:T(8,128)(2,1)}), bf16[640,960]{1,0:T(8,128)(2,1)}) %reduce-scatter.19.cloned.1.call-update) | async-done | bytes 1228816
  649.9 2.4 copy.107
  652.3 29.1 %reduce-scatter.13.cloned.1.call-done = bf16[240,960]{1,0:T(8,128)(2,1)} async-done(((bf16[960,960]{1,0:T(8,128)(2,1)}), bf16[240,960]{1,0:T(8,128)(2,1)}) %reduce-scatter.13.cloned.1.call-update) | async-done | bytes 460816 | tf_op jit(solution)/shard_map/reduce_scatter | solution.py:267
  681.4 54.9 %reduce-scatter.15.cloned.1.call-done = bf16[240,2560]{1,0:T(8,128)(2,1)} async-done(((bf16[960,2560]{1,0:T(8,128)(2,1)}), bf16[240,2560]{1,0:T(8,128)(2,1)}) %reduce-scatter.15.cloned.1.call-update) | async-done | bytes 1228816 | tf_op jit(solution)/shard_map/reduce_scatter | solution.py:267
  736.3 54.9 %reduce-scatter.17.cloned.1.call-done = bf16[240,2560]{1,0:T(8,128)(2,1)} async-done(((bf16[960,2560]{1,0:T(8,128)(2,1)}), bf16[240,2560]{1,0:T(8,128)(2,1)}) %reduce-scatter.17.cloned.1.call-update) | async-done | bytes 1228816 | tf_op jit(solution)/shard_map/reduce_scatter | solution.py:267
  791.2 40.9 %reduce-scatter.11.cloned.1.call-done = bf16[240,1600]{1,0:T(8,128)(2,1)} async-done(((bf16[960,1600]{1,0:T(8,128)(2,1)}), bf16[240,1600]{1,0:T(8,128)(2,1)}) %reduce-scatter.11.cloned.1.call-update) | async-done | bytes 768016 | tf_op jit(solution)/shard_map/reduce_scatter | solution.py:267
  833.3 5.2 fusion.18
  839.6 65.6 %psum.42 = bf16[2,960]{1,0:T(2,128)(2,1)S(1)} all-reduce(bf16[2,960]{1,0:T(2,128)(2,1)S(1)} %pad_maximum_fusion.9), channel_id=1, replica_groups=mesh['ctx'=32,'wt'=4] {'wt','ctx'}, use_global_device_ids=true, to_apply=%region_8.9 | all-reduce | flops 1920 | bytes 7680 | tf_op jit(solution)/shard_map/psum | solution.py:408
  907.1 43.7 %all-reduce.10.cloned.1.call-done = (bf16[240,1600]{1,0:T(8,128)(2,1)}, bf16[240,960]{1,0:T(8,128)(2,1)}, bf16[240,2560]{1,0:T(8,128)(2,1)}, bf16[240,2560]{1,0:T(8,128)(2,1)}, bf16[640,960]{0,1:T(8,128)(2,1)}) async-done(((bf16[240,1600]{1,0:T(8,128)(2,1)}, bf16[240,960]{1,0:T(8,128)(2,1)}, bf16[240,2560]{1,0:T(8,128)(2,1)}, bf16[240,2560]{1,0:T(8,128)(2,1)}, bf16[640,960]{0,1:T(8,128)(2,1)}), ...) | async-done | bytes 4915216 | tf_op jit(solution)/shard_map/psum | solution.py:268
  954.9 1.7 convert_element_type.290
  (188 shorter events, 57.4 us)
Async XLA Ops:
  7.2 5.9 copy-start.36
  7.2 7.8 copy-start.16
  7.2 49.1 %all-gather.8.cloned.1.call-start = ((), (), s32[]{:S(2)}) async-start(), calls=%async_computation.5 | async-start | bytes 3993600 | tf_op jit(solution)/shard_map/all_gather | solution.py:263
  13.0 116.8 %all-gather.18.cloned.1.call-start = ((), (), s32[]{:S(2)}) async-start(), calls=%async_computation.14 | async-start | bytes 10813440 | tf_op jit(solution)/shard_map/all_gather | solution.py:316
  15.1 45.9 %copy-start.33 = (f32[256]{0:T(256)}, f32[256]{0:T(256)S(1)}, u32[]{:S(2)}) copy-start(f32[256]{0:T(256)S(1)} %add_rsqrt_fusion.1) | copy-start | bytes 3076
  62.9 169.5 %all-gather.10.cloned.1.call-start = ((), (), s32[]{:S(2)}) async-start(), calls=%async_computation.6 | async-start | bytes 2457600 | tf_op jit(solution)/shard_map/all_gather | solution.py:263
  63.6 171.6 %all-gather.12.cloned.1.call-start = ((), (), s32[]{:S(2)}) async-start(), calls=%async_computation.7 | async-start | bytes 6144000 | tf_op jit(solution)/shard_map/all_gather | solution.py:263
  64.2 208.1 %all-gather.14.cloned.1.call-start = ((), (), s32[]{:S(2)}) async-start(), calls=%async_computation.8 | async-start | bytes 6144000 | tf_op jit(solution)/shard_map/all_gather | solution.py:263
  64.8 263.8 %all-gather.16.cloned.1.call-start = ((), (), s32[]{:S(2)}) async-start(), calls=%async_computation.9 | async-start | bytes 6144000 | tf_op jit(solution)/shard_map/all_gather | solution.py:263
  65.4 526.7 %all-reduce.8.cloned.1.call-start = ((), (), s32[]{:S(2)}) async-start(), calls=%async_computation.16 | async-start | bytes 20971520
  65.5 4.0 copy-start.23
  65.6 3.9 copy-start.25
  73.9 21.7 %collective-permute-start = (bf16[15,64,256]{2,1,0:T(8,128)(2,1)}, bf16[15,64,256]{2,1,0:T(8,128)(2,1)S(1)}, u32[]{:S(2)}, u32[]{:S(2)}) collective-permute-start(bf16[15,64,256]{2,1,0:T(8,128)(2,1)} %copy.88), channel_id=1, source_target_pairs={{0,124},{4,120},{8,116},{12,112},{16,108},{20,104},{24,100},{28,96... | collective-permute-start | bytes 1474568 | tf_op jit(solution)/shard_map/ppermute | solution.py:317
  80.9 15.9 %copy-start.12 = (bf16[1,15,64,256]{2,3,1,0:T(8,128)(2,1)S(1)}, bf16[1,15,64,256]{2,3,1,0:T(8,128)(2,1)}, u32[]{:S(2)}) copy-start(bf16[1,15,64,256]{2,3,1,0:T(8,128)(2,1)} %maximum_multiply_fusion) | copy-start | bytes 1474564
  129.8 1.5 copy-start.1
  131.3 4.0 copy-start.5
  212.3 17.6 %collective-permute-start.1 = (bf16[15,67,256]{2,0,1:T(8,128)(2,1)S(1)}, bf16[15,67,256]{2,0,1:T(8,128)(2,1)S(1)}, u32[]{:S(2)}, u32[]{:S(2)}) collective-permute-start(bf16[15,67,256]{2,0,1:T(8,128)(2,1)S(1)} %copy.91), channel_id=1, source_target_pairs={{0,124},{4,120},{8,116},{12,112},{16,108},{20,104},{24,100},{28,96... | collective-permute-start | bytes 1543688 | tf_op jit(solution)/shard_map/ppermute | solution.py:328
  229.9 1.4 copy-start.8
  235.0 106.2 %copy-start.10 = (f32[256,960]{0,1:T(8,128)}, f32[256,960]{0,1:T(8,128)S(1)}, u32[]{:S(2)}) copy-start(f32[256,960]{0,1:T(8,128)S(1)} %get-tuple-element.121) | copy-start | bytes 2949124
  336.3 4.9 copy-start.19
  336.3 4.9 copy-start.18
  336.3 4.9 copy-start.6
  341.2 2.2 copy-start.14
  343.5 1.8 copy-start.15
  345.3 1.5 copy-start.31
  350.2 18.5 %collective-permute-start.2 = (bf16[15,70,256]{2,1,0:T(8,128)(2,1)S(1)}, bf16[15,70,256]{2,1,0:T(8,128)(2,1)S(1)}, u32[]{:S(2)}, u32[]{:S(2)}) collective-permute-start(bf16[15,70,256]{2,1,0:T(8,128)(2,1)S(1)} %concatenate.71), channel_id=1, source_target_pairs={{0,124},{4,120},{8,116},{12,112},{16,108},{20,104},{24,100},{28,96... | collective-permute-start | bytes 1612808 | tf_op jit(solution)/shard_map/ppermute | solution.py:374
  376.6 1.5 copy-start
  378.1 1.5 copy-start.2
  379.7 1.5 copy-start.3
  381.2 1.5 copy-start.4
  459.2 190.8 %reduce-scatter.19.cloned.1.call-start = ((), (), s32[]{:S(2)}) async-start(), calls=%async_computation.15 | async-start | bytes 6553600
  472.2 209.2 %reduce-scatter.13.cloned.1.call-start = ((), (), s32[]{:S(2)}) async-start(), calls=%async_computation.11 | async-start | bytes 2457600 | tf_op jit(solution)/shard_map/reduce_scatter | solution.py:267
  475.3 260.9 %reduce-scatter.15.cloned.1.call-start = ((), (), s32[]{:S(2)}) async-start(), calls=%async_computation.12 | async-start | bytes 6144000 | tf_op jit(solution)/shard_map/reduce_scatter | solution.py:267
  480.4 310.8 %reduce-scatter.17.cloned.1.call-start = ((), (), s32[]{:S(2)}) async-start(), calls=%async_computation.13 | async-start | bytes 6144000 | tf_op jit(solution)/shard_map/reduce_scatter | solution.py:267
  485.4 346.6 %reduce-scatter.11.cloned.1.call-start = ((), (), s32[]{:S(2)}) async-start(), calls=%async_computation.10 | async-start | bytes 3993600 | tf_op jit(solution)/shard_map/reduce_scatter | solution.py:267
  485.6 22.1 %collective-permute-start.3 = (bf16[15,64,256]{2,1,0:T(8,128)(2,1)S(1)}, bf16[15,64,256]{2,1,0:T(8,128)(2,1)}, u32[]{:S(2)}, u32[]{:S(2)}) collective-permute-start(bf16[15,64,256]{2,1,0:T(8,128)(2,1)S(1)} %fusion.30), channel_id=1, source_target_pairs={{0,124},{4,120},{8,116},{12,112},{16,108},{20,104},{24,100},{28,96... | collective-permute-start | bytes 1474568 | tf_op jit(solution)/shard_map/ppermute | solution.py:392
  509.2 1.9 copy-start.24
  509.2 1.9 copy-start.26
  512.7 81.3 %copy-start.17 = (bf16[1,256,960]{1,2,0:T(8,128)(2,1)S(1)}, bf16[1,256,960]{1,2,0:T(8,128)(2,1)}, u32[]{:S(2)}) copy-start(bf16[1,256,960]{1,2,0:T(8,128)(2,1)} %param.12) | copy-start | bytes 1474564
  512.7 81.3 %copy-start.34 = (f32[256]{0:T(256)S(1)}, f32[256]{0:T(256)}, u32[]{:S(2)}) copy-start(f32[256]{0:T(256)} %copy-done.33) | copy-start | bytes 3076
  596.9 353.8 %all-reduce.10.cloned.1.call-start = ((), (), s32[]{:S(2)}) async-start(), calls=%async_computation.17 | async-start | bytes 9953280 | tf_op jit(solution)/shard_map/psum | solution.py:268
  832.1 1.2 copy-start.11
  833.3 5.2 copy-start.32
  950.7 1.3 copy-start.13
  950.7 2.4 copy-start.22
  953.1 1.7 copy-start.21
  954.9 1.7 copy-start.20
  956.6 3.4 copy-start.28
  (7 other events, 5.7 us)
Sparse Core Ops, SparseCore 0:
  13.1 43.1 all-gather.7
  63.0 66.7 all-gather.17
  131.5 28.7 all-gather.9
  161.7 54.3 all-gather.11
  217.6 54.6 all-gather.13
  273.9 54.6 all-gather.15
  459.3 132.7 all-reduce.7
  594.6 55.2 reduce-scatter.18
  653.1 28.3 reduce-scatter.12
  683.8 52.4 reduce-scatter.14
  738.7 52.4 reduce-scatter.16
  793.6 38.4 reduce-scatter.10
  836.8 113.9 all-reduce.9

commit v2 on v1

--- a/solution.py
+++ b/solution.py
@@ -18,7 +18,6 @@
 LOG2E = 1.4426950408889634
 F32 = jnp.float32
 BF16 = jnp.bfloat16
-HEAD_SETS = ((0, KEY_VALUE_HEADS),)
 
 
 def dot_f32(left, right, dims=((1,), (0,))):
@@ -217,6 +216,467 @@
     )(place, kv, q_turned, do_turned, q_flat, do_flat, stats)
 
 
+MESH = pl.DeviceIdType.MESH
+GAIN_ROWS = 16
+
+
+def torus(n):
+    side = {32: 4, 8: 2, 4: 1}[n]
+    return side, n // (2 * side)
+
+
+def coordinates(n):
+    sy, sz = torus(n)
+    ctx, x = lax.axis_index("ctx"), lax.axis_index("wt")
+    return {"x": x, "y": ctx // (2 * sz), "z": (ctx // 2) % sz, "core": ctx % 2}
+
+
+def device_at(n, here, **moved):
+    sy, sz = torus(n)
+    at = {**here, **moved}
+    return ((at["y"] * sz + at["z"]) * 2 + at["core"], at["x"])
+
+
+def remote(source, target, send, receive, device):
+    return pltpu.make_async_remote_copy(
+        src_ref=source, dst_ref=target, send_sem=send, recv_sem=receive, device_id=device, device_id_type=MESH
+    )
+
+
+def greet(devices):
+    barrier = pltpu.get_barrier_semaphore()
+    for device in devices:
+        pl.semaphore_signal(barrier, inc=1, device_id=device, device_id_type=MESH)
+    pl.semaphore_wait(barrier, len(devices))
+
+
+def peers_along(n, here, axis, size):
+    return [lax.rem(here[axis] + d, size) for d in range(1, size)]
+
+
+def reduce_kernel(n, sizes, cuts, first, gate, up, down, gains, out, acc, near, near_gains, *scratch):
+    steps, sems = scratch[:-7], scratch[-7:]
+    local_sem, near_send, near_recv, send_sem, recv_sem, spread_send, spread_recv = sems
+    here = coordinates(n)
+    sx, sy, sz = sizes["x"], sizes["y"], sizes["z"]
+    partner = device_at(n, here, core=1 - here["core"])
+    tall = first.shape[0] // sx
+    padded, wide = acc.shape[2], acc.shape[3]
+    deep = padded // sz
+    per_array = first.shape[1] // wide
+    block = down.shape[1] // sx
+    greet(
+        [partner]
+        + [device_at(n, here, **{a: i}) for a in "xyz" for i in peers_along(n, here, a, sizes[a])]
+    )
+
+    def pieces(core):
+        found = []
+        for x in range(sx):
+            for part in range(sy):
+                array, inner = divmod(part, per_array)
+                source = ((first, gate), (up, down))[core][array]
+                if source is down:
+                    for k in range(wide // block):
+                        row = (inner * (wide // block) + k) * tall
+                        found.append((source.at[pl.ds(row, tall), pl.ds(x * block, block)], x, part, k * block, block))
+                else:
+                    found.append((source.at[pl.ds(x * tall, tall), pl.ds(inner * wide, wide)], x, part, 0, wide))
+        return found
+
+    for core in range(2):
+        @pl.when(here["core"] == core)
+        def _():
+            for source, x, part, column, width in pieces(1 - core):
+                remote(
+                    source, near.at[x, part, :, pl.ds(column, width)], near_send.at[0], near_recv.at[0], partner
+                ).start()
+            for source, x, part, column, width in pieces(core):
+                pltpu.make_async_copy(
+                    source, acc.at[x, part, pl.ds(0, tall), pl.ds(column, width)], local_sem
+                ).start()
+
+    to_partner = remote(gains, near_gains, near_send.at[1], near_recv.at[1], partner)
+    to_partner.start()
+    pltpu.make_async_copy(near, acc.at[:, :, pl.ds(0, tall), :], local_sem).wait()
+    whole = remote(near, near, near_send.at[0], near_recv.at[0], partner)
+    whole.wait_recv()
+    to_partner.wait_recv()
+    acc[:, :, tall:, :] = jnp.zeros((sx, sy, padded - tall, wide), BF16)
+    both = gains[...].astype(F32) + near_gains[...].astype(F32)
+    acc[:, 0, tall : tall + GAIN_ROWS, : gains.shape[2]] = both.astype(BF16)
+
+    def join(i, carry):
+        x, part = i // sy, i % sy
+        acc[x, part, :tall] = (acc[x, part, :tall].astype(F32) + near[x, part].astype(F32)).astype(BF16)
+        return carry
+
+    lax.fori_loop(0, sx * sy, join, 0)
+
+    orders = ("xyz", "yzx", "zxy")
+
+    def region(third, done, axis, index):
+        column, width = cuts[third]
+        at = {a: here[a] for a in done}
+        if axis is not None:
+            at[axis] = index
+        pick = lambda a: at[a] if a in at else slice(None)
+        rows = pl.ds(pl.multiple_of(at["z"] * deep, deep), deep) if "z" in at else slice(None)
+        return acc.at[pick("x"), pick("y"), rows, pl.ds(column, width)]
+
+    def copies(third, step):
+        axis = orders[third][step]
+        size = sizes[axis]
+        buffer = steps[third * 3 + step]
+        return [
+            remote(
+                region(third, orders[third][:step], axis, peer),
+                buffer.at[d],
+                send_sem.at[third, step, d],
+                recv_sem.at[third, step, d],
+                device_at(n, here, **{axis: peer}),
+            )
+            for d, peer in enumerate(peers_along(n, here, axis, size))
+        ]
+
+    flights = []
+    current = [copies(third, 0) for third in range(3)]
+    for third in range(3):
+        for copy in current[third]:
+            copy.start()
+    for step in range(3):
+        for third in range(3):
+            for copy in current[third]:
+                copy.wait_recv()
+            flights += current[third]
+            buffer = steps[third * 3 + step]
+            mine = region(third, orders[third][: step + 1], None, None)
+            lead = mine.shape[:-2]
+            if current[third]:
+                def add(i, carry):
+                    at = []
+                    for extent in reversed(lead):
+                        at.append(i % extent)
+                        i = i // extent
+                    at = tuple(reversed(at))
+                    total = mine[at].astype(F32) if at else mine[...].astype(F32)
+                    for d in range(len(current[third])):
+                        total += buffer[(d, *at)].astype(F32)
+                    if at:
+                        mine[at] = total.astype(BF16)
+                    else:
+                        mine[...] = total.astype(BF16)
+                    return carry
+
+                count = 1
+                for extent in lead:
+                    count *= extent
+                if count == 1:
+                    add(0, 0)
+                else:
+                    lax.fori_loop(0, count, add, 0)
+            if step < 2:
+                current[third] = copies(third, step + 1)
+                for copy in current[third]:
+                    copy.start()
+
+    rows = pl.ds(pl.multiple_of(here["z"] * deep, deep), deep)
+    out[here["core"], here["y"], rows, :] = acc[here["x"], here["y"], rows, :]
+    half = wide // 2
+
+    def spread(step, part):
+        columns = pl.ds(part * half, half)
+        axis = "yz"[(step + part) % 2]
+        if step == 0:
+            piece = out.at[here["core"], here["y"], rows, columns]
+        elif axis == "z":
+            piece = out.at[here["core"], :, rows, columns]
+        else:
+            piece = out.at[here["core"], here["y"], :, columns]
+        return [
+            remote(
+                piece, piece, spread_send.at[step, part, d], spread_recv.at[step, part, d],
+                device_at(n, here, **{axis: peer}),
+            )
+            for d, peer in enumerate(peers_along(n, here, axis, sizes[axis]))
+        ]
+
+    for step in range(2):
+        moved = [spread(step, part) for part in range(2)]
+        for part in range(2):
+            for copy in moved[part]:
+                copy.start()
+        for part in range(2):
+            for copy in moved[part]:
+                copy.wait_recv()
+            flights += moved[part]
+    home = remote(
+        out.at[here["core"]], out.at[here["core"]], near_send.at[2], near_recv.at[2], partner
+    )
+    home.start()
+    home.wait_recv()
+    for copy in flights + [to_partner, home, whole]:
+        copy.wait_send()
+
+
+def sum_gradients(first, gate, up, down, gains):
+    n, sx = lax.axis_size("ctx"), lax.axis_size("wt")
+    sy, sz = torus(n)
+    sizes = {"x": sx, "y": sy, "z": sz}
+    tall = first.shape[0] // sx
+    padded = -(-(tall + GAIN_ROWS) // (16 * sz)) * 16 * sz
+    wide = 2 * first.shape[1] // sy
+    unit = wide // 128
+    widths = [unit * 128 // 3 // 128 * 128] * 2
+    widths.append(wide - sum(widths))
+    cuts = [(sum(widths[:i]), widths[i]) for i in range(3)]
+    orders = ("xyz", "yzx", "zxy")
+    extents = {"x": sx, "y": sy}
+    buffers = []
+    for third in range(3):
+        for step in range(3):
+            done = orders[third][: step + 1]
+            shape = [extents[a] for a in "xy" if a not in done]
+            shape.append(padded // sz if "z" in done else padded)
+            peers = max(sizes[orders[third][step]] - 1, 1)
+            buffers.append(pltpu.VMEM((peers, *shape, cuts[third][1]), BF16))
+    peers = max(sx, sy, sz)
+    anywhere = pl.BlockSpec(memory_space=pl.ANY)
+    inside = pl.BlockSpec(memory_space=pltpu.VMEM)
+    dma = pltpu.SemaphoreType.DMA
+    return pl.pallas_call(
+        functools.partial(reduce_kernel, n, sizes, cuts),
+        out_shape=jax.ShapeDtypeStruct((2, sy, padded, wide), BF16),
+        in_specs=[anywhere] * 4 + [inside],
+        out_specs=inside,
+        scratch_shapes=[
+            pltpu.VMEM((sx, sy, padded, wide), BF16),
+            pltpu.VMEM((sx, sy, tall, wide), BF16),
+            pltpu.VMEM(gains.shape, BF16),
+            *buffers,
+            dma,
+            dma((3,)),
+            dma((3,)),
+            dma((3, 3, peers)),
+            dma((3, 3, peers)),
+            dma((2, 2, peers)),
+            dma((2, 2, peers)),
+        ],
+        compiler_params=pltpu.CompilerParams(
+            collective_id=1, has_side_effects=True, vmem_limit_bytes=56 * 2**20
+        ),
+        name="sum_gradients",
+    )(first, gate, up, down, gains)
+
+
+def mirror_of(n, here):
+    sy, sz = torus(n)
+    return device_at(n, here, y=sy - 1 - here["y"], z=sz - 1 - here["z"], core=1 - here["core"])
+
+
+def plane_peers(n, here, sizes):
+    return [device_at(n, here, **{a: i}) for a in "yz" for i in peers_along(n, here, a, sizes[a])]
+
+
+def gather_kernel(n, own, query, blocks, mirrored, local_sem, step_send, step_recv, near_send, near_recv, far_sem):
+    here = coordinates(n)
+    sy, sz = torus(n)
+    sizes = {"y": sy, "z": sz}
+    y, z, core = here["y"], here["z"], here["core"]
+    partner, mirror = device_at(n, here, core=1 - core), mirror_of(n, here)
+    greet([partner, mirror] + plane_peers(n, here, sizes))
+    half = own.shape[1] // 2
+    part_rows = [pl.ds(part * half, half) for part in range(2)]
+
+    def along(step, part):
+        axis = "yz"[(step + part) % 2]
+        rows = part_rows[part]
+        copies = []
+        for d, peer in enumerate(peers_along(n, here, axis, sizes[axis])):
+            if step == 0:
+                source, target = own.at[:, rows], blocks.at[:, y, z, core, rows]
+            else:
+                source = blocks.at[:, :, z, core, rows] if axis == "z" else blocks.at[:, y, :, core, rows]
+                target = source
+            copies.append(
+                remote(
+                    source, target, step_send.at[step, part, d], step_recv.at[step, part, d],
+                    device_at(n, here, **{axis: peer}),
+                )
+            )
+        return copies
+
+    first = [along(0, 0), along(0, 1)]
+    for copy in first[0] + first[1]:
+        copy.start()
+    to_mirror = remote(query, mirrored, far_sem.at[0], far_sem.at[1], mirror)
+    keep = pltpu.make_async_copy(own, blocks.at[:, y, z, core], local_sem)
+    keep.start()
+    keep.wait()
+    for copy in first[0] + first[1]:
+        copy.wait_recv()
+    second = [along(1, 0), along(1, 1)]
+    for copy in second[0] + second[1]:
+        copy.start()
+
+    def give(slot, region):
+        copy = remote(region, region, near_send.at[slot], near_recv.at[slot], partner)
+        copy.start()
+        return copy
+
+    passed = [
+        give(0, blocks.at[:, :, z, core, part_rows[0]]),
+        give(1, blocks.at[:, y, :, core, part_rows[1]]),
+    ]
+    to_mirror.start()
+    for d in range(max(sy, sz) - 1):
+        if d < len(second[0]):
+            second[0][d].wait_recv()
+            passed.append(give(2 + 2 * d, blocks.at[:, :, lax.rem(z + sz - 1 - d, sz), core, part_rows[0]]))
+        if d < len(second[1]):
+            second[1][d].wait_recv()
+            passed.append(give(3 + 2 * d, blocks.at[:, lax.rem(y + sy - 1 - d, sy), :, core, part_rows[1]]))
+    for copy in passed:
+        copy.wait_recv()
+    to_mirror.wait_recv()
+    for copy in first[0] + first[1] + second[0] + second[1] + passed + [to_mirror]:
+        copy.wait_send()
+
+
+def gather_blocks(own, query):
+    n = lax.axis_size("ctx")
+    sy, sz = torus(n)
+    peers = max(sy, sz, 2) - 1
+    heads, rows, pair = own.shape
+    dma = pltpu.SemaphoreType.DMA
+    anywhere = pl.BlockSpec(memory_space=pl.ANY)
+    blocks, mirrored = pl.pallas_call(
+        functools.partial(gather_kernel, n),
+        out_shape=(
+            jax.ShapeDtypeStruct((heads, sy, sz, 2, rows, pair), BF16),
+            jax.ShapeDtypeStruct(query.shape, BF16),
+        ),
+        in_specs=[anywhere, anywhere],
+        out_specs=(anywhere, anywhere),
+        scratch_shapes=[
+            dma, dma((2, 2, peers)), dma((2, 2, peers)), dma((2 + 2 * peers,)), dma((2 + 2 * peers,)), dma((2,)),
+        ],
+        compiler_params=pltpu.CompilerParams(collective_id=2, has_side_effects=True),
+        name="gather_blocks",
+    )(own, query)
+    return blocks.reshape(heads, n, rows, pair), mirrored
+
+
+def home_kernel(n, blocks, query, out, mirrored, acc, near, far, local_sem, near_sem, step_send, step_recv, far_sem, *steps):
+    here = coordinates(n)
+    sy, sz = torus(n)
+    sizes = {"y": sy, "z": sz}
+    y, z, core = here["y"], here["z"], here["core"]
+    partner, mirror = device_at(n, here, core=1 - core), mirror_of(n, here)
+    greet([partner, mirror] + plane_peers(n, here, sizes))
+    heads, half = acc.shape[0], acc.shape[3] // 2
+    swap = remote(blocks.at[:, :, :, 1 - core], near, near_sem.at[0], near_sem.at[1], partner)
+    swap.start()
+    keep = pltpu.make_async_copy(blocks.at[:, :, :, core], acc, local_sem)
+    keep.start()
+    to_mirror = remote(query, far, far_sem.at[0], far_sem.at[1], mirror)
+    keep.wait()
+    swap.wait_recv()
+    to_mirror.start()
+
+    def join(i, carry):
+        head, a, b = i // (sy * sz), (i // sz) % sy, i % sz
+        acc[head, a, b] = (acc[head, a, b].astype(F32) + near[head, a, b].astype(F32)).astype(BF16)
+        return carry
+
+    lax.fori_loop(0, heads * sy * sz, join, 0)
+
+    def region(part, done, axis, index):
+        at = {a: here[a] for a in done}
+        if axis is not None:
+            at[axis] = index
+        pick = lambda a: at[a] if a in at else slice(None)
+        return acc.at[:, pick("y"), pick("z"), pl.ds(part * half, half)]
+
+    orders = ("yz", "zy")
+    flights = []
+    for step in range(2):
+        moved = []
+        for part in range(2):
+            axis = orders[part][step]
+            moved.append(
+                [
+                    remote(
+                        region(part, orders[part][:step], axis, peer),
+                        steps[part * 2 + step].at[d],
+                        step_send.at[step, part, d],
+                        step_recv.at[step, part, d],
+                        device_at(n, here, **{axis: peer}),
+                    )
+                    for d, peer in enumerate(peers_along(n, here, axis, sizes[axis]))
+                ]
+            )
+            for copy in moved[part]:
+                copy.start()
+        for part in range(2):
+            buffer = steps[part * 2 + step]
+            for copy in moved[part]:
+                copy.wait_recv()
+            flights += moved[part]
+            mine = region(part, orders[part][: step + 1], None, None)
+            inner = mine.shape[1] if step == 0 else 1
+            if moved[part]:
+                def add(i, carry):
+                    at = (i // inner, i % inner) if step == 0 else (i,)
+                    total = mine[at].astype(F32)
+                    for d in range(len(moved[part])):
+                        total += buffer[(d, *at)].astype(F32)
+                    mine[at] = total.astype(BF16)
+                    return carry
+
+                lax.fori_loop(0, heads * inner, add, 0)
+    out[...] = acc[:, y, z]
+    to_mirror.wait_recv()
+    mirrored[...] = far[...]
+    for copy in flights + [swap, to_mirror]:
+        copy.wait_send()
+
+
+def bring_home(blocks, query):
+    n = lax.axis_size("ctx")
+    sy, sz = torus(n)
+    heads, _, rows, pair = blocks.shape
+    dma = pltpu.SemaphoreType.DMA
+    peers = max(sy, sz, 2) - 1
+    extents = {"y": sy, "z": sz}
+    buffers = []
+    for order in ("yz", "zy"):
+        buffers.append(pltpu.VMEM((max(extents[order[0]] - 1, 1), heads, extents[order[1]], rows // 2, pair), BF16))
+        buffers.append(pltpu.VMEM((max(extents[order[1]] - 1, 1), heads, rows // 2, pair), BF16))
+    anywhere = pl.BlockSpec(memory_space=pl.ANY)
+    inside = pl.BlockSpec(memory_space=pltpu.VMEM)
+    return pl.pallas_call(
+        functools.partial(home_kernel, n),
+        out_shape=(
+            jax.ShapeDtypeStruct((heads, rows, pair), BF16),
+            jax.ShapeDtypeStruct(query.shape, BF16),
+        ),
+        in_specs=[anywhere, anywhere],
+        out_specs=(inside, inside),
+        scratch_shapes=[
+            pltpu.VMEM((heads, sy, sz, rows, pair), BF16),
+            pltpu.VMEM((heads, sy, sz, rows, pair), BF16),
+            pltpu.VMEM(query.shape, BF16),
+            dma, dma((2,)), dma((2, 2, peers)), dma((2, 2, peers)), dma((2,)),
+            *buffers,
+        ],
+        compiler_params=pltpu.CompilerParams(
+            collective_id=3, has_side_effects=True, vmem_limit_bytes=40 * 2**20
+        ),
+        name="bring_home",
+    )(blocks.reshape(heads, sy, sz, 2, rows, pair), query)
+
+
 def rms_forward(values, gain):
     inverse = lax.rsqrt(jnp.mean(values * values, axis=-1, keepdims=True) + EPSILON)
     normal = values * inverse
@@ -263,9 +723,10 @@
     return lax.all_gather(shard, "wt", axis=0, tiled=True)
 
 
-def reduce_gradient(gradient):
-    part = lax.psum_scatter(gradient.astype(BF16), "wt", scatter_dimension=0, tiled=True)
-    return lax.psum(part, "ctx").astype(F32)
+def gather_weight_halves(half):
+    n = lax.axis_size("ctx")
+    along = lax.all_gather(half, "wt", axis=0)
+    return lax.all_gather(along, "ctx", axis=0, axis_index_groups=[[i, i + 1] for i in range(0, n, 2)])
 
 
 def per_device(
@@ -313,35 +774,31 @@
     q = q * BF16(HEAD_SIZE**-0.5)
     own_kv = jnp.concatenate([k, v], axis=1).transpose(0, 2, 1)
 
-    kv_sets = [lax.all_gather(own_kv[j : j + c], "ctx", axis=1) for j, c in HEAD_SETS]
-    q_both = jnp.stack([q, lax.ppermute(q, "ctx", across)])
+    kv, mirrored = gather_blocks(own_kv, q)
+    q_both = jnp.stack([q, mirrored])
     blank = jnp.zeros_like(q_both)
     q_turned = jnp.concatenate([q_both, blank], axis=2)
     q_flat = q_turned.transpose(0, 1, 3, 2)
 
     later = token >= edges[1]
-    own_o, own_stat = [], []
-    for (j, c), kv in zip(HEAD_SETS, kv_sets):
-        some = slice(j * GROUP, (j + c) * GROUP)
-        o_part, stat_part = attention_forward(n, place, kv, q_turned[:, some])
-        sent = jnp.concatenate([o_part[1].astype(BF16)] + three_parts(stat_part[1]) , axis=1)
-        got = lax.ppermute(sent, "ctx", across)
-        other_stat = joined([got[:, HEAD_SIZE + i : HEAD_SIZE + i + 1] for i in range(3)])
-        other_stat = jnp.where(later, NEG, other_stat)
-        stat = jnp.logaddexp(stat_part[0], other_stat)
-        own_o.append(
-            o_part[0] * jnp.exp(stat_part[0] - stat)
-            + got[:, :HEAD_SIZE].astype(F32) * jnp.exp(other_stat - stat)
-        )
-        own_stat.append(stat)
-    attended = jnp.concatenate(own_o)
-    log_total = jnp.concatenate(own_stat)
+    o_part, stat_part = attention_forward(n, place, kv, q_turned)
+    sent = jnp.concatenate([o_part[1].astype(BF16)] + three_parts(stat_part[1]), axis=1)
+    got = lax.ppermute(sent, "ctx", across)
+    other_stat = joined([got[:, HEAD_SIZE + i : HEAD_SIZE + i + 1] for i in range(3)])
+    other_stat = jnp.where(later, NEG, other_stat)
+    log_total = jnp.logaddexp(stat_part[0], other_stat)
+    attended = o_part[0] * jnp.exp(stat_part[0] - log_total) + got[:, :HEAD_SIZE].astype(F32) * jnp.exp(
+        other_stat - log_total
+    )
     mixed = attended.reshape(queries, rows).astype(BF16)
 
     full_out = gather_weight(w_out)
-    full_gate = gather_weight(w_gate)
-    full_up = gather_weight(w_up)
-    full_down = gather_weight(w_down)
+    core = me % 2
+    both = gather_weight_halves(jnp.where(core == 0, w_gate, w_up)).reshape(2, width, -1)
+    full_gate, full_up = both[0], both[1]
+    down_rows = w_down.shape[0] // 2
+    both = gather_weight_halves(lax.dynamic_slice_in_dim(w_down, core * down_rows, down_rows))
+    full_down = both.transpose(1, 0, 2, 3).reshape(-1, width)
     resid = x + dot_f32(mixed, full_out, ((0,), (0,)))
     normed_two, normal_mlp, inverse_mlp = rms_forward(resid, mlp_scale)
     normed_two = normed_two.astype(BF16)
@@ -352,7 +809,7 @@
     hidden = (activated * up).astype(BF16)
     layer_output = (resid + dot_f32(hidden, full_down)).astype(BF16)[None]
     upstream = cotangent[0]
-    grad_w_down = dot_f32(hidden, upstream, ((0,), (0,)))
+    grad_w_down = dot_f32(upstream, hidden, ((0,), (0,)))
     grad_hidden = dot_f32(upstream, full_down, ((1,), (1,)))
     grad_up_in = (grad_hidden * activated).astype(BF16)
     grad_gate_in = (grad_hidden * up * sig * (1.0 + gate * (1.0 - sig))).astype(BF16)
@@ -383,17 +840,10 @@
     do_both = jnp.stack([grad_attended, got[:, :HEAD_SIZE]])
     do_turned = jnp.concatenate([blank, do_both], axis=2)
     do_flat = do_turned.transpose(0, 1, 3, 2)
-    dq_all, dkv_all = [], []
-    for (j, c), kv in zip(HEAD_SETS, kv_sets):
-        some = slice(j * GROUP, (j + c) * GROUP)
-        dq, dkv = attention_backward(
-            n, place, kv, q_turned[:, some], do_turned[:, some], q_flat[:, some], do_flat[:, some], stats[:, some]
-        )
-        other = lax.ppermute(dq[1].astype(BF16), "ctx", across)
-        dq_all.append(dq[0] + other.astype(F32))
-        dkv_all.append(lax.psum_scatter(dkv, "ctx", scatter_dimension=1, tiled=False))
-    grad_q = turn_back(jnp.concatenate(dq_all) * HEAD_SIZE**-0.5, cosine, sine).astype(BF16)
-    dkv = jnp.concatenate(dkv_all).astype(F32).transpose(0, 2, 1)
+    dq, dkv = attention_backward(n, place, kv, q_turned, do_turned, q_flat, do_flat, stats)
+    dkv, dq_more = bring_home(dkv, dq[1].astype(BF16))
+    grad_q = turn_back((dq[0] + dq_more.astype(F32)) * HEAD_SIZE**-0.5, cosine, sine).astype(BF16)
+    dkv = dkv.astype(F32).transpose(0, 2, 1)
     grad_k = turn_back(dkv[:, :HEAD_SIZE], cosine, sine).astype(BF16)
     grad_v = dkv[:, HEAD_SIZE:].astype(BF16)
     grad_qkv = jnp.concatenate(
@@ -404,22 +854,33 @@
     grad_in, grad_attn_gain = rms_backward(grad_normed, attn_scale, normal_in, inverse_in)
     input_grad = (grad_resid + grad_in)[None]
 
-    sum_qkv = reduce_gradient(grad_w_qkv)
-    gain_sum = lax.psum(jnp.stack([grad_attn_gain, grad_mlp_gain]).astype(BF16), ("wt", "ctx"))
-    mine = lax.dynamic_slice_in_dim(gain_sum, lax.axis_index("wt") * attn_gain.shape[0], attn_gain.shape[0], 1)
-    mine = mine.astype(F32)
+    sx = lax.axis_size("wt")
+    tall = width // sx
+    gains = jnp.stack([grad_attn_gain, grad_mlp_gain]).reshape(2, sx, tall).transpose(1, 0, 2)
+    gains = jnp.pad(gains, ((0, 0), (0, GAIN_ROWS - 2), (0, -tall % 128))).astype(BF16)
+    first = jnp.concatenate([grad_w_qkv.astype(BF16), grad_w_out.astype(BF16)], axis=1)
+    sums = sum_gradients(
+        first, grad_w_gate.astype(BF16), grad_w_up.astype(BF16), grad_w_down.astype(BF16), gains
+    )
+    parts = sums.reshape(-1, *sums.shape[2:])
+    parts = jnp.concatenate([parts[i] for i in range(parts.shape[0])], axis=1)
+    gain_sums = parts[tall : tall + 2, :tall].astype(F32)
+    parts = parts[:tall].astype(F32)
+    ff = w_gate.shape[1]
+    block = ff // sx
+    sum_down = jnp.concatenate([parts[:, 3 * ff + i * block : 3 * ff + (i + 1) * block] for i in range(sx)]).T
     return (
         layer_output,
         input_grad,
-        mine[0],
-        sum_qkv[:, :queries],
-        sum_qkv[:, queries : queries + keys],
-        sum_qkv[:, queries + keys :],
-        reduce_gradient(grad_w_out),
-        mine[1],
-        reduce_gradient(grad_w_gate),
-        reduce_gradient(grad_w_up),
-        reduce_gradient(grad_w_down),
+        gain_sums[0],
+        parts[:, :queries],
+        parts[:, queries : queries + keys],
+        parts[:, queries + keys : queries + 2 * keys],
+        parts[:, queries + 2 * keys : ff],
+        gain_sums[1],
+        parts[:, ff : 2 * ff],
+        parts[:, 2 * ff : 3 * ff],
+        sum_down,
     )
 
 

time: 978 us -> 713 us (0.73)
  waiting for transfers between devices: 569 us -> 151 us
  Pallas kernels: 153 us -> 401 us
  blocking collectives: 65.6 us -> 0 us
  matrix products: 59.6 us -> 41.4 us
  starting transfers between devices: 12.9 us -> 1.68 us
    pallas_call x0 -> x3, Pallas kernels: none -> 248 us  [the longest x1 120 us: sum_gradients(): pl.pallas_call(functools.partial(reduce_kernel, n, sizes, cuts), out_shap...]
    reduce_scatter x4 -> x0, waiting for transfers between devices: 180 us -> none  [reduce_gradient(): lax.psum_scatter(gradient.astype(BF16), 'wt', scatter_dimension=0, tiled=...]
    unnamed x15 -> x6, waiting for transfers between devices: 135 us -> 0.6 us
    all_gather x5 -> x2, waiting for transfers between devices: 123 us -> 40.1 us  [gather_weight(): return lax.all_gather(shard, 'wt', axis=0, tiled=True)]
    psum x1 -> x0, blocking collectives: 65.6 us -> none  [per_device(): lax.psum(jnp.stack([grad_attn_gain, grad_mlp_gain]).astype(BF16), ('wt',...]
    all_gather x1 -> x4, waiting for transfers between devices: 27.6 us -> 91.4 us  [the longest x2 91.3 us: gather_weight_halves(): along = lax.all_gather(half, 'wt', axis=0)]
    psum x1 -> x0, waiting for transfers between devices: 43.7 us -> none  [reduce_gradient(): return lax.psum(part, 'ctx').astype(F32)]
    ppermute x2 -> x0, waiting for transfers between devices: 32.5 us -> none  [the longest x1 17.9 us: per_device(): other = lax.ppermute(dq[1].astype(BF16), 'ctx', across)]
  transfers between devices with their start and end apart: 17 -> 8, of which waited for: 15 -> 5; matrix products, arithmetic and copies ran while one was open for 9% -> 6% of each run, Pallas kernels for 8% -> 19%
where the time goes in v2:
time: 713 us; the launch traced here: 706 us
  Pallas kernels  401 us (56%)
  waiting for transfers between devices  151 us (21%)
  local copies, waits for them, and re-layouts  65.8 us (9%)
  matrix products  41.4 us (6%)
  other arithmetic  29.1 us (4%)
  between operations  15.6 us (2%)
    pallas_call x1, Pallas kernels, sum_gradients(): pl.pallas_call(functools.partial(reduce_kernel, n, sizes, cuts), out_shap...  120 us
    all_gather x2, waiting for transfers between devices, gather_weight_halves(): along = lax.all_gather(half, 'wt', axis=0)  91.3 us
    pallas_call x1, Pallas kernels, attention_forward(): pl.pallas_call(functools.partial(forward_kernel, n), grid=(heads,), out_s...  76.6 us
    pallas_call x1, Pallas kernels, attention_backward(): pl.pallas_call(functools.partial(backward_kernel, n), grid=(heads,), out_...  76.4 us
    pallas_call x1, Pallas kernels, bring_home(): pl.pallas_call(functools.partial(home_kernel, n), out_shape=(jax.ShapeDty...  70.2 us
    pallas_call x1, Pallas kernels, gather_blocks(): pl.pallas_call(functools.partial(gather_kernel, n), out_shape=(jax.ShapeD...  57.3 us
    dot_general x15, matrix products, dot_f32(): lax.dot_general(left, right, (dims, ((), ())), preferred_element_type=F32)  41.4 us
    all_gather x2, waiting for transfers between devices, gather_weight(): return lax.all_gather(shard, 'wt', axis=0, tiled=True)  40.1 us
  transfers between devices with their start and end apart: 8, of which 5 were waited for; matrix products, arithmetic and copies ran while one was open for 6% of the time, Pallas kernels for 19%

profile of v2, /device:TPU:1, one launch (start us, length us, event | category | flops | bytes accessed | tf_op | source)
XLA Modules:
  0.0 705.8 jit_solution(6076814077412349074)
XLA Ops:
  13.9 34.8 %all-gather.19.cloned.1.call-done = bf16[1280,960]{1,0:T(8,128)(2,1)} async-done(((bf16[320,960]{1,0:T(8,128)(2,1)}), bf16[1280,960]{1,0:T(8,128)(2,1)}) %all-gather.19.cloned.1.call-update) | async-done | bytes 2457616 | tf_op jit(solution)/shard_map/all_gather | solution.py:728
  48.8 56.5 %all-gather.15.cloned.1.call-done = bf16[960,2560]{1,0:T(8,128)(2,1)} async-done(((bf16[240,2560]{1,0:T(8,128)(2,1)}), bf16[960,2560]{1,0:T(8,128)(2,1)}) %all-gather.15.cloned.1.call-update) | async-done | bytes 4915216 | tf_op jit(solution)/shard_map/all_gather | solution.py:728
  105.9 1.3 fusion.59
  107.9 40.1 %all-gather.11.cloned.1.call-done = bf16[960,1664]{1,0:T(8,128)(2,1)} async-done(((bf16[240,1664]{1,0:T(8,128)(2,1)}), bf16[960,1664]{1,0:T(8,128)(2,1)}) %all-gather.11.cloned.1.call-update) | async-done | bytes 3194896 | tf_op jit(solution)/shard_map/all_gather | solution.py:723
  149.5 3.2 fusion.7
  155.8 57.3 %gather_blocks.1 = (bf16[5,4,4,2,256,128]{5,4,3,2,1,0:T(8,128)(2,1)}, bf16[15,64,256]{2,1,0:T(8,128)(2,1)}) custom-call(bf16[5,256,128]{2,1,0:T(8,128)(2,1)} %maximum_bitcast_fusion.1.own, bf16[15,64,256]{2,1,0:T(8,128)(2,1)} %maximum_multiply_fusion.query), custom_call_target="tpu_custom_call" | custom-call | tf_op jit(solution)/shard_map/gather_blocks/pallas_call | solution.py:553
  213.3 2.9 fusion.64
  216.1 6.1 copy-done.8
  222.3 76.6 %attend_forward.1 = (f32[2,15,64,256]{3,2,1,0:T(8,128)S(1)}, f32[2,15,1,256]{3,2,1,0:T(1,128)S(1)}) custom-call(s32[3]{0:T(128)S(1)} %pad_add_fusion.place, bf16[5,32,256,128]{3,2,1,0:T(8,128)(2,1)S(1)} %bitcast.178, bf16[2,15,128,256]{3,2,1,0:T(8,128)(2,1)S(1)} %get-tuple-element.94.q_ref), custom_call_target="tpu_custom_call" | custom-call | flops 16609443840 | bytes 10485760 | tf_op jit(solution)/shard_map/attend_forward/pallas_call | solution.py:157
  300.8 4.0 copy.67.q_flat
  304.8 12.1 %collective-permute-done = bf16[15,67,256]{2,0,1:T(8,128)(2,1)} collective-permute-done((bf16[15,67,256]{2,0,1:T(8,128)(2,1)}, bf16[15,67,256]{2,0,1:T(8,128)(2,1)}, u32[]{:S(2)}, u32[]{:S(2)}) %collective-permute-start) | collective-permute-done | bytes 514592 | tf_op jit(solution)/shard_map/ppermute | solution.py:786
  320.2 2.6 multiply_reduce_fusion.3
  324.0 5.4 copy.65
  329.4 8.2 %fusion.69 = (bf16[4,240,2560]{2,1,0:T(8,128)(2,1)}, bf16[4,240,2560]{2,1,0:T(8,128)(2,1)}) fusion(bf16[8,240,2560]{2,1,0:T(8,128)(2,1)} %all-gather.17.cloned.1.call-done), kind=kLoop, calls=%fused_computation.178 | loop fusion | bytes 19660800 | tf_op jit(solution)/shard_map/slice | solution.py:798
  337.6 4.1 fusion.75
  341.8 1.5 fusion.74
  343.4 3.9 multiply_convert_fusion
  347.3 1.5 fusion.76
  348.8 1.6 multiply_reduce_fusion
  350.7 1.2 copy-done.20
  353.3 2.0 convolution_convert_fusion.4
  355.3 3.7 convolution_convert_fusion.1.up
  359.0 3.7 convolution_convert_fusion.2.gate
  362.8 2.3 concatenate.82
  365.1 1.3 collective-permute-start.1
  366.4 5.1 fusion.down
  371.5 3.0 fusion.17
  374.5 7.3 %collective-permute-done.1 = bf16[15,70,256]{2,1,0:T(8,128)(2,1)S(1)} collective-permute-done((bf16[15,70,256]{2,1,0:T(8,128)(2,1)}, bf16[15,70,256]{2,1,0:T(8,128)(2,1)S(1)}, u32[]{:S(2)}, u32[]{:S(2)}) %collective-permute-start.1) | collective-permute-done | bytes 537632 | tf_op jit(solution)/shard_map/ppermute | solution.py:831
  381.9 2.4 fusion.63
  384.3 4.3 copy.68.do_flat
  388.7 1.4 fusion.51
  390.1 1.5 copy-done.5
  391.7 1.5 copy-done.6
  393.2 1.5 copy-done.7
  394.8 76.4 %attend_backward.1 = (f32[2,15,64,256]{3,2,1,0:T(8,128)S(1)}, bf16[5,32,256,128]{3,2,1,0:T(8,128)(2,1)}) custom-call(s32[3]{0:T(128)S(1)} %pad_add_fusion.place, bf16[5,32,256,128]{3,2,1,0:T(8,128)(2,1)} %bitcast.177, bf16[2,15,128,256]{3,2,1,0:T(8,128)(2,1)S(1)} %copy-done.4, bf16[2,15,128,256]{3,2,1,0:T(8,128)(2,1)S(1)} %copy-done.6, ...), custom_call_target="tpu_custom_call" | custom-call | flops 41523609600 | bytes 20971520 | tf_op jit(solution)/shard_map/attend_backward/pallas_call | solution.py:188
  471.2 4.0 copy-done.2
  475.2 70.2 %bring_home.1 = (bf16[5,256,128]{2,1,0:T(8,128)(2,1)S(1)}, bf16[15,64,256]{2,1,0:T(8,128)(2,1)S(1)}) custom-call(bf16[5,4,4,2,256,128]{5,4,3,2,1,0:T(8,128)(2,1)S(1)} %bitcast.175, bf16[15,64,256]{2,1,0:T(8,128)(2,1)S(1)} %fusion.37.query), custom_call_target="tpu_custom_call" | custom-call | tf_op jit(solution)/shard_map/bring_home/pallas_call | solution.py:658
  546.9 2.8 convolution_convert_fusion.3
  549.7 2.0 fusion.24
  552.5 5.5 pad_maximum_fusion.first
  558.0 120.4 %sum_gradients.1 = bf16[2,4,256,1280]{3,2,1,0:T(8,128)(2,1)} custom-call(bf16[960,2560]{1,0:T(8,128)(2,1)} %pad_maximum_fusion.first, bf16[960,2560]{1,0:T(8,128)(2,1)} %convolution_convert_fusion.2.gate, bf16[960,2560]{1,0:T(8,128)(2,1)} %convolution_convert_fusion.1.up, bf16[960,2560]{1,0:T(8,128)(2,1)} %fusion.down, bf16[4,16,256]{2,1,0:T(8,128)(2,1)} %pad.12.gains), custom_call_target="tpu_custom_call" | custom-call | tf_op jit(solution)/shard_map/sum_gradients/pallas_call | solution.py:447
  678.4 1.3 slice_bitcast_fusion.7
  679.7 1.5 constant_dynamic-update-slice_fusion
  685.2 1.6 fusion.67
  686.8 1.2 fusion.65
  688.0 2.6 fusion.66
  693.0 2.6 fusion.23
  695.6 2.9 maximum_bitcast_fusion
  (189 shorter events, 29.3 us)
Async XLA Ops:
  7.2 2.8 copy-start.27
  7.2 41.5 %all-gather.19.cloned.1.call-start = ((), (), s32[]{:S(2)}) async-start(), calls=%async_computation.4 | async-start | bytes 3276800 | tf_op jit(solution)/shard_map/all_gather | solution.py:728
  8.8 1.5 copy-start.28
  9.9 1.6 copy-start.35
  10.0 1.6 copy-start.36
  10.0 1.8 copy-start.31
  10.0 95.3 %all-gather.15.cloned.1.call-start = ((), (), s32[]{:S(2)}) async-start(), calls=%async_computation.2 | async-start | bytes 6144000 | tf_op jit(solution)/shard_map/all_gather | solution.py:728
  10.3 1.6 copy-start.32
  10.3 1.8 copy-start.30
  11.4 136.5 %all-gather.11.cloned.1.call-start = ((), (), s32[]{:S(2)}) async-start(), calls=%async_computation | async-start | bytes 3993600 | tf_op jit(solution)/shard_map/all_gather | solution.py:723
  13.3 306.9 %all-gather.13.cloned.1.call-start = ((), (), s32[]{:S(2)}) async-start(), calls=%async_computation.1 | async-start | bytes 2457600 | tf_op jit(solution)/shard_map/all_gather | solution.py:723
  13.8 310.1 %all-gather.21.cloned.1.call-start = ((), (), s32[]{:S(2)}) async-start(), calls=%async_computation.5 | async-start | bytes 7864320 | tf_op jit(solution)/shard_map/all_gather | solution.py:729
  48.7 56.6 %copy-start.34 = (s32[1,2]{1,0:T(1,128)S(1)}, s32[1,2]{1,0:T(1,128)}, u32[]{:S(2)}) copy-start(s32[1,2]{1,0:T(1,128)} %param.13) | copy-start | bytes 28
  48.7 280.7 %all-gather.17.cloned.1.call-start = ((), (), s32[]{:S(2)}) async-start(), calls=%async_computation.3 | async-start | bytes 14745600 | tf_op jit(solution)/shard_map/all_gather | solution.py:729
  105.3 2.4 copy-start.21
  216.1 82.8 %copy-start.3 = (bf16[2,15,128,256]{3,2,1,0:T(8,128)(2,1)}, bf16[2,15,128,256]{3,2,1,0:T(8,128)(2,1)S(1)}, u32[]{:S(2)}) copy-start(bf16[2,15,128,256]{3,2,1,0:T(8,128)(2,1)S(1)} %get-tuple-element.94.q_ref) | copy-start | bytes 5898244
  216.1 6.1 copy-start.8
  300.0 16.9 %collective-permute-start = (bf16[15,67,256]{2,0,1:T(8,128)(2,1)}, bf16[15,67,256]{2,0,1:T(8,128)(2,1)}, u32[]{:S(2)}, u32[]{:S(2)}) collective-permute-start(bf16[15,67,256]{2,0,1:T(8,128)(2,1)} %copy.59), channel_id=1, source_target_pairs={{0,124},{4,120},{8,116},{12,112},{16,108},{20,104},{24,100},{28,96... | collective-permute-start | bytes 1543688 | tf_op jit(solution)/shard_map/ppermute | solution.py:786
  304.8 15.3 %copy-start.22 = (bf16[1,256,960]{1,2,0:T(8,128)(2,1)S(1)}, bf16[1,256,960]{1,2,0:T(8,128)(2,1)}, u32[]{:S(2)}) copy-start(bf16[1,256,960]{1,2,0:T(8,128)(2,1)} %param.12) | copy-start | bytes 1474564
  318.0 4.8 copy-start.13
  337.6 4.1 slice-start.2
  337.6 4.1 slice-start.3
  337.6 5.7 slice-start.4
  341.7 1.6 slice-start.5
  341.7 1.6 copy-start.18
  341.8 7.0 slice-start
  343.3 5.4 slice-start.1
  347.3 1.5 copy-start.16
  350.4 1.6 copy-start.20
  350.4 2.2 copy-start.14
  359.0 7.4 %copy-start.19 = (bf16[1,256,960]{1,2,0:T(8,128)(2,1)S(1)}, bf16[1,256,960]{1,2,0:T(8,128)(2,1)}, u32[]{:S(2)}) copy-start(bf16[1,256,960]{1,2,0:T(8,128)(2,1)} %param.23) | copy-start | bytes 1474564
  362.8 8.7 %slice-start.6 = ((s8[5242880]{0:T(1024)(128)(4,1)}), s8[1048576]{0:T(1024)(128)(4,1)S(1)}, s32[]{:S(2)}) async-start(s8[5242880]{0:T(1024)(128)(4,1)} %bitcast.203), calls=%async_computation.12 | async-start | bytes 2097152
  365.1 16.7 %collective-permute-start.1 = (bf16[15,70,256]{2,1,0:T(8,128)(2,1)}, bf16[15,70,256]{2,1,0:T(8,128)(2,1)S(1)}, u32[]{:S(2)}, u32[]{:S(2)}) collective-permute-start(bf16[15,70,256]{2,1,0:T(8,128)(2,1)} %concatenate.82), channel_id=1, source_target_pairs={{0,124},{4,120},{8,116},{12,112},{16,108},{20,104},{24,100},{28,96... | collective-permute-start | bytes 1612808 | tf_op jit(solution)/shard_map/ppermute | solution.py:831
  366.4 5.1 slice-start.7
  366.4 5.1 copy-start.17
  366.4 5.1 copy-start.26
  381.8 2.5 copy-start.29
  384.3 5.8 copy-start.4
  390.1 1.5 copy-start.5
  391.7 1.5 copy-start.6
  393.2 1.5 copy-start.7
  471.2 4.0 copy-start.2
  546.9 2.8 copy-start.24
  546.9 2.8 copy-start.33
  549.7 2.8 copy-start.12
  678.4 5.1 copy-start.9
  688.0 5.0 copy-start.11
  693.0 5.5 copy-start.1
  (5 other events, 5.9 us)
Sparse Core Ops, SparseCore 0:
  10.3 38.3 all-gather.18
  50.9 54.3 all-gather.14
  107.5 40.3 all-gather.10
  149.5 29.9 all-gather.12
  180.9 18.3 all-gather.20
  200.8 26.9 all-gather.16

commit v3 on v1

v3 whole, which is shorter than its diff:
```python
import functools

import jax
import jax.numpy as jnp
from jax import lax
from jax.experimental import pallas as pl
from jax.experimental.pallas import tpu as pltpu
from jax.sharding import PartitionSpec as P

QUERY_HEADS = 15
KEY_VALUE_HEADS = 5
HEAD_SIZE = 64
GROUP = QUERY_HEADS // KEY_VALUE_HEADS
PAIR = 2 * HEAD_SIZE
EPSILON = 1e-05
NEG = -1e30
BIG = 1e30
TAIL = 16
LOG2E = 1.4426950408889634
F32 = jnp.float32
BF16 = jnp.bfloat16


def dot_f32(left, right, dims=((1,), (0,))):
    return lax.dot_general(left, right, (dims, ((), ())), preferred_element_type=F32)


def ranges(me, half):
    light = me < half
    first = jnp.where(light, 0, me - half + 1)
    mirrored = jnp.where(light, half - me, 0)
    return first, mirrored


def query_index(owner, rows, height):
    column = lax.broadcasted_iota(jnp.int32, (height, GROUP * rows), 1)
    return owner * rows + (column & (rows - 1))


def visible_pairs(b0, b1, block, owner, rows):
    key = block * rows + lax.broadcasted_iota(jnp.int32, (rows, GROUP * rows), 0)
    query = query_index(owner, rows, rows)
    return (key <= query) & ((key >= b0) | (query < b0)) & ((key >= b1) | (query < b1))


def sweep(me, n, widest, step):
    first, mirrored = ranges(me, n // 2)

    def plain(which, low, high):
        turns = (high - low) // widest

        def several(i, carry):
            step(which, low + i * widest, widest, False, False)
            return carry

        lax.fori_loop(0, turns, several, 0)
        at, count = low + turns * widest, widest // 2
        while count:
            more = (high - at) >= count

            def rest(at=at, count=count):
                step(which, at, count, False, False)

            pl.when(more)(rest)
            at = at + jnp.where(more, count, 0)
            count //= 2

    @pl.when((first == 0) & (me > 0))
    def _():
        step(0, 0, 1, True, False)

    low = jnp.maximum(first, 1)
    plain(0, low, jnp.maximum(me, low))
    step(0, me, 1, True, True)

    @pl.when(mirrored > 0)
    def _():
        step(1, 0, 1, True, False)
        plain(1, 1, mirrored)


def lay_out(wide, first_row, own, mirrored):
    rows = own.shape[-1]
    for which, source in enumerate((own, mirrored)):
        wide[which] = jnp.zeros(wide.shape[1:], BF16)
        for g in range(GROUP):
            wide[which, first_row : first_row + HEAD_SIZE, g * rows : (g + 1) * rows] = source[g, :HEAD_SIZE]


def split_three(values):
    first = values.astype(BF16)
    rest = values - first.astype(F32)
    second = rest.astype(BF16)
    third = (rest - second.astype(F32)).astype(BF16)
    return first, second, third


def forward_kernel(n, place, kv_ref, q_own, q_mirrored, o_ref, stat_ref, sent_ref, wide_q, peak, mass, total):
    me, b0, b1 = place[0], place[1], place[2]
    rows = q_own.shape[-1]
    peak[...] = jnp.full_like(peak, NEG)
    mass[...] = jnp.zeros_like(mass)
    total[...] = jnp.zeros_like(total)
    lay_out(wide_q, 0, q_own, q_mirrored)

    def step(which, block, count, masked, diagonal):
        kv = kv_ref[pl.ds(pl.multiple_of(block * rows, rows), count * rows)]
        v_turned = kv.T[HEAD_SIZE:]
        old, held, summed = peak[which], mass[which], total[which]
        if diagonal:
            fresh = query_index(me, rows, 1) >= b1
            old = jnp.where(fresh, NEG, old)
            held = jnp.where(fresh, 0.0, held)
            summed = jnp.where(fresh, 0.0, summed)
        scores = dot_f32(kv, wide_q[which])
        if masked:
            owner = me if which == 0 else n - 1 - me
            scores = jnp.where(visible_pairs(b0, b1, block, owner, rows), scores, NEG)
        new = jnp.maximum(old, jnp.max(scores, axis=0, keepdims=True))
        weights = jnp.exp2((scores - new) * LOG2E)
        factor = jnp.exp2((old - new) * LOG2E)
        peak[which] = new
        mass[which] = held * factor + jnp.sum(weights, axis=0, keepdims=True)
        total[which] = summed * factor + dot_f32(v_turned, weights.astype(BF16))

    sweep(me, n, 4, step)
    for which in range(2):
        held = mass[which]
        live = held > 0.0
        safe = jnp.where(live, held, 1.0)
        result = total[which] / safe
        stat = jnp.where(live, peak[which] + jnp.log(safe), NEG)
        for g in range(GROUP):
            columns = slice(g * rows, (g + 1) * rows)
            if which == 0:
                o_ref[g] = result[:, columns]
                stat_ref[g] = stat[:, columns]
            else:
                sent_ref[g, :HEAD_SIZE] = result[:, columns].astype(BF16)
                tail = [part.astype(F32) for part in split_three(stat[:, columns])]
                tail.append(jnp.zeros((TAIL - 3, rows), F32))
                sent_ref[g, HEAD_SIZE:] = jnp.concatenate(tail).astype(BF16)


def per_group(*shape):
    return pl.BlockSpec((GROUP, *shape), lambda j: (j,) + (0,) * len(shape))


def attention_forward(n, place, kv, q_own, q_mirrored):
    heads, rows = kv.shape[0], q_own.shape[-1]
    units = (n + 1) * heads
    columns = GROUP * rows
    return pl.pallas_call(
        functools.partial(forward_kernel, n),
        grid=(heads,),
        out_shape=(
            jax.ShapeDtypeStruct((QUERY_HEADS, HEAD_SIZE, rows), F32),
            jax.ShapeDtypeStruct((QUERY_HEADS, 1, rows), F32),
            jax.ShapeDtypeStruct((QUERY_HEADS, HEAD_SIZE + TAIL, rows), BF16),
        ),
        in_specs=[
            pl.BlockSpec(memory_space=pltpu.SMEM),
            pl.BlockSpec((None, n * rows, PAIR), lambda j: (j, 0, 0)),
            per_group(HEAD_SIZE, rows),
            per_group(HEAD_SIZE, rows),
        ],
        out_specs=(per_group(HEAD_SIZE, rows), per_group(1, rows), per_group(HEAD_SIZE + TAIL, rows)),
        scratch_shapes=[
            pltpu.VMEM((2, PAIR, columns), BF16),
            pltpu.VMEM((2, 1, columns), F32),
            pltpu.VMEM((2, 1, columns), F32),
            pltpu.VMEM((2, HEAD_SIZE, columns), F32),
        ],
        compiler_params=pltpu.CompilerParams(vmem_limit_bytes=40 * 2**20),
        cost_estimate=pl.CostEstimate(
            flops=units * GROUP * rows * rows * 24 * PAIR,
            bytes_accessed=2 * n * rows * PAIR * heads,
            transcendentals=units * GROUP * rows * rows,
        ),
        name="attend_forward",
    )(place, kv, q_own, q_mirrored)


MESH = pl.DeviceIdType.MESH
GAIN_ROWS = 16


def torus(n):
    side = {32: 4, 8: 2, 4: 1}[n]
    return side, n // (2 * side)


def coordinates(n):
    sy, sz = torus(n)
    ctx, x = lax.axis_index("ctx"), lax.axis_index("wt")
    return {"x": x, "y": ctx // (2 * sz), "z": (ctx // 2) % sz, "core": ctx % 2}


def device_at(n, here, **moved):
    sy, sz = torus(n)
    at = {**here, **moved}
    return ((at["y"] * sz + at["z"]) * 2 + at["core"], at["x"])


def remote(source, target, send, receive, device):
    return pltpu.make_async_remote_copy(
        src_ref=source, dst_ref=target, send_sem=send, recv_sem=receive, device_id=device, device_id_type=MESH
    )


def greet(devices):
    barrier = pltpu.get_barrier_semaphore()
    for device in devices:
        pl.semaphore_signal(barrier, inc=1, device_id=device, device_id_type=MESH)
    pl.semaphore_wait(barrier, len(devices))


def peers_along(n, here, axis, size):
    return [lax.rem(here[axis] + d, size) for d in range(1, size)]


def mirror_of(n, here):
    sy, sz = torus(n)
    return device_at(n, here, y=sy - 1 - here["y"], z=sz - 1 - here["z"], core=1 - here["core"])


def plane_peers(n, here, sizes):
    return [device_at(n, here, **{a: i}) for a in "yz" for i in peers_along(n, here, a, sizes[a])]


def gather_kernel(n, own, query, blocks, mirrored, local_sem, step_send, step_recv, near_send, near_recv, far_sem):
    here = coordinates(n)
    sy, sz = torus(n)
    sizes = {"y": sy, "z": sz}
    y, z, core = here["y"], here["z"], here["core"]
    partner, mirror = device_at(n, here, core=1 - core), mirror_of(n, here)
    greet([partner, mirror] + plane_peers(n, here, sizes))
    half = own.shape[1] // 2
    part_rows = [pl.ds(part * half, half) for part in range(2)]

    def along(step, part):
        axis = "yz"[(step + part) % 2]
        rows = part_rows[part]
        copies = []
        for d, peer in enumerate(peers_along(n, here, axis, sizes[axis])):
            if step == 0:
                source, target = own.at[:, rows], blocks.at[:, y, z, core, rows]
            else:
                source = blocks.at[:, :, z, core, rows] if axis == "z" else blocks.at[:, y, :, core, rows]
                target = source
            copies.append(
                remote(
                    source, target, step_send.at[step, part, d], step_recv.at[step, part, d],
                    device_at(n, here, **{axis: peer}),
                )
            )
        return copies

    first = [along(0, 0), along(0, 1)]
    for copy in first[0] + first[1]:
        copy.start()
    to_mirror = remote(query, mirrored, far_sem.at[0], far_sem.at[1], mirror)
    keep = pltpu.make_async_copy(own, blocks.at[:, y, z, core], local_sem)
    keep.start()
    keep.wait()
    for copy in first[0] + first[1]:
        copy.wait_recv()
    second = [along(1, 0), along(1, 1)]
    for copy in second[0] + second[1]:
        copy.start()

    def give(slot, region):
        copy = remote(region, region, near_send.at[slot], near_recv.at[slot], partner)
        copy.start()
        return copy

    passed = [
        give(0, blocks.at[:, :, z, core, part_rows[0]]),
        give(1, blocks.at[:, y, :, core, part_rows[1]]),
    ]
    to_mirror.start()
    for d in range(max(sy, sz) - 1):
        if d < len(second[0]):
            second[0][d].wait_recv()
            passed.append(give(2 + 2 * d, blocks.at[:, :, lax.rem(z + sz - 1 - d, sz), core, part_rows[0]]))
        if d < len(second[1]):
            second[1][d].wait_recv()
            passed.append(give(3 + 2 * d, blocks.at[:, lax.rem(y + sy - 1 - d, sy), :, core, part_rows[1]]))
    for copy in passed:
        copy.wait_recv()
    to_mirror.wait_recv()
    for copy in first[0] + first[1] + second[0] + second[1] + passed + [to_mirror]:
        copy.wait_send()


def gather_blocks(own, query):
    n = lax.axis_size("ctx")
    sy, sz = torus(n)
    peers = max(sy, sz, 2) - 1
    heads, rows, pair = own.shape
    dma = pltpu.SemaphoreType.DMA
    anywhere = pl.BlockSpec(memory_space=pl.ANY)
    blocks, mirrored = pl.pallas_call(
        functools.partial(gather_kernel, n),
        out_shape=(
            jax.ShapeDtypeStruct((heads, sy, sz, 2, rows, pair), BF16),
            jax.ShapeDtypeStruct(query.shape, BF16),
        ),
        in_specs=[anywhere, anywhere],
        out_specs=(anywhere, anywhere),
        scratch_shapes=[
            dma, dma((2, 2, peers)), dma((2, 2, peers)), dma((2 + 2 * peers,)), dma((2 + 2 * peers,)), dma((2,)),
        ],
        compiler_params=pltpu.CompilerParams(collective_id=2, has_side_effects=True),
        cost_estimate=pl.CostEstimate(flops=5 * 10**10, bytes_accessed=heads * n * rows * pair * 4, transcendentals=0),
        name="gather_blocks",
    )(own, query)
    return blocks, mirrored


def exchange_kernel(n, sent, wide, down, got, full_wide, full_down, local_sem, send_sem, recv_sem):
    here = coordinates(n)
    core = here["core"]
    partner, mirror = device_at(n, here, core=1 - core), mirror_of(n, here)
    greet([partner, mirror])
    mine = [full_wide.at[core], full_down.at[:, core]]
    copies = [
        remote(source, target, send_sem.at[i], recv_sem.at[i], device)
        for i, (source, target, device) in enumerate(
            [(sent, got, mirror), (wide, mine[0], partner), (down, mine[1], partner)]
        )
    ]
    copies += [pltpu.make_async_copy(source, mine[i], local_sem.at[i]) for i, source in enumerate((wide, down))]
    for copy in copies:
        copy.start()
    for copy in copies:
        copy.wait()


def exchange(sent, wide, down):
    n = lax.axis_size("ctx")
    anywhere = pl.BlockSpec(memory_space=pl.ANY)
    dma = pltpu.SemaphoreType.DMA
    sx, rows, columns = down.shape
    return pl.pallas_call(
        functools.partial(exchange_kernel, n),
        out_shape=(
            jax.ShapeDtypeStruct(sent.shape, BF16),
            jax.ShapeDtypeStruct((2, *wide.shape), BF16),
            jax.ShapeDtypeStruct((sx, 2, rows, columns), BF16),
        ),
        in_specs=[anywhere] * 3,
        out_specs=(anywhere,) * 3,
        scratch_shapes=[dma((2,)), dma((3,)), dma((3,))],
        compiler_params=pltpu.CompilerParams(collective_id=4, has_side_effects=True),
        cost_estimate=pl.CostEstimate(flops=10**10, bytes_accessed=4 * wide.size, transcendentals=0),
        name="exchange",
    )(sent, wide, down)


ORDERS = ("xyz", "yzx", "zxy")


class TreeSum:
    def __init__(self, n, sizes, cuts, acc, near, steps, local_sem, near_send, near_recv, send_sem, recv_sem):
        self.n, self.sizes, self.cuts, self.acc, self.near, self.steps = n, sizes, cuts, acc, near, steps
        self.local_sem, self.near_send, self.near_recv = local_sem, near_send, near_recv
        self.send_sem, self.recv_sem = send_sem, recv_sem
        self.here = coordinates(n)
        self.partner = device_at(n, self.here, core=1 - self.here["core"])

    def place(self, buffer, x, chunk, column, width):
        deep, sz = buffer.shape[3], buffer.shape[2]
        row = chunk * 16
        inner = 0 if deep == 16 else pl.multiple_of(row % deep, 16)
        return buffer.at[x, row // (deep * sz), (row // deep) % sz, pl.ds(inner, 16), pl.ds(column, width)]

    def swap(self, pieces, tall):
        chunks, sx = tall // 16, self.sizes["x"]
        for core in range(2):

            def send(core=core):
                def one(i, carry):
                    x, chunk = i // chunks, i % chunks
                    for slot, (source, column, width) in enumerate(pieces(1 - core)):
                        remote(
                            source(x, chunk), self.place(self.near, x, chunk, column, width),
                            self.near_send.at[slot], self.near_recv.at[slot], self.partner,
                        ).start()
                    for slot, (source, column, width) in enumerate(pieces(core)):
                        pltpu.make_async_copy(
                            source(x, chunk), self.place(self.acc, x, chunk, column, width), self.local_sem.at[slot]
                        ).start()
                    return carry

                lax.fori_loop(0, sx * chunks, one, 0)

            pl.when(self.here["core"] == core)(send)

    def join(self, wholes, tall):
        for slot, whole in enumerate(wholes):
            pltpu.make_async_copy(whole, whole, self.local_sem.at[slot]).wait()
            remote(whole, whole, self.near_send.at[slot], self.near_recv.at[slot], self.partner).wait_recv()
        acc, near = self.acc, self.near
        sx, sy, sz, deep, wide = acc.shape
        chunks, every = tall // 16, sy * sz * deep // 16

        def one(i, carry):
            x, chunk = i // chunks, i % chunks
            mine = self.place(acc, x, chunk, 0, wide)
            mine[...] = mine[...] + self.place(near, x, chunk, 0, wide)[...]
            return carry

        lax.fori_loop(0, sx * chunks, one, 0)
        spare = every - chunks

        def blank(i, carry):
            target = self.place(acc, i // spare, chunks + i % spare, 0, wide)
            target[...] = jnp.zeros((16, wide), BF16)
            return carry

        lax.fori_loop(0, sx * spare, blank, 0)

    def sent_swap(self, wholes):
        for slot, whole in enumerate(wholes):
            remote(whole, whole, self.near_send.at[slot], self.near_recv.at[slot], self.partner).wait_send()

    def region(self, third, done, axis=None, index=None):
        column, width = self.cuts[third]
        at = {a: self.here[a] for a in done}
        if axis is not None:
            at[axis] = index
        pick = [at[a] if a in at else slice(None) for a in "xyz"]
        return self.acc.at[(*pick, slice(None), pl.ds(column, width))]

    def copies(self, third, step):
        axis = ORDERS[third][step]
        return [
            remote(
                self.region(third, ORDERS[third][:step], axis, peer),
                self.steps[third * 3 + step].at[d],
                self.send_sem.at[third, step, d],
                self.recv_sem.at[third, step, d],
                device_at(self.n, self.here, **{axis: peer}),
            )
            for d, peer in enumerate(peers_along(self.n, self.here, axis, self.sizes[axis]))
        ]

    def start(self, step):
        for third in range(3):
            for copy in self.copies(third, step):
                copy.start()

    def finish(self, step, follow):
        for third in range(3):
            copies = self.copies(third, step)
            for copy in copies:
                copy.wait_recv()
            buffer = self.steps[third * 3 + step]
            mine = self.region(third, ORDERS[third][: step + 1])
            lead = mine.shape[:-2]
            count = 1
            for extent in lead:
                count *= extent

            def add(i, carry):
                at = []
                for extent in reversed(lead):
                    at.append(i % extent)
                    i = i // extent
                at = tuple(reversed(at))
                total = mine[(*at, slice(None), slice(None))].astype(F32)
                for d in range(len(copies)):
                    total += buffer[(d, *at)].astype(F32)
                mine[(*at, slice(None), slice(None))] = total.astype(BF16)
                return carry

            if count == 1:
                add(0, 0)
            else:
                lax.fori_loop(0, count, add, 0)
            if follow:
                for copy in self.copies(third, step + 1):
                    copy.start()

    def sent_steps(self):
        for step in range(3):
            for third in range(3):
                for copy in self.copies(third, step):
                    copy.wait_send()


def tree_peers(n, here, sizes):
    return [device_at(n, here, **{a: i}) for a in "xyz" for i in peers_along(n, here, a, sizes[a])]


def tree_layout(n, sx, tall, wide):
    sy, sz = torus(n)
    sizes = {"x": sx, "y": sy, "z": sz}
    deep = -(-(tall + GAIN_ROWS) // (16 * sy * sz)) * 16
    third = wide // 384 * 128
    cuts = [(0, third), (third, third), (2 * third, wide - 2 * third)]
    buffers = []
    for order, (_, width) in zip(ORDERS, cuts):
        for step in range(3):
            shape = [sizes[a] for a in "xyz" if a not in order[: step + 1]]
            buffers.append(pltpu.VMEM((max(sizes[order[step]] - 1, 1), *shape, deep, width), BF16))
    peers = max(sx, sy, sz)
    dma = pltpu.SemaphoreType.DMA
    sems = [dma((2,)), dma((2,)), dma((2,)), dma((3, 3, peers)), dma((3, 3, peers))]
    block = pltpu.VMEM((sx, sy, sz, deep, wide), BF16)
    return sizes, cuts, [block, block], buffers, sems


def backward_kernel(
    n, sizes, cuts, tall, place, kv_ref, q_own, q_mirrored, do_own, do_mirrored, stat_ref, gate, up, down,
    dq_ref, home_ref, piece_ref,
    wide_q, wide_do, tall_q, tall_do, stats, dq, gathered, dq_stage, dq_far, kv_acc, kv_near, kv_stage, *rest,
):
    kv_steps, rest = rest[:4], rest[4:]
    swap_send, swap_recv, step_send, step_recv, far_send, far_recv = rest[:6]
    rest = rest[6:]
    tree = TreeSum(n, sizes, cuts, rest[0], rest[1], rest[2:11], *rest[11:])
    here = coordinates(n)
    sy, sz = torus(n)
    y, z, core = here["y"], here["z"], here["core"]
    partner, mirror = tree.partner, mirror_of(n, here)
    me, b0, b1 = lax.axis_index("ctx"), place[1], place[2]
    head = pl.program_id(0)
    heads = home_ref.shape[0]
    rows = q_own.shape[-1]
    half = n // 2
    first, _ = ranges(me, half)
    width = gate.shape[1]
    block = width // sizes["x"]

    def pieces(of):
        main = (gate, up)[of]
        found = [(lambda x, c: main.at[pl.ds(pl.multiple_of(x * tall + c * 16, 16), 16), :], 0, width)]
        each = sizes["x"] // 2
        for k in range(each):
            row = (of * each + k) * tall
            found.append(
                (
                    lambda x, c, row=row: down.at[
                        pl.ds(pl.multiple_of(row + c * 16, 16), 16), pl.ds(pl.multiple_of(x * block, 128), block)
                    ],
                    width + k * block,
                    block,
                )
            )
        return found

    wholes = [gate] + [down.at[pl.ds(0, tall), :]] * (sizes["x"] // 2)

    def swap(h):
        return remote(kv_stage.at[h % 2], kv_near.at[h], swap_send.at[h], swap_recv.at[h], partner)

    def region(h, part, done, axis=None, index=None):
        at = {a: here[a] for a in done}
        if axis is not None:
            at[axis] = index
        pick = [at[a] if a in at else slice(None) for a in "yz"]
        return kv_acc.at[(h, *pick, pl.ds(part * (rows // 2), rows // 2))]

    def steps(h, step, part):
        order = ("yz", "zy")[part]
        axis = order[step]
        return [
            remote(
                region(h, part, order[:step], axis, peer),
                kv_steps[part * 2 + step].at[h, d],
                step_send.at[h, step * 2 + part, d],
                step_recv.at[h, step * 2 + part, d],
                device_at(n, here, **{axis: peer}),
            )
            for d, peer in enumerate(peers_along(n, here, axis, sizes[axis]))
        ]

    def start_steps(h, step):
        for part in range(2):
            for copy in steps(h, step, part):
                copy.start()

    def finish_swap(h):
        swap(h).wait_recv()

        def one(i, carry):
            a, b = i // sz, i % sz
            kv_acc[h, a, b] = kv_acc[h, a, b] + kv_near[h, a, b]
            return carry

        lax.fori_loop(0, sy * sz, one, 0)
        start_steps(h, 0)

    def finish_step(h, step):
        for part in range(2):
            copies = steps(h, step, part)
            for copy in copies:
                copy.wait_recv()
            buffer = kv_steps[part * 2 + step]
            mine = region(h, part, ("yz", "zy")[part][: step + 1])
            for i in range(mine.shape[0] if step == 0 else 1):
                at = (i,) if step == 0 else ()
                total = mine[(*at, slice(None), slice(None))].astype(F32)
                for d in range(len(copies)):
                    total += buffer[(h, d, *at)].astype(F32)
                mine[(*at, slice(None), slice(None))] = total.astype(BF16)
        if step == 0:
            start_steps(h, 1)
        else:
            home_ref[h] = kv_acc[h, y, z]

    def to_mirror(h):
        return remote(dq_stage.at[h], dq_far.at[h], far_send.at[h], far_recv.at[h], mirror)

    @pl.when(head == 0)
    def _():
        greet([partner, mirror] + tree_peers(n, here, sizes))
        tree.swap(pieces, tall)

    gathered[...] = jnp.zeros_like(gathered)
    dq[...] = jnp.zeros_like(dq)
    lay_out(wide_q, 0, q_own, q_mirrored)
    lay_out(wide_do, HEAD_SIZE, do_own, do_mirrored)
    for which in range(2):
        for g in range(GROUP):
            columns = slice(g * rows, (g + 1) * rows)
            tall_q[which, columns] = wide_q[which, :, columns].T
            tall_do[which, columns] = wide_do[which, :, columns].T
    for g in range(GROUP):
        columns = slice(g * rows, (g + 1) * rows)
        got = do_mirrored[g, HEAD_SIZE:].astype(F32)
        stats[0, :, columns] = jnp.concatenate([stat_ref[g, 0:1], stat_ref[g, 2:3]])
        stats[1, :, columns] = jnp.concatenate([got[0:1] + got[1:2] + got[2:3], got[3:4] + got[4:5] + got[5:6]])
        stats[2, :, columns] = stat_ref[g, 1:3]

    def attend(which, block, count, masked, diagonal):
        kv = kv_ref[pl.ds(pl.multiple_of(block * rows, rows), count * rows)]
        k_turned = kv.T[:HEAD_SIZE]
        kind = 2 if diagonal else which
        scores = dot_f32(kv, wide_q[which])
        weights = jnp.exp2((scores - stats[kind, 0:1]) * LOG2E)
        if masked:
            owner = me if which == 0 else n - 1 - me
            weights = jnp.where(visible_pairs(b0, b1, block, owner, rows), weights, 0.0)
        weight_grad = dot_f32(kv, wide_do[which])
        score_grad = (weights * (weight_grad - stats[kind, 1:2])).astype(BF16)
        more = dot_f32(score_grad, tall_q[which]) + dot_f32(weights.astype(BF16), tall_do[which])
        dq[which] += dot_f32(k_turned, score_grad)
        at = pl.ds(pl.multiple_of((block - first) * rows, rows), count * rows)
        gathered[at] += more

    sweep(me, n, 2, attend)

    for g in range(GROUP):
        columns = slice(g * rows, (g + 1) * rows)
        dq_ref[head * GROUP + g] = dq[0, :, columns]
        dq_stage[head, g] = dq[1, :, columns].astype(BF16)
    to_mirror(head).start()

    @pl.when(head >= 2)
    def _():
        swap(head - 2).wait_send()

    def take(i, carry):
        a, b = i // sz, i % sz
        for target, which_core in ((kv_acc.at[head, a, b], core), (kv_stage.at[head % 2, a, b], 1 - core)):
            slot = 2 * i + which_core - first
            inside = (slot >= 0) & (slot < half)
            at = jnp.clip(slot, 0, half - 1)
            values = gathered[pl.ds(pl.multiple_of(at * rows, rows), rows)]
            target[...] = jnp.where(inside, values, 0.0).astype(BF16)
        return carry

    lax.fori_loop(0, sy * sz, take, 0)
    swap(head).start()

    @pl.when(head >= 1)
    def _():
        finish_swap(head - 1)

    @pl.when(head >= 2)
    def _():
        finish_step(head - 2, 0)

    @pl.when(head >= 3)
    def _():
        finish_step(head - 3, 1)

    @pl.when(head == 0)
    def _():
        tree.join(wholes, tall)
        tree.start(0)

    @pl.when(head == 3)
    def _():
        tree.finish(0, True)

    @pl.when(head == heads - 1)
    def _():
        last = heads - 1
        finish_swap(last)
        finish_step(last - 1, 0)
        tree.finish(1, True)
        finish_step(last - 2, 1)
        tree.finish(2, False)
        piece_ref[...] = tree.acc[here["x"], y, z]
        finish_step(last, 0)
        finish_step(last - 1, 1)
        for h in range(heads):
            to_mirror(h).wait_recv()
            for g in range(GROUP):
                dq_ref[h * GROUP + g] += dq_far[h, g].astype(F32)
        finish_step(last, 1)
        for h in range(heads):
            to_mirror(h).wait_send()
            for step in range(2):
                for part in range(2):
                    for copy in steps(h, step, part):
                        copy.wait_send()
        swap(last - 1).wait_send()
        swap(last).wait_send()
        tree.sent_swap(wholes)
        tree.sent_steps()


def attention_backward(n, place, kv, q_own, q_mirrored, do_own, do_mirrored, stats, gate, up, down):
    heads, rows = kv.shape[0], q_own.shape[-1]
    units = (n + 1) * heads
    columns = GROUP * rows
    sx = lax.axis_size("wt")
    sy, sz = torus(n)
    tall = gate.shape[0] // sx
    wide = gate.shape[1] + gate.shape[1] // 2
    sizes, cuts, blocks, buffers, sems = tree_layout(n, sx, tall, wide)
    sems[0:3] = [pltpu.SemaphoreType.DMA((1 + sx // 2,))] * 3
    extents = {"y": sy, "z": sz}
    kv_steps = []
    for order in ("yz", "zy"):
        kv_steps.append(
            pltpu.VMEM((heads, max(extents[order[0]] - 1, 1), extents[order[1]], rows // 2, PAIR), BF16)
        )
        kv_steps.append(pltpu.VMEM((heads, max(extents[order[1]] - 1, 1), rows // 2, PAIR), BF16))
    peers = max(sy, sz, 2) - 1
    dma = pltpu.SemaphoreType.DMA
    anywhere = pl.BlockSpec(memory_space=pl.ANY)
    fixed = lambda *shape: pl.BlockSpec(shape, lambda j: (0,) * len(shape))
    deep = blocks[0].shape[3]
    return pl.pallas_call(
        functools.partial(backward_kernel, n, sizes, cuts, tall),
        grid=(heads,),
        out_shape=(
            jax.ShapeDtypeStruct((QUERY_HEADS, HEAD_SIZE, rows), F32),
            jax.ShapeDtypeStruct((heads, rows, PAIR), BF16),
            jax.ShapeDtypeStruct((deep, wide), BF16),
        ),
        in_specs=[
            pl.BlockSpec(memory_space=pltpu.SMEM),
            pl.BlockSpec((None, n * rows, PAIR), lambda j: (j, 0, 0)),
            per_group(HEAD_SIZE, rows),
            per_group(HEAD_SIZE, rows),
            per_group(HEAD_SIZE, rows),
            per_group(HEAD_SIZE + TAIL, rows),
            per_group(3, rows),
            anywhere,
            anywhere,
            anywhere,
        ],
        out_specs=(fixed(QUERY_HEADS, HEAD_SIZE, rows), fixed(heads, rows, PAIR), fixed(deep, wide)),
        scratch_shapes=[
            pltpu.VMEM((2, PAIR, columns), BF16),
            pltpu.VMEM((2, PAIR, columns), BF16),
            pltpu.VMEM((2, columns, PAIR), BF16),
            pltpu.VMEM((2, columns, PAIR), BF16),
            pltpu.VMEM((3, 2, columns), F32),
            pltpu.VMEM((2, HEAD_SIZE, columns), F32),
            pltpu.VMEM((n // 2 * rows, PAIR), F32),
            pltpu.VMEM((heads, GROUP, HEAD_SIZE, rows), BF16),
            pltpu.VMEM((heads, GROUP, HEAD_SIZE, rows), BF16),
            pltpu.VMEM((heads, sy, sz, rows, PAIR), BF16),
            pltpu.VMEM((heads, sy, sz, rows, PAIR), BF16),
            pltpu.VMEM((2, sy, sz, rows, PAIR), BF16),
            *kv_steps,
            dma((heads,)), dma((heads,)), dma((heads, 4, peers)), dma((heads, 4, peers)), dma((heads,)), dma((heads,)),
            *blocks,
            *buffers,
            *sems,
        ],
        compiler_params=pltpu.CompilerParams(
            collective_id=3, has_side_effects=True, vmem_limit_bytes=61 * 2**20
        ),
        cost_estimate=pl.CostEstimate(
            flops=units * GROUP * rows * rows * 40 * PAIR,
            bytes_accessed=4 * n * rows * PAIR * heads,
            transcendentals=units * GROUP * rows * rows,
        ),
        name="attend_backward",
    )(place, kv, q_own, q_mirrored, do_own, do_mirrored, stats, gate, up, down)


def last_kernel(n, sizes, cuts, tall, first, gains, piece, out, acc, near, *rest):
    buffers, sems, rest = rest[:9], rest[9:14], rest[14:]
    near_gains, gain_sem, spread_send, spread_recv, home_sem = rest
    tree = TreeSum(n, sizes, cuts, acc, near, buffers, *sems)
    here = coordinates(n)
    x, y, z, core = here["x"], here["y"], here["z"], here["core"]
    partner = tree.partner
    greet([partner] + tree_peers(n, here, sizes))
    wide = acc.shape[4]
    sx, sy, sz, deep = acc.shape[:4]

    def pieces(of):
        return [
            (
                lambda x, c: first.at[pl.ds(pl.multiple_of(x * tall + c * 16, 16), 16), pl.ds(of * wide, wide)],
                0,
                wide,
            )
        ]

    wholes = [first.at[:, pl.ds(0, wide)]]
    to_partner = remote(gains, near_gains, gain_sem.at[0], gain_sem.at[1], partner)
    to_partner.start()
    tree.swap(pieces, tall)
    spans = ((wide, piece.shape[1]), (0, wide))

    def spread(kind, step):
        found = []
        for part in range(2):
            half = spans[kind][1] // 2
            columns = pl.ds(spans[kind][0] + part * half, half)
            axis = "yz"[(step + part) % 2]
            if step == 0:
                source = out.at[core, y, z, :, columns]
            elif axis == "z":
                source = out.at[core, :, z, :, columns]
            else:
                source = out.at[core, y, :, :, columns]
            found += [
                remote(
                    source, source, spread_send.at[kind, step, part, d], spread_recv.at[kind, step, part, d],
                    device_at(n, here, **{axis: peer}),
                )
                for d, peer in enumerate(peers_along(n, here, axis, sizes[axis]))
            ]
        return found

    def home(kind):
        half = out.at[core, :, :, :, pl.ds(*spans[kind])]
        return remote(half, half, home_sem.at[kind], home_sem.at[2 + kind], partner)

    def start(copies):
        for copy in copies:
            copy.start()

    def arrived(copies):
        for copy in copies:
            copy.wait_recv()

    out[core, y, z, :, pl.ds(wide, piece.shape[1])] = piece[...]
    start(spread(0, 0))
    tree.join(wholes, tall)
    to_partner.wait_recv()
    both = gains[...] + near_gains[...]
    row = tall % deep
    acc[:, tall // (deep * sz), (tall // deep) % sz, row : row + GAIN_ROWS, : gains.shape[2]] = both
    tree.start(0)
    arrived(spread(0, 0))
    start(spread(0, 1))
    tree.finish(0, True)
    tree.finish(1, True)
    tree.finish(2, False)
    out[core, y, z, :, pl.ds(0, wide)] = acc[x, y, z]
    start(spread(1, 0))
    arrived(spread(0, 1))
    home(0).start()
    arrived(spread(1, 0))
    start(spread(1, 1))
    arrived(spread(1, 1))
    home(1).start()
    arrived([home(0), home(1)])
    for kind in range(2):
        for copy in spread(kind, 0) + spread(kind, 1) + [home(kind)]:
            copy.wait_send()
    to_partner.wait_send()
    tree.sent_swap(wholes)
    tree.sent_steps()


def last_sums(first, gains, piece):
    n, sx = lax.axis_size("ctx"), lax.axis_size("wt")
    sy, sz = torus(n)
    tall = first.shape[0] // sx
    wide = first.shape[1] // 2
    sizes, cuts, blocks, buffers, sems = tree_layout(n, sx, tall, wide)
    deep = blocks[0].shape[3]
    peers = max(sy, sz, 2) - 1
    dma = pltpu.SemaphoreType.DMA
    inside = pl.BlockSpec(memory_space=pltpu.VMEM)
    out = pl.pallas_call(
        functools.partial(last_kernel, n, sizes, cuts, tall),
        out_shape=jax.ShapeDtypeStruct((2, sy, sz, deep, wide + piece.shape[1]), BF16),
        in_specs=[pl.BlockSpec(memory_space=pl.ANY), inside, inside],
        out_specs=inside,
        scratch_shapes=[
            *blocks, *buffers, *sems,
            pltpu.VMEM(gains.shape, BF16), dma((2,)), dma((2, 2, 2, peers)), dma((2, 2, 2, peers)), dma((4,)),
        ],
        compiler_params=pltpu.CompilerParams(
            collective_id=1, has_side_effects=True, vmem_limit_bytes=40 * 2**20
        ),
        name="last_sums",
    )(first, gains, piece)
    return out.reshape(2, sy * sz * deep, out.shape[4])


def rms_forward(values, gain):
    inverse = lax.rsqrt(jnp.mean(values * values, axis=-1, keepdims=True) + EPSILON)
    normal = values * inverse
    return (normal * gain, normal, inverse)


def rms_backward(upstream, gain, normal, inverse):
    scaled = upstream * gain
    inner = jnp.mean(scaled * normal, axis=-1, keepdims=True)
    return (inverse * (scaled - normal * inner), jnp.sum(upstream * normal, axis=0))


def positions_of(edges, me, rows):
    token = me * rows + jnp.arange(rows, dtype=jnp.int32)
    start = jnp.where(token >= edges[1], edges[1], jnp.where(token >= edges[0], edges[0], 0))
    return token, token - start


def turn(heads, cosine, sine):
    half = HEAD_SIZE // 2
    low, high = heads[:, :half], heads[:, half:]
    return jnp.concatenate([low * cosine - high * sine, high * cosine + low * sine], axis=1)


def turn_back(heads, cosine, sine):
    half = HEAD_SIZE // 2
    low, high = heads[:, :half], heads[:, half:]
    return jnp.concatenate([low * cosine + high * sine, high * cosine - low * sine], axis=1)


def three_parts(values):
    first = lax.reduce_precision(values, 8, 7)
    rest = values - first
    second = lax.reduce_precision(rest, 8, 7)
    third = rest - second
    return [part.astype(BF16) for part in (first, second, third)]


def joined(parts):
    return parts[0].astype(F32) + parts[1].astype(F32) + parts[2].astype(F32)


def gather_weight(shard):
    return lax.all_gather(shard, "wt", axis=0, tiled=True)


def per_device(
    layer_input,
    doc_bounds,
    attn_gain,
    w_query,
    key_weight,
    value_weight,
    w_out,
    mlp_gain,
    w_gate,
    w_up,
    w_down,
    cotangent,
):
    n = lax.axis_size("ctx")
    me = lax.axis_index("ctx")
    rows, width = layer_input.shape[1:]
    queries = QUERY_HEADS * HEAD_SIZE
    keys = KEY_VALUE_HEADS * HEAD_SIZE
    edges = doc_bounds[0]
    place = jnp.concatenate([jnp.full((1,), me, jnp.int32), edges])
    across = [(i, n - 1 - i) for i in range(n)]

    gains = jnp.pad(jnp.stack([attn_gain, mlp_gain], axis=1), ((0, 0), (0, 62)))
    shard_qkv = jnp.concatenate([w_query, key_weight, value_weight, gains], axis=1)
    full_qkv = gather_weight(shard_qkv)
    full_qkv, w_out, w_gate, w_up, w_down = lax.optimization_barrier((full_qkv, w_out, w_gate, w_up, w_down))
    gain_rows = full_qkv[:, queries + 2 * keys : queries + 2 * keys + 2].T.astype(F32)
    attn_scale, mlp_scale = gain_rows[0], gain_rows[1]
    full_qkv = full_qkv[:, : queries + 2 * keys]

    x = layer_input[0].astype(F32)
    normed, normal_in, inverse_in = rms_forward(x, attn_scale)
    normed = normed.astype(BF16)
    turned = dot_f32(full_qkv, normed, ((0,), (1,)))
    token, position = positions_of(edges, me, rows)
    freqs = 10000.0 ** (-jnp.arange(HEAD_SIZE // 2, dtype=F32) * 2.0 / HEAD_SIZE)
    angles = freqs[:, None] * position.astype(F32)[None, :]
    cosine, sine = jnp.cos(angles), jnp.sin(angles)

    q = turn(turned[:queries].reshape(QUERY_HEADS, HEAD_SIZE, rows), cosine, sine).astype(BF16)
    k = turn(turned[queries : queries + keys].reshape(KEY_VALUE_HEADS, HEAD_SIZE, rows), cosine, sine).astype(BF16)
    v = turned[queries + keys :].reshape(KEY_VALUE_HEADS, HEAD_SIZE, rows).astype(BF16)
    q = q * BF16(HEAD_SIZE**-0.5)
    own_kv = jnp.concatenate([k, v], axis=1).transpose(0, 2, 1)

    kv, mirrored = gather_blocks(own_kv, q)
    kv = kv.reshape(KEY_VALUE_HEADS, n * rows, PAIR)

    core = me % 2
    full_out = gather_weight(w_out)
    along_wide = lax.all_gather(jnp.where(core == 0, w_gate, w_up), "wt", axis=0)
    down_rows = w_down.shape[0] // 2
    along_down = lax.all_gather(lax.dynamic_slice_in_dim(w_down, core * down_rows, down_rows), "wt", axis=0)

    later = token >= edges[1]
    o_part, stat_part, sent = attention_forward(n, place, kv, q, mirrored)
    got, full_wide, full_down = exchange(sent, along_wide, along_down)
    full_wide = full_wide.reshape(2, width, -1)
    full_gate, full_up = full_wide[0], full_wide[1]
    full_down = full_down.reshape(-1, width)
    other_stat = joined([got[:, HEAD_SIZE + i : HEAD_SIZE + i + 1] for i in range(3)])
    other_stat = jnp.where(later, NEG, other_stat)
    log_total = jnp.logaddexp(stat_part, other_stat)
    attended = o_part * jnp.exp(stat_part - log_total) + got[:, :HEAD_SIZE].astype(F32) * jnp.exp(
        other_stat - log_total
    )
    mixed = attended.reshape(queries, rows).astype(BF16)

    resid = x + dot_f32(mixed, full_out, ((0,), (0,)))
    normed_two, normal_mlp, inverse_mlp = rms_forward(resid, mlp_scale)
    normed_two = normed_two.astype(BF16)
    gate = dot_f32(normed_two, full_gate)
    up = dot_f32(normed_two, full_up)
    sig = jax.nn.sigmoid(gate)
    activated = gate * sig
    hidden = (activated * up).astype(BF16)
    layer_output = (resid + dot_f32(hidden, full_down)).astype(BF16)[None]
    upstream = cotangent[0]
    grad_w_down = dot_f32(upstream, hidden, ((0,), (0,)))
    grad_hidden = dot_f32(upstream, full_down, ((1,), (1,)))
    grad_up_in = (grad_hidden * activated).astype(BF16)
    grad_gate_in = (grad_hidden * up * sig * (1.0 + gate * (1.0 - sig))).astype(BF16)
    grad_w_gate = dot_f32(normed_two, grad_gate_in, ((0,), (0,)))
    grad_w_up = dot_f32(normed_two, grad_up_in, ((0,), (0,)))
    grad_normed_two = dot_f32(grad_gate_in, full_gate, ((1,), (1,))) + dot_f32(
        grad_up_in, full_up, ((1,), (1,))
    )
    grad_resid_mlp, grad_mlp_gain = rms_backward(grad_normed_two, mlp_scale, normal_mlp, inverse_mlp)
    grad_resid = upstream.astype(F32) + grad_resid_mlp
    grad_mixed = grad_resid.astype(BF16)
    grad_w_out = dot_f32(mixed, grad_mixed)
    grad_attended = dot_f32(full_out, grad_mixed, ((1,), (1,))).astype(BF16)
    grad_attended = grad_attended.reshape(QUERY_HEADS, HEAD_SIZE, rows)
    grad_dot = jnp.sum(grad_attended.astype(F32) * attended, axis=1, keepdims=True)

    before = jnp.where(later, BIG, log_total)
    blank = jnp.zeros((QUERY_HEADS, TAIL - 6, rows), BF16)
    sent = jnp.concatenate([grad_attended] + three_parts(before) + three_parts(grad_dot) + [blank], axis=1)
    got = lax.ppermute(sent, "ctx", across)
    stats = jnp.concatenate([before, log_total, grad_dot], axis=1)
    dq, dkv, piece = attention_backward(
        n, place, kv, q, mirrored, grad_attended, got, stats,
        grad_w_gate.astype(BF16), grad_w_up.astype(BF16), grad_w_down.astype(BF16),
    )
    grad_q = turn_back(dq * HEAD_SIZE**-0.5, cosine, sine).astype(BF16)
    dkv = dkv.astype(F32).transpose(0, 2, 1)
    grad_k = turn_back(dkv[:, :HEAD_SIZE], cosine, sine).astype(BF16)
    grad_v = dkv[:, HEAD_SIZE:].astype(BF16)
    grad_qkv = jnp.concatenate(
        [grad_q.reshape(queries, rows), grad_k.reshape(keys, rows), grad_v.reshape(keys, rows)]
    )
    grad_w_qkv = dot_f32(normed, grad_qkv, ((0,), (1,)))
    grad_normed = dot_f32(grad_qkv, full_qkv, ((0,), (1,)))
    grad_in, grad_attn_gain = rms_backward(grad_normed, attn_scale, normal_in, inverse_in)
    input_grad = (grad_resid + grad_in)[None]

    sx = lax.axis_size("wt")
    tall = width // sx
    gains = jnp.stack([grad_attn_gain, grad_mlp_gain]).reshape(2, sx, tall).transpose(1, 0, 2)
    gains = jnp.pad(gains, ((0, 0), (0, GAIN_ROWS - 2), (0, -tall % 128))).astype(BF16)
    first = jnp.concatenate([grad_w_qkv.astype(BF16), grad_w_out.astype(BF16)], axis=1)
    sums = last_sums(first, gains, piece)
    wide = first.shape[1] // 2
    ff = w_gate.shape[1]
    block = ff // sx
    gain_sums = sums[0, tall : tall + 2, :tall].astype(F32)
    sums = sums[:, :tall].astype(F32)
    mixed_sums = jnp.concatenate([sums[0, :, :wide], sums[1, :, :wide]], axis=1)
    sum_down = jnp.concatenate(
        [sums[i, :, at : at + block] for i in range(2) for at in range(wide + ff, wide + ff + ff // 2, block)]
    ).T
    return (
        layer_output,
        input_grad,
        gain_sums[0],
        mixed_sums[:, :queries],
        mixed_sums[:, queries : queries + keys],
        mixed_sums[:, queries + keys : queries + 2 * keys],
        mixed_sums[:, queries + 2 * keys :],
        gain_sums[1],
        sums[0, :, wide : wide + ff],
        sums[1, :, wide : wide + ff],
        sum_down,
    )


def solution(mesh):
    tokens, weights, gains = P("wt", "ctx", None), P("wt", None), P("wt")
    return jax.shard_map(
        per_device,
        mesh=mesh,
        in_specs=(
            tokens, weights, gains, weights, weights, weights, weights, gains, weights, weights, weights, tokens,
        ),
        out_specs=(
            tokens, tokens, gains, weights, weights, weights, weights, gains, weights, weights, weights,
        ),
        check_vma=False,
    )
```

time: 978 us -> 680 us (0.70)
  waiting for transfers between devices: 569 us -> 46.3 us
  Pallas kernels: 153 us -> 500 us
  blocking collectives: 65.6 us -> 0 us
  local copies, waits for them, and re-layouts: 59.5 us -> 41.7 us
  matrix products: 59.6 us -> 43.2 us
  other arithmetic: 33.7 us -> 23.3 us
    pallas_call x1 -> x4, Pallas kernels: 76.4 us -> 458 us  [the longest x1 230 us: exchange(): pl.pallas_call(functools.partial(exchange_kernel, n), out_shape=(jax.Shap...]
    reduce_scatter x4 -> x0, waiting for transfers between devices: 180 us -> none  [reduce_gradient(): lax.psum_scatter(gradient.astype(BF16), 'wt', scatter_dimension=0, tiled=...]
    unnamed x15 -> x4, waiting for transfers between devices: 135 us -> 0.07 us
    all_gather x5 -> x2, waiting for transfers between devices: 123 us -> 43.2 us  [gather_weight(): return lax.all_gather(shard, 'wt', axis=0, tiled=True)]
    psum x1 -> x0, blocking collectives: 65.6 us -> none  [per_device(): lax.psum(jnp.stack([grad_attn_gain, grad_mlp_gain]).astype(BF16), ('wt',...]
    psum x1 -> x0, waiting for transfers between devices: 43.7 us -> none  [reduce_gradient(): return lax.psum(part, 'ctx').astype(F32)]
    pallas_call x1, Pallas kernels: 76.6 us -> 41.2 us  [attention_forward(): pl.pallas_call(functools.partial(forward_kernel, n), grid=(heads,), out_s...]
    ppermute x2 -> x0, waiting for transfers between devices: 32.5 us -> none  [the longest x1 17.9 us: per_device(): other = lax.ppermute(dq[1].astype(BF16), 'ctx', across)]
  transfers between devices with their start and end apart: 17 -> 5, of which waited for: 15 -> 2; matrix products, arithmetic and copies ran while one was open for 9% -> 5% of each run, Pallas kernels for 8% -> 49%
where the time goes in v3:
time: 680 us; the launch traced here: 674 us
  Pallas kernels  500 us (74%)
  waiting for transfers between devices  46.3 us (7%)
  matrix products  43.2 us (6%)
  local copies, waits for them, and re-layouts  41.7 us (6%)
  other arithmetic  23.3 us (3%)
  between operations  14.8 us (2%)
    pallas_call x1, Pallas kernels, exchange(): pl.pallas_call(functools.partial(exchange_kernel, n), out_shape=(jax.Shap...  230 us
    pallas_call x1, Pallas kernels, attention_backward(): pl.pallas_call(functools.partial(backward_kernel, n, sizes, cuts, tall),...  120 us
    pallas_call x1, Pallas kernels, gather_blocks(): pl.pallas_call(functools.partial(gather_kernel, n), out_shape=(jax.ShapeD...  57.2 us
    pallas_call x1, Pallas kernels, last_sums(): pl.pallas_call(functools.partial(last_kernel, n, sizes, cuts, tall), out_...  51.4 us
    all_gather x2, waiting for transfers between devices, gather_weight(): return lax.all_gather(shard, 'wt', axis=0, tiled=True)  43.2 us
    dot_general x15, matrix products, dot_f32(): lax.dot_general(left, right, (dims, ((), ())), preferred_element_type=F32)  43.2 us
    pallas_call x1, Pallas kernels, attention_forward(): pl.pallas_call(functools.partial(forward_kernel, n), grid=(heads,), out_s...  41.2 us
    unnamed x92, local copies, waits for them, and re-layouts  16.3 us
  transfers between devices with their start and end apart: 5, of which 2 were waited for; matrix products, arithmetic and copies ran while one was open for 5% of the time, Pallas kernels for 49%

profile of v3, /device:TPU:1, one launch (start us, length us, event | category | flops | bytes accessed | tf_op | source)
XLA Modules:
  0.0 674.3 jit_solution(11827435917779879934)
XLA Ops:
  8.8 1.1 copy.47
  9.9 1.1 copy.48
  11.0 2.0 concatenate.42
  13.1 43.2 %all-gather.7.cloned.1.call-done = bf16[960,1664]{1,0:T(8,128)(2,1)} async-done(((bf16[240,1664]{1,0:T(8,128)(2,1)}), bf16[960,1664]{1,0:T(8,128)(2,1)}) %all-gather.7.cloned.1.call-update) | async-done | bytes 3194896 | tf_op jit(solution)/shard_map/all_gather | solution.py:961
  56.3 1.1 copy.55
  58.9 2.5 broadcast_select_fusion
  62.1 1.3 fusion.31
  63.8 1.2 fusion.32
  65.3 1.1 convert_bitcast_fusion
  66.4 1.0 slice_reduce_fusion
  67.3 3.4 fusion.3
  72.9 1.0 maximum_bitcast_fusion.1.own
  74.0 57.2 %gather_blocks.1 = (bf16[5,4,4,2,256,128]{5,4,3,2,1,0:T(8,128)(2,1)}, bf16[15,64,256]{2,1,0:T(8,128)(2,1)}) custom-call(bf16[5,256,128]{2,1,0:T(8,128)(2,1)} %maximum_bitcast_fusion.1.own, bf16[15,64,256]{2,1,0:T(8,128)(2,1)} %maximum_multiply_fusion.query.q_own), custom_call_target="tpu_custom_call" | custom-call | flops 49999998976 | bytes 20971520 | tf_op jit(solution)/shard_map/gather_blocks/pallas_call | solution.py:303
  131.2 4.1 copy-done.2
  135.2 1.0 copy-done.5
  136.3 41.2 %attend_forward.1 = (f32[15,64,256]{2,1,0:T(8,128)S(1)}, f32[15,1,256]{2,1,0:T(1,128)S(1)}, bf16[15,80,256]{2,1,0:T(8,128)(2,1)S(1)}) custom-call(s32[3]{0:T(128)S(1)} %pad_add_fusion.place, bf16[5,8192,128]{2,1,0:T(8,128)(2,1)S(1)} %bitcast.100, bf16[15,64,256]{2,1,0:T(8,128)(2,1)S(1)} %copy-done, bf16[15,64,256]{2,1,0:T(8,128)(2,1)S(1)} %copy-done.5), custom_call_target="tpu_custom_call" | custom-call | flops 99656663040 | bytes 10485760 | tf_op jit(solution)/shard_map/attend_forward/pallas_call | solution.py:153
  178.4 229.5 %exchange.1 = (bf16[15,80,256]{2,1,0:T(8,128)(2,1)}, bf16[2,4,240,2560]{3,2,1,0:T(8,128)(2,1)}, bf16[4,2,320,960]{3,2,1,0:T(8,128)(2,1)}) custom-call(bf16[15,80,256]{2,1,0:T(8,128)(2,1)} %copy-done.4, bf16[4,240,2560]{2,1,0:T(8,128)(2,1)} %bitcast.125, bf16[4,320,960]{2,1,0:T(8,128)(2,1)} %bitcast.126), custom_call_target="tpu_custom_call" | custom-call | flops 10000000000 | bytes 9830400 | tf_op jit(solution)/shard_map/exchange/pallas_call | solution.py:345
  407.9 1.1 fusion.27
  409.1 1.2 fusion.20
  410.3 8.3 %fusion.35 = (bf16[1,4,240,2560]{3,2,1,0:T(8,128)(2,1)}, bf16[1,4,240,2560]{3,2,1,0:T(8,128)(2,1)}) fusion(bf16[2,4,240,2560]{3,2,1,0:T(8,128)(2,1)} %get-tuple-element.38), kind=kLoop, calls=%fused_computation.117 | loop fusion | bytes 19660800 | tf_op jit(solution)/shard_map/slice | solution.py:1023
  418.6 2.6 multiply_reduce_fusion.3
  421.6 1.5 fusion.40
  423.7 1.5 fusion.39
  425.6 3.9 multiply_convert_fusion
  429.5 1.5 fusion.41
  430.9 1.6 multiply_reduce_fusion
  432.8 1.3 copy-done.12
  435.1 2.0 convolution_convert_fusion.4
  437.1 3.6 convolution_convert_fusion.1.up
  440.7 3.6 convolution_convert_fusion.2.gate
  446.0 5.1 collective-permute-start
  451.1 5.2 fusion.down
  456.9 5.4 fusion.11
  462.4 3.0 collective-permute-done.do_mirrored
  466.3 120.4 %attend_backward.1 = (f32[15,64,256]{2,1,0:T(8,128)}, bf16[5,256,128]{2,1,0:T(8,128)(2,1)}, bf16[16,3840]{1,0:T(8,128)(2,1)}) custom-call(s32[3]{0:T(128)} %copy-done.3, bf16[5,8192,128]{2,1,0:T(8,128)(2,1)} %bitcast.99, bf16[15,64,256]{2,1,0:T(8,128)(2,1)} %maximum_multiply_fusion.query.q_own, bf16[15,64,256]{2,1,0:T(8,128)(2,1)} %get-tuple-element.29.q_mirrored, ...), custom_call_target="tpu_custom_call" | custom-call | flops 166094438400 | bytes 20971520 | tf_op jit(solution)/shard_map/attend_backward/pallas_call | solution.py:750
  586.7 1.3 broadcast_multiply_fusion
  589.4 3.9 fusion.18
  593.3 2.7 convolution_convert_fusion.3
  596.2 3.3 pad_maximum_fusion.first
  599.5 51.4 %last_sums.1 = bf16[2,4,4,16,5120]{4,3,2,1,0:T(8,128)(2,1)S(1)} custom-call(bf16[960,2560]{1,0:T(8,128)(2,1)S(1)} %pad_maximum_fusion.first, bf16[4,16,256]{2,1,0:T(8,128)(2,1)S(1)} %pad.10.gains, bf16[16,3840]{1,0:T(8,128)(2,1)S(1)} %copy-done.1), custom_call_target="tpu_custom_call" | custom-call | tf_op jit(solution)/shard_map/last_sums/pallas_call | solution.py:901
  651.0 1.2 slice_convert_fusion
  652.6 2.6 slice_bitcast_fusion
  656.0 1.3 slice.196
  658.1 1.1 slice.192
  659.8 1.9 copy.62
  661.6 1.9 copy.61
  663.5 2.5 fusion.17
  666.0 1.6 maximum_bitcast_fusion
  (151 shorter events, 17.2 us)
Async XLA Ops:
  7.2 49.1 %copy-start.19 = (bf16[640,960]{0,1:T(8,128)(2,1)S(1)}, bf16[640,960]{0,1:T(8,128)(2,1)}, u32[]{:S(2)}) copy-start(bf16[640,960]{0,1:T(8,128)(2,1)} %param.22) | copy-start | bytes 3686404
  7.2 49.1 %all-gather.7.cloned.1.call-start = ((), (), s32[]{:S(2)}) async-start(), calls=%async_computation | async-start | bytes 3993600 | tf_op jit(solution)/shard_map/all_gather | solution.py:961
  13.0 165.3 %all-gather.13.cloned.1.call-start = ((), (), s32[]{:S(2)}) async-start(), calls=%async_computation.3 | async-start | bytes 3276800 | tf_op jit(solution)/shard_map/all_gather | solution.py:1017
  57.4 1.5 copy-start.20
  58.3 3.2 copy-start.35
  58.3 120.0 %all-gather.11.cloned.1.call-start = ((), (), s32[]{:S(2)}) async-start(), calls=%async_computation.2 | async-start | bytes 6144000 | tf_op jit(solution)/shard_map/all_gather | solution.py:1015
  58.9 6.2 copy-start.13
  61.4 357.1 %all-gather.9.cloned.1.call-start = ((), (), s32[]{:S(2)}) async-start(), calls=%async_computation.1 | async-start | bytes 2457600 | tf_op jit(solution)/shard_map/all_gather | solution.py:961
  63.6 8.1 %copy-start.25 = (f32[32,256]{1,0:T(8,128)}, f32[32,256]{1,0:T(8,128)S(1)}, u32[]{:S(2)}) copy-start(f32[32,256]{1,0:T(8,128)S(1)} %get-tuple-element.118) | copy-start | bytes 98308
  63.6 8.1 %copy-start.27 = (f32[32,256]{1,0:T(8,128)}, f32[32,256]{1,0:T(8,128)S(1)}, u32[]{:S(2)}) copy-start(f32[32,256]{1,0:T(8,128)S(1)} %get-tuple-element.119) | copy-start | bytes 98308
  63.7 9.0 %copy-start.21 = (f32[32,256]{0,1:T(8,128)}, f32[32,256]{0,1:T(8,128)S(1)}, u32[]{:S(2)}) copy-start(f32[32,256]{0,1:T(8,128)S(1)} %copy.51) | copy-start | bytes 98308
  63.8 8.9 %copy-start.23 = (f32[32,256]{0,1:T(8,128)}, f32[32,256]{0,1:T(8,128)S(1)}, u32[]{:S(2)}) copy-start(f32[32,256]{0,1:T(8,128)S(1)} %copy.53) | copy-start | bytes 98308
  65.1 66.1 %copy-start.3 = (s32[3]{0:T(128)}, s32[3]{0:T(128)S(1)}, u32[]{:S(2)}) copy-start(s32[3]{0:T(128)S(1)} %pad_add_fusion.place) | copy-start | bytes 40
  65.3 5.5 copy-start.33
  67.3 3.5 copy-start.30
  74.0 57.2 %copy-start = (bf16[15,64,256]{2,1,0:T(8,128)(2,1)S(1)}, bf16[15,64,256]{2,1,0:T(8,128)(2,1)}, u32[]{:S(2)}) copy-start(bf16[15,64,256]{2,1,0:T(8,128)(2,1)} %maximum_multiply_fusion.query.q_own) | copy-start | bytes 1474564
  131.2 4.1 copy-start.2
  135.2 1.0 copy-start.5
  177.5 0.8 copy-start.4
  178.4 229.5 %copy-start.36 = (pred[256]{0:T(512)(128)(4,1)S(1)}, pred[256]{0:T(512)(128)(4,1)}, u32[]{:S(2)}) copy-start(pred[256]{0:T(512)(128)(4,1)} %fusion.32) | copy-start | bytes 772
  410.3 8.3 %copy-start.14 = (bf16[1,256,960]{1,2,0:T(8,128)(2,1)S(1)}, bf16[1,256,960]{1,2,0:T(8,128)(2,1)}, u32[]{:S(2)}) copy-start(bf16[1,256,960]{1,2,0:T(8,128)(2,1)} %param.12) | copy-start | bytes 1474564
  418.6 2.7 copy-start.29
  418.6 3.0 copy-start.6
  421.4 2.2 slice-start
  421.6 2.2 slice-start.1
  421.6 3.7 slice-start.2
  423.7 1.6 copy-start.11
  423.7 1.9 slice-start.3
  432.5 1.6 copy-start.12
  432.5 2.2 copy-start.16
  434.1 1.1 copy-start.7
  434.7 10.4 %copy-start.10 = (bf16[960,256]{1,0:T(8,128)(2,1)}, bf16[960,256]{1,0:T(8,128)(2,1)S(1)}, u32[]{:S(2)}) copy-start(bf16[960,256]{1,0:T(8,128)(2,1)S(1)} %convolution_convert_fusion.5) | copy-start | bytes 1474564
  446.0 19.4 %collective-permute-start = (bf16[15,80,256]{2,1,0:T(8,128)(2,1)S(1)}, bf16[15,80,256]{2,1,0:T(8,128)(2,1)S(1)}, u32[]{:S(2)}, u32[]{:S(2)}) collective-permute-start(bf16[15,80,256]{2,1,0:T(8,128)(2,1)S(1)} %concatenate.45), channel_id=1, source_target_pairs={{0,124},{4,120},{8,116},{12,112},{16,108},{20,104},{24,100},{28,96... | collective-permute-start | bytes 1843208 | tf_op jit(solution)/shard_map/ppermute | solution.py:1063
  451.1 5.8 copy-start.18
  465.4 0.8 copy-start.37
  466.3 121.7 %copy-start.26 = (f32[32,256]{1,0:T(8,128)S(1)}, f32[32,256]{1,0:T(8,128)}, u32[]{:S(2)}) copy-start(f32[32,256]{1,0:T(8,128)} %copy-done.25) | copy-start | bytes 98308
  466.3 121.8 %copy-start.28 = (f32[32,256]{1,0:T(8,128)S(1)}, f32[32,256]{1,0:T(8,128)}, u32[]{:S(2)}) copy-start(f32[32,256]{1,0:T(8,128)} %copy-done.27) | copy-start | bytes 98308
  586.6 1.5 copy-start.17
  586.6 2.0 copy-start.22
  586.6 2.0 copy-start.24
  588.4 1.0 copy-start.15
  588.4 1.0 copy-start.31
  588.4 1.0 copy-start.34
  593.3 2.8 copy-start.32
  593.3 2.9 copy-start.9
  596.2 3.3 copy-start.1
  656.0 7.5 %copy-start.8 = (f32[256,960]{0,1:T(8,128)S(1)}, f32[256,960]{0,1:T(8,128)}, u32[]{:S(2)}) copy-start(f32[256,960]{0,1:T(8,128)} %copy-done.7) | copy-start | bytes 2949124
Sparse Core Ops, SparseCore 0:
  13.1 43.1 all-gather.6
  58.5 35.3 all-gather.12
  96.2 54.3 all-gather.10
  152.1 30.1 all-gather.8
